TPU v7x, 32 devices: a whole 2x2x4 slice. The times are simulated.
32 devices in a mesh: atoms: 8 (over z, y), grp: 4 (over x, core).
Axes of the slice: x: 2, y: 2, z: 4, core: 2. Of those that a mesh axis runs over, the one named last changes fastest.
Arguments:
- params: float32 [89344], replicated
- first_moment: float32 [89344], replicated, may hold values from -2.2888184e-05 to 2.2888184e-05
- second_moment: float32 [89344], replicated, may hold values from 1.1192694e-12 to 4.4770776e-12
- average: float32 [89344], replicated
- edge_vectors: float32 [3, 4, 8192], P(None, 'grp', 'atoms'), as said below
- owner_rank: int32 [4, 8192, 1], P('grp', 'atoms'), may hold values from 0 to 7; in each aligned block of 1024 rows (0 to 1023, 1024 to 2047, ..., all dimensions but the last counted through in order) at most 256 rows name the same one
- neighbour_local: int32 [4, 8192], P('grp', 'atoms'), may hold values from 0 to 31
- centre_species: int32 [4, 256], P('grp', 'atoms'), may hold values from 0 to 4
- neighbour_species: int32 [4, 8192], P('grp', 'atoms'), may hold values from 0 to 4
- live_atoms: int32 [4, 8], P('grp', 'atoms'), may hold values from 1 to 32, as said below
- target_forces: float32 [3, 4, 256], P(None, 'grp', 'atoms'), may hold values from -6 to 6
Outputs:
- loss_sum: float32 [], replicated
- count: float32 [], replicated
- grad_norm: float32 [], replicated
- forces: float32 [3, 4, 256], P(None, 'grp', 'atoms')
- new_first: float32 [89344], replicated
- new_second: float32 [89344], replicated
- new_params: float32 [89344], replicated
- low_params: bfloat16 [89344], replicated
- new_average: float32 [89344], replicated
Inputs may be any that keep to these rules, and one draw needn't show every extreme that they name: `owner_rank`: among the 1024 edges of one device, at most 256 have their neighbour on any one owner, a bound that some block reaches. `live_atoms`: A device's true atoms are its first ones; some device has all 32. `edge_vectors`: edge lengths lie between 0.9 and 4.8.
All inputs are finite; a program needn't handle non-finite values.
Results may differ from a plain program's by a relative error of at most 0.001.
Values sent between devices are 32-bit elements; how exact they have to be, the bound alone decides.
No kernel may reach another device: no remote copies, remote signals or barrier semaphores. Data moves between devices by JAX's collectives and lax.ppermute only.
A program may use at most 128 MiB of HBM per device.

v0:
```python
import functools
import math

import jax
import jax.numpy as jnp
from jax import lax
from jax.experimental import pallas as pl
from jax.experimental.pallas import tpu as pltpu
from jax.sharding import Mesh
from jax.sharding import PartitionSpec as P

LATENT = 64
UNITS = 128
CHANNELS = 32
BASES = 8
SPECIES = 5
LAYERS = 3
STEP = 10
NEI = 32
NPARAM = 89344

cutoff_radius = 5.0
clip_level = 0.01
learn_rate = 0.1
beta_one = 0.9
beta_two = 0.999
epsilon_adam = 1e-08
decay_rate = 0.01
average_keep = 0.99
mix = 0.7071

f32 = jnp.float32
bf16 = jnp.bfloat16

ATOMS = 32
EDGES = 1024
TILES = 8
CH = 256
CHUNKS = EDGES // CH
FEAT = 32

AT_EMBED = 0
AT_ENV = 9
AT_INV = AT_ENV + 96
AT_ONE = AT_INV + 144
AT_TWO = AT_ONE + 192
AT_HEAD = AT_TWO + 192
AT_VEC = AT_HEAD + 64
ROWS = AT_VEC + 1
PADDED = 768
HALF = PADDED // 2

STATE = [
    ("wf_emb", (LATENT, 3 * FEAT), bf16),
    ("wf_env", (3, 64, 192), bf16),
    ("wb_env", (3, 64, 192), bf16),
    ("wf_inv", (3, 64, 288), bf16),
    ("wb_inv", (3, 96, 192), bf16),
    ("wf_one", (3, 128, 192), bf16),
    ("wb_one", (3, 64, 384), bf16),
    ("wf_two", (3, 64, 384), bf16),
    ("wb_two", (3, 128, 192), bf16),
    ("wf_head", (128, 192), bf16),
    ("wb_head", (64, 384), bf16),
    ("whcol", (128, 128), f32),
    ("place", (3, 8, 128), f32),
    ("owner", (8, 128), jnp.int32),
    ("hot", (ATOMS, EDGES), bf16),
    ("geo", (10, 8, 128), f32),
    ("bes", (2, BASES, EDGES), f32),
    ("phi", (2 * FEAT, EDGES), bf16),
    ("latx", (4, 128, EDGES), bf16),
    ("pq", (3, 64, EDGES), f32),
    ("vv", (3, 64, EDGES), f32),
    ("ivx", (3, 192, EDGES), bf16),
    ("inx", (3, 128, EDGES), bf16),
    ("sx", (3, 256, EDGES), bf16),
    ("s1", (3, 128, EDGES), f32),
    ("t2", (3, 128, EDGES), f32),
    ("oo", (3, 64, EDGES), f32),
    ("lb", (3, 64, EDGES), f32),
    ("ob", (3, 128, EDGES), bf16),
    ("hb", (3, 256, EDGES), bf16),
    ("ib", (3, 128, EDGES), bf16),
    ("vb", (3, 96, EDGES), f32),
    ("ab", (3, 32, EDGES), f32),
    ("pb", (3, 128, EDGES), bf16),
    ("qq", (3, 32, EDGES), f32),
    ("qb", (3, 32, EDGES), f32),
    ("z1", (64, EDGES), f32),
    ("tz", (64, EDGES), f32),
    ("zb", (128, EDGES), bf16),
    ("sh", (128, EDGES), f32),
    ("h1", (128, EDGES), f32),
    ("h2", (128, EDGES), f32),
    ("hhb", (256, EDGES), bf16),
    ("env", (3, 9, 32, 128), f32),
    ("eh", (3, 8, 32, 128), f32),
    ("bb", (3, 3, 32, 128), f32),
    ("eb", (3, 9, 32, 128), f32),
    ("cot", (3, 11, 32, 128), f32),
]

SCRATCH_A = [
    ("tmp", (128, 128), f32),
    ("run", (64, EDGES), f32),
    ("ybar", (9, 8, 8, 128), f32),
    ("dbar", (8, 8, 128), f32),
]

SCRATCH_B = [
    ("tmp", (128, 128), f32),
    ("run", (64, EDGES), f32),
    ("cdir", (3, 8, 128), f32),
    ("gd", (10, 8, 128), f32),
    ("phid", (2 * FEAT, EDGES), bf16),
    ("zd", (64, EDGES), f32),
    ("latd", (4, 128, EDGES), bf16),
    ("pqd", (3, 64, EDGES), f32),
    ("vvd", (3, 64, EDGES), f32),
    ("qd", (3, 32, EDGES), f32),
    ("ivd", (3, 192, EDGES), bf16),
    ("ind", (3, 128, EDGES), bf16),
    ("hd", (3, 128, EDGES), f32),
    ("sd", (3, 256, EDGES), bf16),
    ("envd", (3, 9, 32, 128), f32),
    ("ehd", (3, 8, 32, 128), f32),
    ("bd", (3, 3, 32, 128), f32),
    ("hht", (256, EDGES), bf16),
    ("ot", (128, EDGES), bf16),
    ("ht", (256, EDGES), bf16),
    ("it", (128, EDGES), bf16),
    ("vt", (96, EDGES), f32),
    ("qt", (3, 32, EDGES), f32),
    ("pt", (128, EDGES), bf16),
    ("zt", (128, EDGES), bf16),
    ("et", (3, 9, 32, 128), f32),
    ("cott", (11, 32, 128), f32),
    ("grad", (PADDED, 128), f32),
]


class Refs:
    def __init__(self, entries, refs):
        for (name, _, _), ref in zip(entries, refs, strict=True):
            setattr(self, name, ref)


def split(x):
    high = x.astype(bf16)
    return high, (x - high.astype(f32)).astype(bf16)


def product(weights, high, low):
    return jnp.dot(
        weights, jnp.concatenate([high, low, high], 0), preferred_element_type=f32
    )


def put(ref, rows, columns, value, lead=()):
    high, low = split(value)
    half = ref.shape[-2] // 2
    ref[(*lead, slice(rows, rows + value.shape[0]), columns)] = high
    ref[(*lead, slice(half + rows, half + rows + value.shape[0]), columns)] = low
    return high, low


def pair(ref, columns, lead=()):
    half = ref.shape[-2] // 2
    return ref[(*lead, slice(0, half), columns)], ref[(*lead, slice(half, 2 * half), columns)]


def spin(x, amount):
    return pltpu.roll(x, amount % 128, 1)


def group_sum(x):
    x = x + spin(x, 64)
    return x + spin(x, 32)


def lanes(shape):
    return lax.broadcasted_iota(jnp.int32, shape, len(shape) - 1)


def rows_of(shape):
    return lax.broadcasted_iota(jnp.int32, shape, len(shape) - 2)


def silu_parts(h):
    gate = 1.0 / (1.0 + jnp.exp(-h))
    slope = gate * (1.0 - gate)
    return h * gate, gate + h * slope, slope * (2.0 + h * (1.0 - 2.0 * gate))


def geometry(x, y, z):
    d = jnp.sqrt(x * x + y * y + z * z)
    u, v, w = x / d, y / d, z / d
    s = d / cutoff_radius
    s2 = s * s
    s6 = s2 * s2 * s2
    f = 1.0 - 28.0 * s6 + 48.0 * (s6 * s) - 21.0 * (s6 * s2)
    r3, r5, r15 = math.sqrt(3.0), math.sqrt(5.0), math.sqrt(15.0)
    harmonics = [
        r3 * u,
        r3 * v,
        r3 * w,
        r15 * u * v,
        r15 * v * w,
        0.5 * r5 * (3.0 * w * w - 1.0),
        r15 * u * w,
        0.5 * r15 * (u * u - v * v),
    ]
    return d, f, harmonics


def dots(left, right):
    total = left[0] * right[0]
    for a, b in zip(left[1:], right[1:], strict=True):
        total = total + a * b
    return total


def degree(m):
    return 1 if m <= 3 else 2


def atom_terms(envs):
    if len(envs) == 1:
        (one,) = envs
        zero = jnp.zeros_like(one[0])
        return [one[0], zero, zero], one[1:]
    if len(envs) == 2:
        one, two = envs
        return (
            [2.0 * one[0] * two[0], dots(one[1:4], two[1:4]), dots(one[4:], two[4:])],
            [one[0] * two[m] for m in range(1, 9)],
        )
    one, two, three = envs
    both = one[0] * two[0]
    twice = 2.0 * one[0]
    part = [two[0] * one[m] + twice * two[m] for m in range(1, 9)]
    return (
        [4.0 * both * three[0], dots(part[:3], three[1:4]), dots(part[3:], three[4:])],
        [both * three[m] for m in range(1, 9)],
    )


def atom_back(envs, cots):
    return jax.vjp(atom_terms, envs)[1](cots)[0]


def tile(t):
    return slice(128 * t, 128 * t + 128)


def chunk(c):
    return slice(CH * c, CH * c + CH)


def wide(ref, index, c):
    per = CH // 128
    return jnp.concatenate([ref[index, t : t + 1, :] for t in range(per * c, per * c + per)], 1)


def fold(value):
    total = value[0:8]
    for r in range(8, value.shape[0], 8):
        total = total + value[r : r + 8]
    return total


def unpack(packed, count, tmp):
    half = count // 2
    tmp[pl.ds(0, half, stride=2), :] = packed
    tmp[pl.ds(1, half, stride=2), :] = spin(packed, 64)
    value = tmp[0:count, :]
    return jnp.where(lanes(value.shape) < 64, value, spin(value, 64))


def store_64(ref, lead, doubled):
    high, low = split(doubled)
    ref[(*lead, slice(None), slice(0, 128))] = high
    ref[(*lead, slice(None), slice(128, 192))] = low[:, 0:64]


def store_128(ref, lead, value):
    high, low = split(value)
    ref[(*lead, slice(None), slice(0, 128))] = high
    ref[(*lead, slice(None), slice(128, 256))] = high
    ref[(*lead, slice(None), slice(256, 384))] = low


def store_96(ref, lead, value):
    high = value.astype(bf16).astype(f32)
    low = value - high
    high_on, low_on = spin(high, 96), spin(low, 64)
    lane = lanes(value.shape)
    ref[(*lead, slice(None), slice(0, 128))] = jnp.where(lane < 96, high, high_on).astype(bf16)
    ref[(*lead, slice(None), slice(128, 256))] = jnp.where(lane < 64, high_on, low_on).astype(bf16)
    ref[(*lead, slice(None), slice(256, 288))] = low_on[:, 0:32].astype(bf16)


def prepare(par, st, wb_emb, tmp):
    for k in range(LAYERS):
        w = unpack(par[AT_ENV + 32 * k : AT_ENV + 32 * k + 32, :], 64, tmp)
        store_64(st.wb_env, (k,), w)
        store_64(st.wf_env, (k,), jnp.concatenate([w, w], 0).T[0:64])
        w = unpack(par[AT_INV + 48 * k : AT_INV + 48 * k + 48, :], 96, tmp)
        store_64(st.wb_inv, (k,), w)
        store_96(st.wf_inv, (k,), jnp.concatenate([w, jnp.zeros((32, 128), f32)], 0).T[0:64])
        w = par[AT_ONE + 64 * k : AT_ONE + 64 * k + 64, :]
        store_128(st.wb_one, (k,), w)
        store_64(st.wf_one, (k,), jnp.concatenate([w, w], 0).T)
        w = unpack(par[AT_TWO + 64 * k : AT_TWO + 64 * k + 64, :], 128, tmp)
        store_64(st.wb_two, (k,), w)
        store_128(st.wf_two, (k,), w.T[0:64])
    w = par[AT_HEAD : AT_HEAD + 64, :]
    store_128(st.wb_head, (), w)
    store_64(st.wf_head, (), jnp.concatenate([w, w], 0).T)
    w = unpack(par[0:9, :], 18, tmp)
    w = jnp.concatenate([w[0:16], jnp.where(rows_of((16, 128)) < 2, tmp_rows(w, 16), 0.0)], 0)
    store_64(wb_emb, (), w[0:16])
    high = w.astype(bf16).astype(f32)
    low = w - high
    turned = jnp.concatenate([high, high, low, jnp.zeros((32, 128), f32)], 0).T[0:64]
    st.wf_emb[...] = turned[:, 0 : 3 * FEAT].astype(bf16)
    st.whcol[...] = jnp.broadcast_to(par[AT_VEC : AT_VEC + 1, :], (128, 128)).T


def tmp_rows(w, start):
    return jnp.concatenate([w[start : start + 2], jnp.zeros((14, 128), f32)], 0)


def sine_parts(turns):
    whole = jnp.round(turns)
    rest = (turns - whole) * math.pi
    odd = whole - 2.0 * jnp.floor(whole * 0.5)
    sign = 1.0 - 2.0 * odd
    r2 = rest * rest
    sine = 0.0
    for n in (13, 11, 9, 7, 5, 3, 1):
        sine = sine * r2 + (-1.0) ** (n // 2) / math.factorial(n)
    cosine = 0.0
    for n in (14, 12, 10, 8, 6, 4, 2, 0):
        cosine = cosine * r2 + (-1.0) ** (n // 2) / math.factorial(n)
    return sign * rest * sine, sign * cosine


def first_kernel(ranks, axis, par, vec, own, loc, nsp, cen, live, tgt, pay, *refs):
    st = Refs(STATE, refs[: len(STATE)])
    wb_emb, payload, scatter = refs[len(STATE) : len(STATE) + 3]
    sc = Refs(SCRATCH_A, refs[len(STATE) + 3 :])
    me = lax.axis_index(axis)
    prepare(par, st, wb_emb, sc.tmp)

    code = ((own[...] * 32 + loc[...]) * 8 + nsp[...]).astype(f32)
    for q, value in enumerate((vec[0], vec[1], vec[2], code)):
        for a in range(4):
            sc.tmp[pl.ds(32 * q + a, 8, stride=4), :] = spin(value, -32 * a)
    turned = sc.tmp[...].T
    lane = lanes((8, 128))

    def picked(q):
        out = spin(turned[0:8], -32 * q)
        for g in range(1, 4):
            out = jnp.where(lane // 32 == g, spin(turned[8 * g : 8 * g + 8], 32 * (g - q)), out)
        return out

    xyz = [picked(q) for q in range(3)]
    codes = picked(3).astype(jnp.int32)
    for q in range(3):
        st.place[q] = xyz[q]
    local = lax.shift_right_logical(codes, 3) & 31
    owner = lax.shift_right_logical(codes, 8)
    kind = codes & 7
    st.owner[...] = owner
    sc.tmp[0:8, :] = jnp.zeros((8, 128), f32)
    sc.tmp[0:1, 0:32] = cen[...].astype(f32)
    centre_kind = group_sum(sc.tmp[0:8, :])[0:1].astype(jnp.int32)

    d, f, harmonics = geometry(*xyz)
    st.geo[0] = f
    for m in range(8):
        st.geo[m + 1] = harmonics[m]
    st.geo[9] = f * (1.0 / math.sqrt(NEI))
    geo = st.geo

    orders = (rows_of((8, 128)) + 1).astype(f32)
    inv_d = 1.0 / d
    scale = math.sqrt(2.0 / cutoff_radius)
    for t in range(TILES):
        row_inv = inv_d[t : t + 1]
        sine, cosine = sine_parts(orders * (d[t : t + 1] / cutoff_radius))
        b = (scale * sine) * row_inv
        slope = (scale * math.pi / cutoff_radius) * orders * cosine * row_inv - b * row_inv
        st.bes[0, :, tile(t)] = b
        st.bes[1, :, tile(t)] = slope
        row = rows_of((FEAT - 8, 128)) + 8
        hot = (row == centre_kind + 8) | (row == kind[t : t + 1] + 13)
        features = jnp.concatenate([b * f[t : t + 1], hot.astype(f32)], 0)
        put(st.phi, 0, tile(t), features)
        st.hot[:, tile(t)] = (rows_of((ATOMS, 128)) == local[t : t + 1]).astype(f32).astype(bf16)

    for c in range(CHUNKS):
        cs = chunk(c)
        s, s1, s2 = silu_parts(product(st.wf_emb[...], *pair(st.phi, cs)))
        st.z1[:, cs] = s1
        st.tz[:, cs] = s2
        sc.run[:, cs] = s
        put(st.latx, 0, cs, s, (0,))

    for k in range(LAYERS):
        for c in range(CHUNKS):
            cs = chunk(c)
            st.pq[k, :, cs] = product(st.wf_env[k], *pair(st.latx, cs, (k,)))
        for r in range(0, 32, 16):
            rs = slice(r, r + 16)
            sums = None
            for t in range(TILES):
                a = st.pq[k, rs, tile(t)] * geo[9, t : t + 1, :]
                terms = [a] + [a * geo[m, t : t + 1, :] for m in range(1, 9)]
                sums = terms if sums is None else [x + y for x, y in zip(sums, terms, strict=True)]
            for m in range(9):
                st.env[k, m, rs, :] = group_sum(sums[m])
        for r in range(0, 32, 8):
            rs = slice(r, r + 8)
            envs = [[st.env[j, m, rs, :] for m in range(9)] for j in range(k + 1)]
            base, factors = atom_terms(envs)
            for l in range(3):
                st.bb[k, l, rs, :] = base[l]
            for m in range(8):
                st.eh[k, m, rs, :] = factors[m]
        for r in range(0, 32, 16):
            rs = slice(r, r + 16)
            for t in range(TILES):
                ts = tile(t)
                q = st.pq[k, 32 + r : 48 + r, ts]
                if k > 0:
                    q = mix * st.qq[k - 1, rs, ts] * q
                st.qq[k, rs, ts] = q
                values = [st.bb[k, l, rs, :] for l in range(3)]
                for m in range(1, 9):
                    l = degree(m)
                    values[l] = values[l] + geo[m, t : t + 1, :] * st.eh[k, m - 1, rs, :]
                st.vv[k, rs, ts] = values[1]
                st.vv[k, 32 + r : 48 + r, ts] = values[2]
                for l in range(3):
                    put(st.ivx, 32 * l + r, ts, q * values[l], (k,))
        for c in range(CHUNKS):
            cs = chunk(c)
            inner = sc.run[:, cs] + product(st.wf_inv[k], *pair(st.ivx, cs, (k,)))
            h = product(st.wf_one[k], *put(st.inx, 0, cs, inner, (k,)))
            s, s1, s2 = silu_parts(h)
            st.s1[k, :, cs] = s1
            st.t2[k, :, cs] = s2
            o = product(st.wf_two[k], *put(st.sx, 0, cs, s, (k,)))
            st.oo[k, :, cs] = o
            latent = sc.run[:, cs] + wide(geo, 0, c) * o
            sc.run[:, cs] = latent
            put(st.latx, 0, cs, latent, (k + 1,))

    per = CH // 128
    for c in range(CHUNKS):
        cs = chunk(c)
        s, s1, s2 = silu_parts(product(st.wf_head[...], *pair(st.latx, cs, (3,))))
        st.sh[:, cs] = s
        st.h1[:, cs] = s1
        st.h2[:, cs] = s2
        whcol = jnp.concatenate([st.whcol[...]] * per, 1)
        energy = whcol * s
        for j in range(per):
            sc.ybar[0, per * c + j] = fold(energy[:, 128 * j : 128 * j + 128])
        back = put(st.hhb, 0, cs, wide(geo, 0, c) * whcol * s1)
        st.lb[2, :, cs] = product(st.wb_head[...], *back)

    for k in reversed(range(LAYERS)):
        for c in range(CHUNKS):
            cs = chunk(c)
            lb = st.lb[k, :, cs]
            share = st.oo[k, :, cs] * lb
            for j in range(per):
                sc.ybar[0, per * c + j] += fold(share[:, 128 * j : 128 * j + 128])
            sb = product(st.wb_two[k], *put(st.ob, 0, cs, wide(geo, 0, c) * lb, (k,)))
            st.t2[k, :, cs] = st.t2[k, :, cs] * sb
            ib = product(st.wb_one[k], *put(st.hb, 0, cs, st.s1[k, :, cs] * sb, (k,)))
            st.vb[k, :, cs] = product(st.wb_inv[k], *put(st.ib, 0, cs, ib, (k,)))
            sc.run[:, cs] = lb + ib
        for r in range(0, 32, 16):
            rs = slice(r, r + 16)
            sums = None
            for t in range(TILES):
                ts = tile(t)
                q = st.qq[k, rs, ts]
                vb = [st.vb[k, 32 * l + r : 32 * l + r + 16, ts] for l in range(3)]
                qb = (
                    vb[0] * st.bb[k, 0, rs, :]
                    + vb[1] * st.vv[k, rs, ts]
                    + vb[2] * st.vv[k, 32 + r : 48 + r, ts]
                )
                if k < LAYERS - 1:
                    qb = qb + mix * st.pq[k + 1, 32 + r : 48 + r, ts] * st.qb[k + 1, rs, ts]
                st.qb[k, rs, ts] = qb
                back = [x * q for x in vb]
                terms = list(back)
                for m in range(1, 9):
                    terms.append(back[degree(m)] * geo[m, t : t + 1, :])
                    share = fold(back[degree(m)] * st.eh[k, m - 1, rs, :])
                    if k == LAYERS - 1 and r == 0:
                        sc.ybar[m, t] = share
                    else:
                        sc.ybar[m, t] += share
                sums = terms if sums is None else [x + y for x, y in zip(sums, terms, strict=True)]
            for n in range(11):
                st.cot[k, n, rs, :] = group_sum(sums[n])
        for r in range(0, 32, 8):
            rs = slice(r, r + 8)
            envs = [[st.env[j, m, rs, :] for m in range(9)] for j in range(k + 1)]
            cots = [st.cot[k, n, rs, :] for n in range(11)]
            back = atom_back(envs, (cots[:3], cots[3:]))
            for j in range(k + 1):
                for m in range(9):
                    if k == LAYERS - 1:
                        st.eb[j, m, rs, :] = back[j][m]
                    else:
                        st.eb[j, m, rs, :] += back[j][m]
        for r in range(0, 32, 16):
            rs = slice(r, r + 16)
            for t in range(TILES):
                ts = tile(t)
                p = st.pq[k, rs, ts]
                fs = geo[9, t : t + 1, :]
                a = p * fs
                ab = st.eb[k, 0, rs, :]
                for m in range(1, 9):
                    e = st.eb[k, m, rs, :]
                    ab = ab + geo[m, t : t + 1, :] * e
                    sc.ybar[m, t] += fold(a * e)
                st.ab[k, rs, ts] = ab
                sc.ybar[0, t] += fold((1.0 / math.sqrt(NEI)) * ab * p)
                put(st.pb, r, ts, ab * fs, (k,))
                qb = st.qb[k, rs, ts]
                if k > 0:
                    qb = mix * st.qq[k - 1, rs, ts] * qb
                put(st.pb, 32 + r, ts, qb, (k,))
        for c in range(CHUNKS):
            cs = chunk(c)
            lb = sc.run[:, cs] + product(st.wb_env[k], *pair(st.pb, cs, (k,)))
            if k > 0:
                st.lb[k - 1, :, cs] = lb
                continue
            st.tz[:, cs] = st.tz[:, cs] * lb
            pb = product(wb_emb[...], *put(st.zb, 0, cs, st.z1[:, cs] * lb))[0:8]
            for j in range(per):
                t = per * c + j
                part = pb[:, 128 * j : 128 * j + 128]
                sc.ybar[0, t] += st.bes[0, :, tile(t)] * part
                sc.dbar[t] = geo[0, t : t + 1, :] * st.bes[1, :, tile(t)] * part

    bars = [jnp.sum(sc.ybar[m], axis=1) for m in range(9)]
    slopes = jax.vjp(geometry, *xyz)[1]((jnp.sum(sc.dbar[...], axis=1), bars[0], bars[1:]))

    for t in range(TILES):
        mine = rows_of((ranks, 128)) == owner[t : t + 1]
        parts = jnp.concatenate([jnp.where(mine, s[t : t + 1], 0.0) for s in slopes], 0)
        high = parts.astype(bf16).astype(f32)
        scatter[:, tile(t)] = jnp.concatenate([high, parts - high], 0).astype(bf16)
    sums = lax.dot_general(
        scatter[...], st.hot[...], (((1,), (1,)), ((), ())), preferred_element_type=f32
    )
    payload[...] = jnp.zeros(payload.shape, f32)
    for q in range(3):
        at = ranks * q
        total = jnp.broadcast_to(jnp.sum(slopes[q], axis=0, keepdims=True), (8, 128))
        total = group_sum(total)[0:1, 0:32]
        part = -(sums[at : at + ranks] + sums[3 * ranks + at : 4 * ranks + at])
        payload[at : at + ranks, 0:32] = part + jnp.where(
            rows_of((ranks, 32)) == me, total, 0.0
        )
    payload[3 * ranks : 3 * ranks + 3, 0:32] = tgt[...]
    payload[3 * ranks + 3 : 3 * ranks + 4, 0:32] = (lanes((1, 32)) < live[0, 0]).astype(f32)

    def spread(j, carry):
        pay[j] = payload[...]
        return carry

    lax.fori_loop(0, ranks, spread, 0)


def outer(*pairs):
    full = None
    for x, y in pairs:
        part = lax.dot_general(x, y, (((1,), (1,)), ((), ())), preferred_element_type=f32)
        full = part if full is None else full + part
    rows, columns = full.shape[0] // 2, full.shape[1] // 2
    if columns == 64:
        return full[:rows] + (spin(full[:rows], 64) + full[rows:])
    return full[:rows, :columns] + (full[:rows, columns:] + full[rows:, :columns])


def pack(value, tmp):
    count = value.shape[0]
    tmp[0:count, :] = value
    even, odd = tmp[pl.ds(0, count // 2, stride=2), :], tmp[pl.ds(1, count // 2, stride=2), :]
    return jnp.where(lanes(even.shape) < 64, even, spin(odd, 64))


def second_kernel(ranks, axis, pick, live, got, *refs):
    st = Refs(STATE, refs[: len(STATE)])
    keep, give, forces, tm, aim = refs[len(STATE) : len(STATE) + 5]
    sc = Refs(SCRATCH_B, refs[len(STATE) + 5 :])
    me = lax.axis_index(axis)
    geo, gd = st.geo, sc.gd

    total = got[0, 0 : 3 * ranks, :]
    for j in range(1, ranks):
        total = total + got[j, 0 : 3 * ranks, :]
    for j in range(ranks):
        for q in range(4):
            tm[q * ranks + j : q * ranks + j + 1, :] = got[j, 3 * ranks + q : 3 * ranks + q + 1, :]
    mask = tm[3 * ranks : 4 * ranks, :]
    mine = rows_of((ranks, 128)) == me
    loss = jnp.zeros((ranks, 128), f32)
    centre = []
    for q in range(3):
        at = slice(q * ranks, q * ranks + ranks)
        error = mask * (total[at] - tm[at, :])
        loss = loss + jnp.where(mine, error * error, 0.0)
        forces[q : q + 1, :] = jnp.sum(jnp.where(mine, total[at], 0.0), axis=0, keepdims=True)[:, 0:32]
        error = 2.0 * error
        aim[at, :] = error
        own = jnp.sum(jnp.where(mine, error, 0.0), axis=0, keepdims=True)
        centre.append(group_sum(jnp.broadcast_to(own, (8, 128)))[0:1])
    aims = aim[...]
    high = aims.astype(bf16).astype(f32)
    stacked = jnp.concatenate([high, aims - high], 0).astype(bf16)[:, 0:32]
    seen = jnp.dot(stacked, st.hot[...], preferred_element_type=f32)
    seen = seen[0 : 3 * ranks] + seen[3 * ranks :]
    for t in range(TILES):
        at_owner = rows_of((ranks, 128)) == st.owner[t : t + 1, :]
        for q in range(3):
            there = jnp.where(at_owner, seen[q * ranks : q * ranks + ranks, tile(t)], 0.0)
            sc.cdir[q, t : t + 1, :] = centre[q] - jnp.sum(there, axis=0, keepdims=True)

    xyz = tuple(st.place[q] for q in range(3))
    ways = tuple(sc.cdir[q] for q in range(3))
    _, (dd, fd, yd) = jax.jvp(geometry, xyz, ways)
    gd[0] = fd
    for m in range(8):
        gd[m + 1] = yd[m]
    gd[9] = fd * (1.0 / math.sqrt(NEI))
    for t in range(TILES):
        b, slope = st.bes[0, :, tile(t)], st.bes[1, :, tile(t)]
        row = fd[t : t + 1] * b + (geo[0, t : t + 1, :] * dd[t : t + 1]) * slope
        put(sc.phid, 0, tile(t), jnp.concatenate([row, jnp.zeros((FEAT - 8, 128), f32)], 0))

    for c in range(CHUNKS):
        cs = chunk(c)
        zd = product(st.wf_emb[...], *pair(sc.phid, cs))
        sc.zd[:, cs] = zd
        ld = st.z1[:, cs] * zd
        sc.run[:, cs] = ld
        put(sc.latd, 0, cs, ld, (0,))

    for k in range(LAYERS):
        for c in range(CHUNKS):
            cs = chunk(c)
            sc.pqd[k, :, cs] = product(st.wf_env[k], *pair(sc.latd, cs, (k,)))
        for r in range(0, 32, 16):
            rs = slice(r, r + 16)
            sums = None
            for t in range(TILES):
                ts = tile(t)
                p = st.pq[k, rs, ts]
                a = p * geo[9, t : t + 1, :]
                ad = sc.pqd[k, rs, ts] * geo[9, t : t + 1, :] + p * gd[9, t : t + 1, :]
                terms = [ad] + [
                    ad * geo[m, t : t + 1, :] + a * gd[m, t : t + 1, :] for m in range(1, 9)
                ]
                sums = terms if sums is None else [x + y for x, y in zip(sums, terms, strict=True)]
            for m in range(9):
                sc.envd[k, m, rs, :] = group_sum(sums[m])
        for r in range(0, 32, 8):
            rs = slice(r, r + 8)
            envs = [[st.env[j, m, rs, :] for m in range(9)] for j in range(k + 1)]
            envds = [[sc.envd[j, m, rs, :] for m in range(9)] for j in range(k + 1)]
            _, (base, factors) = jax.jvp(atom_terms, (envs,), (envds,))
            for l in range(3):
                sc.bd[k, l, rs, :] = base[l]
            for m in range(8):
                sc.ehd[k, m, rs, :] = factors[m]
        for r in range(0, 32, 16):
            rs = slice(r, r + 16)
            ru = slice(32 + r, 48 + r)
            for t in range(TILES):
                ts = tile(t)
                qd = sc.pqd[k, ru, ts]
                if k > 0:
                    qd = mix * (
                        sc.qd[k - 1, rs, ts] * st.pq[k, ru, ts] + st.qq[k - 1, rs, ts] * qd
                    )
                sc.qd[k, rs, ts] = qd
                q = st.qq[k, rs, ts]
                values = [st.bb[k, 0, rs, :], st.vv[k, rs, ts], st.vv[k, ru, ts]]
                moves = [sc.bd[k, l, rs, :] for l in range(3)]
                for m in range(1, 9):
                    l = degree(m)
                    moves[l] = (
                        moves[l]
                        + geo[m, t : t + 1, :] * sc.ehd[k, m - 1, rs, :]
                        + gd[m, t : t + 1, :] * st.eh[k, m - 1, rs, :]
                    )
                sc.vvd[k, rs, ts] = moves[1]
                sc.vvd[k, ru, ts] = moves[2]
                for l in range(3):
                    put(sc.ivd, 32 * l + r, ts, qd * values[l] + q * moves[l], (k,))
        for c in range(CHUNKS):
            cs = chunk(c)
            ind = sc.run[:, cs] + product(st.wf_inv[k], *pair(sc.ivd, cs, (k,)))
            hd = product(st.wf_one[k], *put(sc.ind, 0, cs, ind, (k,)))
            sc.hd[k, :, cs] = hd
            od = product(st.wf_two[k], *put(sc.sd, 0, cs, st.s1[k, :, cs] * hd, (k,)))
            ld = sc.run[:, cs] + wide(gd, 0, c) * st.oo[k, :, cs] + wide(geo, 0, c) * od
            sc.run[:, cs] = ld
            put(sc.latd, 0, cs, ld, (k + 1,))

    per = CH // 128
    vector = jnp.zeros((128, 128), f32)
    for c in range(CHUNKS):
        cs = chunk(c)
        hhd = product(st.wf_head[...], *pair(sc.latd, cs, (3,)))
        fw, fdw = wide(geo, 0, c), wide(gd, 0, c)
        h1 = st.h1[:, cs]
        whcol = jnp.concatenate([st.whcol[...]] * per, 1)
        part = fw * h1 * hhd + fdw * st.sh[:, cs]
        for j in range(per):
            vector = vector + part[:, 128 * j : 128 * j + 128]
        back = put(sc.hht, 0, cs, whcol * (fdw * h1 + fw * st.h2[:, cs] * hhd))
        sc.run[:, cs] = product(st.wb_head[...], *back)
    sc.grad[AT_HEAD : AT_HEAD + 64, :] = outer((sc.latd[3], st.hhb[...]), (st.latx[3], sc.hht[...]))
    sc.grad[AT_VEC : AT_VEC + 1, :] = jnp.sum(vector.T, axis=0, keepdims=True)

    for k in reversed(range(LAYERS)):
        for c in range(CHUNKS):
            cs = chunk(c)
            lt = sc.run[:, cs]
            ot = wide(gd, 0, c) * st.lb[k, :, cs] + wide(geo, 0, c) * lt
            tt = product(st.wb_two[k], *put(sc.ot, 0, cs, ot))
            ht = tt * st.s1[k, :, cs] + st.t2[k, :, cs] * sc.hd[k, :, cs]
            it = product(st.wb_one[k], *put(sc.ht, 0, cs, ht))
            sc.vt[:, cs] = product(st.wb_inv[k], *put(sc.it, 0, cs, it))
            sc.run[:, cs] = lt + it
        for r in range(0, 32, 16):
            rs = slice(r, r + 16)
            ru = slice(32 + r, 48 + r)
            sums = None
            for t in range(TILES):
                ts = tile(t)
                q, qd = st.qq[k, rs, ts], sc.qd[k, rs, ts]
                ls = [slice(32 * l + r, 32 * l + r + 16) for l in range(3)]
                vb = [st.vb[k, s, ts] for s in ls]
                vt = [sc.vt[s, ts] for s in ls]
                qt = (
                    vt[0] * st.bb[k, 0, rs, :]
                    + vt[1] * st.vv[k, rs, ts]
                    + vt[2] * st.vv[k, ru, ts]
                    + vb[0] * sc.bd[k, 0, rs, :]
                    + vb[1] * sc.vvd[k, rs, ts]
                    + vb[2] * sc.vvd[k, ru, ts]
                )
                if k < LAYERS - 1:
                    qt = qt + mix * (
                        sc.pqd[k + 1, ru, ts] * st.qb[k + 1, rs, ts]
                        + st.pq[k + 1, ru, ts] * sc.qt[k + 1, rs, ts]
                    )
                sc.qt[k, rs, ts] = qt
                back = [x * q for x in vb]
                turn = [x * q + y * qd for x, y in zip(vt, vb, strict=True)]
                terms = list(turn)
                for m in range(1, 9):
                    l = degree(m)
                    terms.append(turn[l] * geo[m, t : t + 1, :] + back[l] * gd[m, t : t + 1, :])
                sums = terms if sums is None else [x + y for x, y in zip(sums, terms, strict=True)]
            for n in range(11):
                sc.cott[n, rs, :] = group_sum(sums[n])
        for r in range(0, 32, 8):
            rs = slice(r, r + 8)
            envs = [[st.env[j, m, rs, :] for m in range(9)] for j in range(k + 1)]
            envds = [[sc.envd[j, m, rs, :] for m in range(9)] for j in range(k + 1)]
            cots = [st.cot[k, n, rs, :] for n in range(11)]
            cotts = [sc.cott[n, rs, :] for n in range(11)]
            _, back = jax.jvp(
                atom_back,
                (envs, (cots[:3], cots[3:])),
                (envds, (cotts[:3], cotts[3:])),
            )
            for j in range(k + 1):
                for m in range(9):
                    if k == LAYERS - 1:
                        sc.et[j, m, rs, :] = back[j][m]
                    else:
                        sc.et[j, m, rs, :] += back[j][m]
        for r in range(0, 32, 16):
            rs = slice(r, r + 16)
            for t in range(TILES):
                ts = tile(t)
                at = sc.et[k, 0, rs, :]
                for m in range(1, 9):
                    at = (
                        at
                        + geo[m, t : t + 1, :] * sc.et[k, m, rs, :]
                        + gd[m, t : t + 1, :] * st.eb[k, m, rs, :]
                    )
                pt = at * geo[9, t : t + 1, :] + st.ab[k, rs, ts] * gd[9, t : t + 1, :]
                put(sc.pt, r, ts, pt)
                qt = sc.qt[k, rs, ts]
                if k > 0:
                    qt = mix * (sc.qd[k - 1, rs, ts] * st.qb[k, rs, ts] + st.qq[k - 1, rs, ts] * qt)
                put(sc.pt, 32 + r, ts, qt)
        for c in range(CHUNKS):
            cs = chunk(c)
            lt = sc.run[:, cs] + product(st.wb_env[k], *pair(sc.pt, cs))
            sc.run[:, cs] = lt
            if k == 0:
                put(sc.zt, 0, cs, lt * st.z1[:, cs] + st.tz[:, cs] * sc.zd[:, cs])
        at = AT_TWO + 64 * k
        sc.grad[at : at + 64, :] = pack(outer((sc.sd[k], st.ob[k]), (st.sx[k], sc.ot[...])), sc.tmp)
        at = AT_ONE + 64 * k
        sc.grad[at : at + 64, :] = outer((sc.ind[k], st.hb[k]), (st.inx[k], sc.ht[...]))
        at = AT_INV + 48 * k
        sc.grad[at : at + 48, :] = pack(outer((sc.ivd[k], st.ib[k]), (st.ivx[k], sc.it[...])), sc.tmp)
        at = AT_ENV + 32 * k
        sc.grad[at : at + 32, :] = pack(outer((sc.latd[k], st.pb[k]), (st.latx[k], sc.pt[...])), sc.tmp)
    packed = pack(outer((sc.phid[...], st.zb[...]), (st.phi[...], sc.zt[...])), sc.tmp)
    sc.grad[0:9, :] = packed[0:9]
    sc.grad[ROWS:PADDED, :] = jnp.zeros((PADDED - ROWS, 128), f32)
    lane = lanes((1, 128))
    amount = 3.0 * live[0, 0].astype(f32)
    sc.grad[ROWS : ROWS + 1, :] = jnp.where(
        lane == 0, jnp.sum(loss), jnp.where(lane == 1, amount, 0.0)
    )
    half = lax.axis_index(pick)
    keep[...] = sc.grad[pl.ds(pl.multiple_of(half * HALF, HALF), HALF), :]
    give[...] = sc.grad[pl.ds(pl.multiple_of((1 - half) * HALF, HALF), HALF), :]


def third_kernel(pick, mine, other, par, first, second, avg, *outs):
    loss, count, norm, new_first, new_second, new_par, low, new_avg = outs
    half = lax.axis_index(pick)
    lower = jnp.where(half == 0, mine[...], other[...])
    upper = jnp.where(half == 0, other[...], mine[...])
    last = ROWS - HALF
    scalars = upper[last : last + 1]
    loss[...] = scalars[:, 0:1]
    amount = scalars[:, 1:2]
    count[...] = amount
    squares = jnp.sum(lower * lower, keepdims=True) + jnp.sum(
        upper[0:last] * upper[0:last], keepdims=True
    )
    length = jnp.sqrt(squares) / amount
    norm[...] = length
    factor = (clip_level / jnp.maximum(length, clip_level)) / amount
    for start, stop, value in ((0, HALF, lower), (HALF, ROWS, upper[0:last])):
        rows = slice(start, stop)
        gradient = value * factor
        one = beta_one * first[rows, :] + (1.0 - beta_one) * gradient
        two = beta_two * second[rows, :] + (1.0 - beta_two) * gradient * gradient
        fixed_one = one / (1.0 - beta_one**STEP)
        fixed_two = two / (1.0 - beta_two**STEP)
        weights = par[rows, :]
        weights = weights - learn_rate * (
            fixed_one / (jnp.sqrt(fixed_two) + epsilon_adam) + decay_rate * weights
        )
        new_first[rows, :] = one
        new_second[rows, :] = two
        new_par[rows, :] = weights
        low[rows, :] = weights.astype(bf16)
        new_avg[rows, :] = average_keep * avg[rows, :] + (1.0 - average_keep) * weights


VMEM = pl.BlockSpec(memory_space=pltpu.VMEM)
SMEM = pl.BlockSpec(memory_space=pltpu.SMEM)


def scratch(entries):
    return [pltpu.VMEM(shape, dtype) for _, shape, dtype in entries]


def local(
    ranks,
    wide_axes,
    params,
    first_moment,
    second_moment,
    average,
    edge_vectors,
    owner_rank,
    neighbour_local,
    centre_species,
    neighbour_species,
    live_atoms,
    target_forces,
):
    shape = jax.ShapeDtypeStruct
    flat = (ROWS, 128)
    par = params.reshape(flat)
    live = live_atoms.reshape(1, 1)
    tall = 3 * ranks + 8
    parts = len(wide_axes[1])
    state = [shape(s, t) for _, s, t in STATE]
    pay, *kept = pl.pallas_call(
        functools.partial(first_kernel, ranks, "atoms"),
        out_shape=[shape((ranks, tall, 128), f32), *state],
        in_specs=[VMEM] * 6 + [SMEM, VMEM],
        out_specs=[VMEM] * (1 + len(state)),
        scratch_shapes=[
            pltpu.VMEM((16, 192), bf16),
            pltpu.VMEM((tall, 128), f32),
            pltpu.VMEM((6 * ranks, EDGES), bf16),
            *scratch(SCRATCH_A),
        ],
        compiler_params=pltpu.CompilerParams(vmem_limit_bytes=16 * 2**20),
        name="forward",
    )(
        par,
        edge_vectors.reshape(3, 8, 128),
        owner_rank.reshape(8, 128),
        neighbour_local.reshape(8, 128),
        neighbour_species.reshape(8, 128),
        centre_species.reshape(1, ATOMS),
        live,
        target_forces.reshape(3, ATOMS),
    )
    got = lax.all_to_all(pay, "atoms", split_axis=0, concat_axis=0, tiled=True)
    keep, give, forces = pl.pallas_call(
        functools.partial(second_kernel, ranks, "atoms", "low"),
        out_shape=[shape((HALF, 128), f32), shape((HALF, 128), f32), shape((3, ATOMS), f32)],
        in_specs=[SMEM, VMEM] + [VMEM] * len(state),
        out_specs=[VMEM] * 3,
        scratch_shapes=[
            pltpu.VMEM((4 * ranks, 128), f32),
            pltpu.VMEM((3 * ranks, 128), f32),
            *scratch(SCRATCH_B),
        ],
        compiler_params=pltpu.CompilerParams(vmem_limit_bytes=20 * 2**20),
        name="gradient",
    )(live, got, *kept)
    swap = [(0, 1), (1, 0)]
    axes, size = ("atoms", "high"), ranks * 2
    held = keep + lax.ppermute(give, "low", swap)
    pieces = size * 8 * -(-HALF // (8 * size))
    held = jnp.pad(held, ((0, pieces - HALF), (0, 0))).reshape(size, pieces // size, 128)
    summed = lax.all_to_all(held, axes, split_axis=0, concat_axis=0, tiled=True).sum(0)
    summed = jnp.broadcast_to(summed[None], (size, *summed.shape))
    mine = lax.all_to_all(summed, axes, split_axis=0, concat_axis=0, tiled=True)
    mine = mine.reshape(pieces, 128)[:HALF]
    other = lax.ppermute(mine, "low", swap)
    one, vec = shape((1, 1), f32), shape(flat, f32)
    loss, count, norm, new_first, new_second, new_params, low, new_average = pl.pallas_call(
        functools.partial(third_kernel, "low"),
        out_shape=[one, one, one, vec, vec, vec, shape(flat, bf16), vec],
        in_specs=[VMEM] * 6,
        out_specs=[VMEM] * 8,
        compiler_params=pltpu.CompilerParams(vmem_limit_bytes=16 * 2**20),
        name="update",
    )(
        mine,
        other,
        par,
        first_moment.reshape(flat),
        second_moment.reshape(flat),
        average.reshape(flat),
    )
    return (
        loss.reshape(()),
        count.reshape(()),
        norm.reshape(()),
        forces.reshape(3, 1, ATOMS),
        new_first.reshape(-1),
        new_second.reshape(-1),
        new_params.reshape(-1),
        low.reshape(-1),
        new_average.reshape(-1),
    )


def solution(mesh):
    ranks, groups = mesh.shape["atoms"], mesh.shape["grp"]
    fine = Mesh(mesh.devices.reshape(ranks, groups // 2, 2), ("atoms", "high", "low"))
    grp = ("high", "low")
    in_specs = (
        P(),
        P(),
        P(),
        P(),
        P(None, grp, "atoms"),
        P(grp, "atoms", None),
        P(grp, "atoms"),
        P(grp, "atoms"),
        P(grp, "atoms"),
        P(grp, "atoms"),
        P(None, grp, "atoms"),
    )
    out_specs = (P(), P(), P(), P(None, grp, "atoms"), P(), P(), P(), P(), P())
    return jax.shard_map(
        functools.partial(local, ranks, (("atoms", "high"), grp)),
        mesh=fine,
        in_specs=in_specs,
        out_specs=out_specs,
        check_vma=False,
    )
```

profile of v0, /device:TPU:0, one launch (start us, length us, event | category | flops | bytes accessed | tf_op | source)
XLA Modules:
  0.0 76.8 jit_solution(7696013238448973529)
XLA Ops:
  1.3 0.7 copy.23
  2.0 0.0 copy-start
  2.0 1.0 %copy-done = f32[89344]{0:T(1024)S(1)} copy-done((f32[89344]{0:T(1024)S(1)}, f32[89344]{0:T(1024)}, u32[]{:S(2)}) %copy-start) | copy-done | bytes 357400
  3.0 0.0 copy-start.5
  3.0 0.7 copy-done.5
  3.7 0.0 copy-start.6
  3.7 0.7 copy-done.6
  4.4 0.0 copy-start.7
  4.4 0.7 copy-done.7
  5.0 0.0 copy-start.8
  5.0 0.7 copy-done.8
  5.7 0.0 copy-start.9
  5.7 0.7 copy-done.9
  6.4 12.3 %forward.1 = (f32[8,32,128]{2,1,0:T(8,128)S(1)}, bf16[64,96]{1,0:T(8,128)(2,1)S(1)}, bf16[3,64,192]{2,1,0:T(8,128)(2,1)S(1)}, bf16[3,64,192]{2,1,0:T(8,128)(2,1)...) custom-call(f32[698,128]{1,0:T(8,128)S(1)} %bitcast.22, ...), custom_call_target="tpu_custom_call" | custom-call | tf_op jit(solution)/shard_map/forward/pallas_call | solution.py:911
  18.7 14.4 %all_to_all.15.got = f32[8,32,128]{2,1,0:T(8,128)S(1)} all-to-all(f32[8,32,128]{2,1,0:T(8,128)S(1)} %get-tuple-element.69), channel_id=1, replica_groups=mesh['atoms'=8,'high'=2,'low'=2] {'atoms'}, dimensions={0} | all-to-all | bytes 262144 | tf_op jit(solution)/shard_map/all_to_all | solution.py:934
  33.1 15.6 %gradient.1 = (f32[384,128]{1,0:T(8,128)S(1)}, f32[384,128]{1,0:T(8,128)S(1)}, f32[3,32]{1,0:T(4,128)S(1)}) custom-call(s32[1,1]{1,0:T(1,128)S(6)} %copy.24.live, f32[8,32,128]{2,1,0:T(8,128)S(1)} %all_to_all.15.got, bf16[64,96]{1,0:T(8,128)(2,1)S(1)} %get-tuple-element.70.refs_0_, bf16[3,64,192]{2,1,0:T(8,128)(2,1)S(1)} %get-tuple-element.71.refs_1_, ...), custom_call_target="tpu_custom_call" | custom-call | tf_op jit(solution)/shard_map/gradient/pallas_call | solution.py:935
  48.7 0.0 copy-start.1
  48.7 0.0 copy-start.2
  48.7 0.0 copy-start.3
  48.7 0.0 copy-start.4
  48.7 0.1 collective-permute-start
  48.8 1.4 %collective-permute-done = f32[384,128]{1,0:T(8,128)S(1)} collective-permute-done((f32[384,128]{1,0:T(8,128)S(1)}, f32[384,128]{1,0:T(8,128)S(1)}, u32[]{:S(2)}, u32[]{:S(2)}) %collective-permute-start) | collective-permute-done | bytes 196640 | tf_op jit(solution)/shard_map/ppermute | solution.py:950
  50.2 12.1 %all_to_all.16 = f32[16,24,128]{2,1,0:T(8,128)S(1)} all-to-all(f32[16,24,128]{2,1,0:T(8,128)S(1)} %bitcast.35), channel_id=1, replica_groups=mesh['atoms'=8,'high'=2,'low'=2] {'atoms','high'}, dimensions={0} | all-to-all | bytes 393216 | tf_op jit(solution)/shard_map/all_to_all | solution.py:953
  62.4 11.3 %all_to_all.17 = f32[16,24,128]{2,1,0:T(8,128)S(1)} all-to-all(f32[16,24,128]{2,1,0:T(8,128)S(1)} %broadcast_in_dim.2), channel_id=1, replica_groups=mesh['atoms'=8,'high'=2,'low'=2] {'atoms','high'}, dimensions={0} | all-to-all | bytes 393216 | tf_op jit(solution)/shard_map/all_to_all | solution.py:955
  73.7 0.0 collective-permute-start.1
  73.7 0.6 copy.20
  74.3 0.9 %collective-permute-done.1.other = f32[384,128]{1,0:T(8,128)S(1)} collective-permute-done((f32[384,128]{1,0:T(8,128)S(1)}, f32[384,128]{1,0:T(8,128)S(1)}, u32[]{:S(2)}, u32[]{:S(2)}) %collective-permute-start.1) | collective-permute-done | bytes 196640 | tf_op jit(solution)/shard_map/ppermute | solution.py:957
  75.1 0.0 copy-done.1
  75.1 0.0 copy-done.2
  75.1 0.0 copy-done.3
  75.1 0.0 copy-done.4
  75.2 1.7 %update.1 = (f32[1,1]{1,0:T(1,128)}, f32[1,1]{1,0:T(1,128)}, f32[1,1]{1,0:T(1,128)}, f32[698,128]{1,0:T(8,128)}, f32[698,128]{1,0:T(8,128)}, /*index=5*/f32[698,...) custom-call(f32[384,128]{1,0:T(8,128)S(1)} %bitcast.25, f32[384,128]{1,0:T(8,128)S(1)} %collective-permute-done.1.other, ...), custom_call_target="tpu_custom_call" | custom-call | tf_op jit(solution)/shard_map/update/pallas_call | solution.py:959
  (3 shorter events, 0.1 us)
Async XLA Ops:
  2.0 1.0 %copy-start = (f32[89344]{0:T(1024)S(1)}, f32[89344]{0:T(1024)}, u32[]{:S(2)}) copy-start(f32[89344]{0:T(1024)} %param.11) | copy-start | bytes 1072132
  3.0 0.7 copy-start.5
  3.7 0.7 copy-start.6
  4.4 0.7 copy-start.7
  5.0 0.7 copy-start.8
  5.7 0.7 copy-start.9
  48.7 26.5 %copy-start.1 = (f32[89344]{0:T(1024)S(1)}, f32[89344]{0:T(1024)}, u32[]{:S(2)}) copy-start(f32[89344]{0:T(1024)} %param.11) | copy-start | bytes 1072132
  48.7 26.5 %copy-start.2 = (f32[89344]{0:T(1024)S(1)}, f32[89344]{0:T(1024)}, u32[]{:S(2)}) copy-start(f32[89344]{0:T(1024)} %param.12) | copy-start | bytes 1072132
  48.7 26.5 %copy-start.3 = (f32[89344]{0:T(1024)S(1)}, f32[89344]{0:T(1024)}, u32[]{:S(2)}) copy-start(f32[89344]{0:T(1024)} %param.13) | copy-start | bytes 1072132
  48.7 26.5 %copy-start.4 = (f32[89344]{0:T(1024)S(1)}, f32[89344]{0:T(1024)}, u32[]{:S(2)}) copy-start(f32[89344]{0:T(1024)} %param.14) | copy-start | bytes 1072132
  48.7 1.5 %collective-permute-start = (f32[384,128]{1,0:T(8,128)S(1)}, f32[384,128]{1,0:T(8,128)S(1)}, u32[]{:S(2)}, u32[]{:S(2)}) collective-permute-start(f32[384,128]{1,0:T(8,128)S(1)} %get-tuple-element.119), channel_id=1, source_target_pairs={{0,1},{1,0},{2,3},{3,2},{4,5},{5,4},{6,7},{7,6},{8,9},{9,8},{10,11... | collective-permute-start | bytes 589832 | tf_op jit(solution)/shard_map/ppermute | solution.py:950
  73.7 1.4 %collective-permute-start.1 = (f32[384,128]{1,0:T(8,128)S(1)}, f32[384,128]{1,0:T(8,128)S(1)}, u32[]{:S(2)}, u32[]{:S(2)}) collective-permute-start(f32[384,128]{1,0:T(8,128)S(1)} %bitcast.24), channel_id=1, source_target_pairs={{0,1},{1,0},{2,3},{3,2},{4,5},{5,4},{6,7},{7,6},{8,9},{9,8},{10,11... | collective-permute-start | bytes 589832 | tf_op jit(solution)/shard_map/ppermute | solution.py:957
where the time goes:
time: 77.3 us; the launch traced here: 76.8 us
  blocking collectives  37.8 us (49%)
  Pallas kernels  29.6 us (38%)
  local copies, waits for them, and re-layouts  5.69 us (7%)
  waiting for transfers between devices  2.3 us (3%)
  between operations  1.37 us (2%)
    pallas_call x1, Pallas kernels, local(): pl.pallas_call(functools.partial(second_kernel, ranks, 'atoms', 'low'), o...  15.6 us
    all_to_all x1, blocking collectives, local(): got = lax.all_to_all(pay, 'atoms', split_axis=0, concat_axis=0, tiled=True)  14.4 us
    pallas_call x1, Pallas kernels, local(): pl.pallas_call(functools.partial(first_kernel, ranks, 'atoms'), out_shape...  12.3 us
    all_to_all x1, blocking collectives, local(): lax.all_to_all(held, axes, split_axis=0, concat_axis=0, tiled=True).sum(0)  12.1 us
    all_to_all x1, blocking collectives, local(): mine = lax.all_to_all(summed, axes, split_axis=0, concat_axis=0, tiled=True)  11.3 us
    unnamed x22, local copies, waits for them, and re-layouts  5.67 us
    pallas_call x1, Pallas kernels, local(): pl.pallas_call(functools.partial(third_kernel, 'low'), out_shape=[one, on...  1.7 us
  transfers between devices with their start and end apart: 2, of which 2 were waited for; matrix products, arithmetic and copies ran while one was open for 1% of the time, Pallas kernels for 0%

commit v1 on v0

--- a/solution.py
+++ b/solution.py
@@ -35,8 +35,6 @@
 ATOMS = 32
 EDGES = 1024
 TILES = 8
-CH = 256
-CHUNKS = EDGES // CH
 FEAT = 32
 
 AT_EMBED = 0
@@ -55,11 +53,16 @@
     ("wf_env", (3, 64, 192), bf16),
     ("wb_env", (3, 64, 192), bf16),
     ("wf_inv", (3, 64, 288), bf16),
-    ("wb_inv", (3, 96, 192), bf16),
     ("wf_one", (3, 128, 192), bf16),
     ("wb_one", (3, 64, 384), bf16),
+    ("wf_io", (3, 128, 288), bf16),
+    ("wb_io", (3, 96, 384), bf16),
     ("wf_two", (3, 64, 384), bf16),
     ("wb_two", (3, 128, 192), bf16),
+    ("wf_te", (2, 64, 384), bf16),
+    ("wb_te", (2, 128, 192), bf16),
+    ("wf_th", (128, 384), bf16),
+    ("wb_th", (128, 384), bf16),
     ("wf_head", (128, 192), bf16),
     ("wb_head", (64, 384), bf16),
     ("whcol", (128, 128), f32),
@@ -73,15 +76,16 @@
     ("pq", (3, 64, EDGES), f32),
     ("vv", (3, 64, EDGES), f32),
     ("ivx", (3, 192, EDGES), bf16),
-    ("inx", (3, 128, EDGES), bf16),
     ("sx", (3, 256, EDGES), bf16),
     ("s1", (3, 128, EDGES), f32),
     ("t2", (3, 128, EDGES), f32),
     ("oo", (3, 64, EDGES), f32),
+    ("ts", (2, 64, EDGES), f32),
+    ("th", (128, EDGES), f32),
     ("lb", (3, 64, EDGES), f32),
     ("ob", (3, 128, EDGES), bf16),
     ("hb", (3, 256, EDGES), bf16),
-    ("ib", (3, 128, EDGES), bf16),
+    ("xb", (3, 128, EDGES), f32),
     ("vb", (3, 96, EDGES), f32),
     ("ab", (3, 32, EDGES), f32),
     ("pb", (3, 128, EDGES), bf16),
@@ -102,15 +106,15 @@
 ]
 
 SCRATCH_A = [
-    ("tmp", (128, 128), f32),
-    ("run", (64, EDGES), f32),
+    ("tmp", (11, 128, 128), f32),
+    ("wb_emb", (16, 192), bf16),
     ("ybar", (9, 8, 8, 128), f32),
     ("dbar", (8, 8, 128), f32),
 ]
 
 SCRATCH_B = [
-    ("tmp", (128, 128), f32),
-    ("run", (64, EDGES), f32),
+    ("tmp", (8, 128, 128), f32),
+    ("part", (320, 256), f32),
     ("cdir", (3, 8, 128), f32),
     ("gd", (10, 8, 128), f32),
     ("phid", (2 * FEAT, EDGES), bf16),
@@ -120,19 +124,16 @@
     ("vvd", (3, 64, EDGES), f32),
     ("qd", (3, 32, EDGES), f32),
     ("ivd", (3, 192, EDGES), bf16),
-    ("ind", (3, 128, EDGES), bf16),
     ("hd", (3, 128, EDGES), f32),
     ("sd", (3, 256, EDGES), bf16),
     ("envd", (3, 9, 32, 128), f32),
     ("ehd", (3, 8, 32, 128), f32),
     ("bd", (3, 3, 32, 128), f32),
     ("hht", (256, EDGES), bf16),
-    ("ot", (128, EDGES), bf16),
-    ("ht", (256, EDGES), bf16),
-    ("it", (128, EDGES), bf16),
-    ("vt", (96, EDGES), f32),
+    ("ot", (3, 128, EDGES), bf16),
+    ("ht", (3, 256, EDGES), bf16),
     ("qt", (3, 32, EDGES), f32),
-    ("pt", (128, EDGES), bf16),
+    ("pt", (3, 128, EDGES), bf16),
     ("zt", (128, EDGES), bf16),
     ("et", (3, 9, 32, 128), f32),
     ("cott", (11, 32, 128), f32),
@@ -254,15 +255,6 @@
     return slice(128 * t, 128 * t + 128)
 
 
-def chunk(c):
-    return slice(CH * c, CH * c + CH)
-
-
-def wide(ref, index, c):
-    per = CH // 128
-    return jnp.concatenate([ref[index, t : t + 1, :] for t in range(per * c, per * c + per)], 1)
-
-
 def fold(value):
     total = value[0:8]
     for r in range(8, value.shape[0], 8):
@@ -301,35 +293,95 @@
     ref[(*lead, slice(None), slice(256, 288))] = low_on[:, 0:32].astype(bf16)
 
 
-def prepare(par, st, wb_emb, tmp):
+def across(ref, index):
+    return jnp.concatenate([ref[index, t : t + 1, :] for t in range(TILES)], 1)
+
+
+def spread_rows(value):
+    return jnp.concatenate([value[t : t + 1] for t in range(TILES)], 1)
+
+
+def joined(grid):
+    return jnp.concatenate([jnp.concatenate(row, 1) for row in grid], 0)
+
+
+def keep_pair(ref, lead, value):
+    high, low = split(value)
+    half = value.shape[0]
+    ref[(*lead, slice(0, half), slice(None))] = high
+    ref[(*lead, slice(half, 2 * half), slice(None))] = low
+    return high, low
+
+
+def both(ref, lead=()):
+    half = ref.shape[-2] // 2
+    return ref[(*lead, slice(0, half), slice(None))], ref[(*lead, slice(half, 2 * half), slice(None))]
+
+
+def shares(value):
+    total = fold(value)
+    return [total[:, tile(t)] for t in range(TILES)]
+
+
+def tmp_rows(w, start):
+    return jnp.concatenate([w[start : start + 2], jnp.zeros((14, 128), f32)], 0)
+
+
+def weights_product(left, right):
+    high, low = split(right)
+    return product(left, high, low)
+
+
+def prepare(par, st, sc):
+    def turned(value):
+        return value.T
+
+    spare = iter(range(11))
+
+    def doubled(at, count):
+        return unpack(par[at : at + count // 2, :], count, sc.tmp.at[next(spare)])
+
+    w = doubled(AT_EMBED, 18)
+    w = jnp.concatenate([w[0:16], tmp_rows(w, 16)], 0)
+    store_64(sc.wb_emb, (), w[0:16])
+    high = w.astype(bf16).astype(f32)
+    low = w - high
+    turn = jnp.concatenate([high, high, low, jnp.zeros((32, 128), f32)], 0).T[0:64]
+    st.wf_emb[...] = turn[:, 0 : 3 * FEAT].astype(bf16)
+    envs, ones = [], []
     for k in range(LAYERS):
-        w = unpack(par[AT_ENV + 32 * k : AT_ENV + 32 * k + 32, :], 64, tmp)
+        w = doubled(AT_ENV + 32 * k, 64)
+        envs.append(w)
         store_64(st.wb_env, (k,), w)
         store_64(st.wf_env, (k,), jnp.concatenate([w, w], 0).T[0:64])
-        w = unpack(par[AT_INV + 48 * k : AT_INV + 48 * k + 48, :], 96, tmp)
-        store_64(st.wb_inv, (k,), w)
+    head = par[AT_HEAD : AT_HEAD + 64, :]
+    for k in range(LAYERS):
+        one = par[AT_ONE + 64 * k : AT_ONE + 64 * k + 64, :]
+        store_128(st.wb_one, (k,), one)
+        store_64(st.wf_one, (k,), jnp.concatenate([one, one], 0).T)
+        w = doubled(AT_INV + 48 * k, 96)
         store_96(st.wf_inv, (k,), jnp.concatenate([w, jnp.zeros((32, 128), f32)], 0).T[0:64])
-        w = par[AT_ONE + 64 * k : AT_ONE + 64 * k + 64, :]
-        store_128(st.wb_one, (k,), w)
-        store_64(st.wf_one, (k,), jnp.concatenate([w, w], 0).T)
-        w = unpack(par[AT_TWO + 64 * k : AT_TWO + 64 * k + 64, :], 128, tmp)
-        store_64(st.wb_two, (k,), w)
+        high, low = split(w)
+        left = jnp.concatenate([high, low[:, 0:64]], 1)
+        w = weights_product(left, one)
+        store_128(st.wb_io, (k,), w)
+        store_96(st.wf_io, (k,), jnp.concatenate([w, jnp.zeros((32, 128), f32)], 0).T)
+        w = doubled(AT_TWO + 64 * k, 128)
+        high, low = split(w)
+        left = jnp.concatenate([high, low[:, 0:64]], 1)
+        st.wb_two[k] = left
         store_128(st.wf_two, (k,), w.T[0:64])
-    w = par[AT_HEAD : AT_HEAD + 64, :]
-    store_128(st.wb_head, (), w)
-    store_64(st.wf_head, (), jnp.concatenate([w, w], 0).T)
-    w = unpack(par[0:9, :], 18, tmp)
-    w = jnp.concatenate([w[0:16], jnp.where(rows_of((16, 128)) < 2, tmp_rows(w, 16), 0.0)], 0)
-    store_64(wb_emb, (), w[0:16])
-    high = w.astype(bf16).astype(f32)
-    low = w - high
-    turned = jnp.concatenate([high, high, low, jnp.zeros((32, 128), f32)], 0).T[0:64]
-    st.wf_emb[...] = turned[:, 0 : 3 * FEAT].astype(bf16)
+        if k < LAYERS - 1:
+            w = weights_product(left, envs[k + 1])
+            store_64(st.wb_te, (k,), w)
+            store_128(st.wf_te, (k,), w.T[0:64])
+        else:
+            w = weights_product(left, head)
+            store_128(st.wb_th, (), w)
+            store_128(st.wf_th, (), w.T)
+    store_128(st.wb_head, (), head)
+    store_64(st.wf_head, (), jnp.concatenate([head, head], 0).T)
     st.whcol[...] = jnp.broadcast_to(par[AT_VEC : AT_VEC + 1, :], (128, 128)).T
-
-
-def tmp_rows(w, start):
-    return jnp.concatenate([w[start : start + 2], jnp.zeros((14, 128), f32)], 0)
 
 
 def sine_parts(turns):
@@ -347,18 +399,30 @@
     return sign * rest * sine, sign * cosine
 
 
-def first_kernel(ranks, axis, par, vec, own, loc, nsp, cen, live, tgt, pay, *refs):
-    st = Refs(STATE, refs[: len(STATE)])
-    wb_emb, payload, scatter = refs[len(STATE) : len(STATE) + 3]
-    sc = Refs(SCRATCH_A, refs[len(STATE) + 3 :])
+def first_kernel(ranks, axis, live, *refs):
+    sources = refs[0:7]
+    pay = refs[7]
+    st = Refs(STATE, refs[8 : 8 + len(STATE)])
+    rest = refs[8 + len(STATE) :]
+    vec, own, loc, nsp, cen, tgt, par = rest[0:7]
+    sems, payload, scatter = rest[7:10]
+    sc = Refs(SCRATCH_A, rest[10:])
     me = lax.axis_index(axis)
-    prepare(par, st, wb_emb, sc.tmp)
-
+    copies = [
+        pltpu.make_async_copy(source, target, sems.at[n])
+        for n, (source, target) in enumerate(zip(sources, rest[0:7], strict=True))
+    ]
+    for copy in copies:
+        copy.start()
+    for copy in copies:
+        copy.wait()
+
+    order = sc.tmp.at[10]
     code = ((own[...] * 32 + loc[...]) * 8 + nsp[...]).astype(f32)
     for q, value in enumerate((vec[0], vec[1], vec[2], code)):
         for a in range(4):
-            sc.tmp[pl.ds(32 * q + a, 8, stride=4), :] = spin(value, -32 * a)
-    turned = sc.tmp[...].T
+            order[pl.ds(32 * q + a, 8, stride=4), :] = spin(value, -32 * a)
+    turned = order[...].T
     lane = lanes((8, 128))
 
     def picked(q):
@@ -375,20 +439,21 @@
     owner = lax.shift_right_logical(codes, 8)
     kind = codes & 7
     st.owner[...] = owner
-    sc.tmp[0:8, :] = jnp.zeros((8, 128), f32)
-    sc.tmp[0:1, 0:32] = cen[...].astype(f32)
-    centre_kind = group_sum(sc.tmp[0:8, :])[0:1].astype(jnp.int32)
+    sc.dbar[0] = jnp.zeros((8, 128), f32)
+    sc.dbar[0, 0:1, 0:32] = cen[...].astype(f32)
+    centre_kind = group_sum(sc.dbar[0])[0:1].astype(jnp.int32)
 
     d, f, harmonics = geometry(*xyz)
-    st.geo[0] = f
+    geo = st.geo
+    geo[0] = f
     for m in range(8):
-        st.geo[m + 1] = harmonics[m]
-    st.geo[9] = f * (1.0 / math.sqrt(NEI))
-    geo = st.geo
+        geo[m + 1] = harmonics[m]
+    geo[9] = f * (1.0 / math.sqrt(NEI))
 
     orders = (rows_of((8, 128)) + 1).astype(f32)
     inv_d = 1.0 / d
     scale = math.sqrt(2.0 / cutoff_radius)
+    tiles = []
     for t in range(TILES):
         row_inv = inv_d[t : t + 1]
         sine, cosine = sine_parts(orders * (d[t : t + 1] / cutoff_radius))
@@ -398,27 +463,29 @@
         st.bes[1, :, tile(t)] = slope
         row = rows_of((FEAT - 8, 128)) + 8
         hot = (row == centre_kind + 8) | (row == kind[t : t + 1] + 13)
-        features = jnp.concatenate([b * f[t : t + 1], hot.astype(f32)], 0)
-        put(st.phi, 0, tile(t), features)
+        tiles.append(jnp.concatenate([b * f[t : t + 1], hot.astype(f32)], 0))
         st.hot[:, tile(t)] = (rows_of((ATOMS, 128)) == local[t : t + 1]).astype(f32).astype(bf16)
-
-    for c in range(CHUNKS):
-        cs = chunk(c)
-        s, s1, s2 = silu_parts(product(st.wf_emb[...], *pair(st.phi, cs)))
-        st.z1[:, cs] = s1
-        st.tz[:, cs] = s2
-        sc.run[:, cs] = s
-        put(st.latx, 0, cs, s, (0,))
+    phi = keep_pair(st.phi, (), jnp.concatenate(tiles, 1))
+
+    prepare(par, st, sc)
+    fw = spread_rows(f)
+
+    s, s1, s2 = silu_parts(product(st.wf_emb[...], *phi))
+    st.z1[...] = s1
+    st.tz[...] = s2
+    latent = s
+    lat = keep_pair(st.latx, (0,), s)
+    pq = product(st.wf_env[0], *lat)
+    base = product(st.wf_one[0], *lat)
+    ahead = product(st.wf_env[1], *lat)
+    st.pq[0] = pq
 
     for k in range(LAYERS):
-        for c in range(CHUNKS):
-            cs = chunk(c)
-            st.pq[k, :, cs] = product(st.wf_env[k], *pair(st.latx, cs, (k,)))
         for r in range(0, 32, 16):
             rs = slice(r, r + 16)
             sums = None
             for t in range(TILES):
-                a = st.pq[k, rs, tile(t)] * geo[9, t : t + 1, :]
+                a = pq[rs, tile(t)] * geo[9, t : t + 1, :]
                 terms = [a] + [a * geo[m, t : t + 1, :] for m in range(1, 9)]
                 sums = terms if sums is None else [x + y for x, y in zip(sums, terms, strict=True)]
             for m in range(9):
@@ -426,16 +493,18 @@
         for r in range(0, 32, 8):
             rs = slice(r, r + 8)
             envs = [[st.env[j, m, rs, :] for m in range(9)] for j in range(k + 1)]
-            base, factors = atom_terms(envs)
+            level, factors = atom_terms(envs)
             for l in range(3):
-                st.bb[k, l, rs, :] = base[l]
+                st.bb[k, l, rs, :] = level[l]
             for m in range(8):
                 st.eh[k, m, rs, :] = factors[m]
+        high = [[None] * TILES for _ in range(6)]
+        low = [[None] * TILES for _ in range(6)]
         for r in range(0, 32, 16):
             rs = slice(r, r + 16)
             for t in range(TILES):
                 ts = tile(t)
-                q = st.pq[k, 32 + r : 48 + r, ts]
+                q = pq[32 + r : 48 + r, ts]
                 if k > 0:
                     q = mix * st.qq[k - 1, rs, ts] * q
                 st.qq[k, rs, ts] = q
@@ -446,62 +515,75 @@
                 st.vv[k, rs, ts] = values[1]
                 st.vv[k, 32 + r : 48 + r, ts] = values[2]
                 for l in range(3):
-                    put(st.ivx, 32 * l + r, ts, q * values[l], (k,))
-        for c in range(CHUNKS):
-            cs = chunk(c)
-            inner = sc.run[:, cs] + product(st.wf_inv[k], *pair(st.ivx, cs, (k,)))
-            h = product(st.wf_one[k], *put(st.inx, 0, cs, inner, (k,)))
-            s, s1, s2 = silu_parts(h)
-            st.s1[k, :, cs] = s1
-            st.t2[k, :, cs] = s2
-            o = product(st.wf_two[k], *put(st.sx, 0, cs, s, (k,)))
-            st.oo[k, :, cs] = o
-            latent = sc.run[:, cs] + wide(geo, 0, c) * o
-            sc.run[:, cs] = latent
-            put(st.latx, 0, cs, latent, (k + 1,))
-
-    per = CH // 128
-    for c in range(CHUNKS):
-        cs = chunk(c)
-        s, s1, s2 = silu_parts(product(st.wf_head[...], *pair(st.latx, cs, (3,))))
-        st.sh[:, cs] = s
-        st.h1[:, cs] = s1
-        st.h2[:, cs] = s2
-        whcol = jnp.concatenate([st.whcol[...]] * per, 1)
-        energy = whcol * s
-        for j in range(per):
-            sc.ybar[0, per * c + j] = fold(energy[:, 128 * j : 128 * j + 128])
-        back = put(st.hhb, 0, cs, wide(geo, 0, c) * whcol * s1)
-        st.lb[2, :, cs] = product(st.wb_head[...], *back)
+                    n = 2 * l + r // 16
+                    high[n][t], low[n][t] = split(q * values[l])
+        high, low = joined(high), joined(low)
+        st.ivx[k, 0:96, :] = high
+        st.ivx[k, 96:192, :] = low
+        h = base + product(st.wf_io[k], high, low)
+        s, s1, s2 = silu_parts(h)
+        st.s1[k] = s1
+        st.t2[k] = s2
+        pair_s = keep_pair(st.sx, (k,), s)
+        if k < LAYERS - 1:
+            step = product(st.wf_te[k], *pair_s)
+            st.ts[k] = step
+            pq = ahead + fw * step
+            st.pq[k + 1] = pq
+        else:
+            step = product(st.wf_th[...], *pair_s)
+            st.th[...] = step
+            hh = ahead + fw * step
+        o = product(st.wf_two[k], *pair_s)
+        st.oo[k] = o
+        latent = latent + fw * o
+        lat = keep_pair(st.latx, (k + 1,), latent)
+        if k < LAYERS - 1:
+            base = product(st.wf_one[k + 1], *lat)
+            ahead = product(st.wf_env[k + 2] if k + 2 < LAYERS else st.wf_head[...], *lat)
+
+    s, s1, s2 = silu_parts(hh)
+    st.sh[...] = s
+    st.h1[...] = s1
+    st.h2[...] = s2
+    whcol = jnp.concatenate([st.whcol[...]] * TILES, 1)
+    back = keep_pair(st.hhb, (), fw * whcol * s1)
+    for t, share in enumerate(shares(whcol * s)):
+        sc.ybar[0, t] = share
+    xb = product(st.wb_th[...], *back)
+    lb = product(st.wb_head[...], *back)
 
     for k in reversed(range(LAYERS)):
-        for c in range(CHUNKS):
-            cs = chunk(c)
-            lb = st.lb[k, :, cs]
-            share = st.oo[k, :, cs] * lb
-            for j in range(per):
-                sc.ybar[0, per * c + j] += fold(share[:, 128 * j : 128 * j + 128])
-            sb = product(st.wb_two[k], *put(st.ob, 0, cs, wide(geo, 0, c) * lb, (k,)))
-            st.t2[k, :, cs] = st.t2[k, :, cs] * sb
-            ib = product(st.wb_one[k], *put(st.hb, 0, cs, st.s1[k, :, cs] * sb, (k,)))
-            st.vb[k, :, cs] = product(st.wb_inv[k], *put(st.ib, 0, cs, ib, (k,)))
-            sc.run[:, cs] = lb + ib
+        st.xb[k] = xb
+        sb = fw * xb
+        pair_h = keep_pair(st.hb, (k,), st.s1[k] * sb)
+        st.t2[k] = st.t2[k] * sb
+        vb = product(st.wb_io[k], *pair_h)
+        ib = product(st.wb_one[k], *pair_h)
+        st.vb[k] = vb
+        st.lb[k] = lb
+        keep_pair(st.ob, (k,), fw * lb)
+        for t, share in enumerate(shares(st.oo[k] * lb)):
+            sc.ybar[0, t] += share
+        run = lb + ib
+        if k > 0:
+            ahead = product(st.wb_two[k - 1], *split(run))
         for r in range(0, 32, 16):
             rs = slice(r, r + 16)
             sums = None
             for t in range(TILES):
                 ts = tile(t)
                 q = st.qq[k, rs, ts]
-                vb = [st.vb[k, 32 * l + r : 32 * l + r + 16, ts] for l in range(3)]
+                vs = [vb[32 * l + r : 32 * l + r + 16, ts] for l in range(3)]
                 qb = (
-                    vb[0] * st.bb[k, 0, rs, :]
-                    + vb[1] * st.vv[k, rs, ts]
-                    + vb[2] * st.vv[k, 32 + r : 48 + r, ts]
+                    vs[0] * st.bb[k, 0, rs, :]
+                    + vs[1] * st.vv[k, rs, ts]
+                    + vs[2] * st.vv[k, 32 + r : 48 + r, ts]
                 )
                 if k < LAYERS - 1:
                     qb = qb + mix * st.pq[k + 1, 32 + r : 48 + r, ts] * st.qb[k + 1, rs, ts]
                 st.qb[k, rs, ts] = qb
-                back = [x * q for x in vb]
+                back = [x * q for x in vs]
                 terms = list(back)
                 for m in range(1, 9):
                     terms.append(back[degree(m)] * geo[m, t : t + 1, :])
@@ -524,6 +606,8 @@
                         st.eb[j, m, rs, :] = back[j][m]
                     else:
                         st.eb[j, m, rs, :] += back[j][m]
+        high = [[None] * TILES for _ in range(4)]
+        low = [[None] * TILES for _ in range(4)]
         for r in range(0, 32, 16):
             rs = slice(r, r + 16)
             for t in range(TILES):
@@ -538,24 +622,24 @@
                     sc.ybar[m, t] += fold(a * e)
                 st.ab[k, rs, ts] = ab
                 sc.ybar[0, t] += fold((1.0 / math.sqrt(NEI)) * ab * p)
-                put(st.pb, r, ts, ab * fs, (k,))
                 qb = st.qb[k, rs, ts]
                 if k > 0:
                     qb = mix * st.qq[k - 1, rs, ts] * qb
-                put(st.pb, 32 + r, ts, qb, (k,))
-        for c in range(CHUNKS):
-            cs = chunk(c)
-            lb = sc.run[:, cs] + product(st.wb_env[k], *pair(st.pb, cs, (k,)))
-            if k > 0:
-                st.lb[k - 1, :, cs] = lb
-                continue
-            st.tz[:, cs] = st.tz[:, cs] * lb
-            pb = product(wb_emb[...], *put(st.zb, 0, cs, st.z1[:, cs] * lb))[0:8]
-            for j in range(per):
-                t = per * c + j
-                part = pb[:, 128 * j : 128 * j + 128]
-                sc.ybar[0, t] += st.bes[0, :, tile(t)] * part
-                sc.dbar[t] = geo[0, t : t + 1, :] * st.bes[1, :, tile(t)] * part
+                high[r // 16][t], low[r // 16][t] = split(ab * fs)
+                high[2 + r // 16][t], low[2 + r // 16][t] = split(qb)
+        high, low = joined(high), joined(low)
+        st.pb[k, 0:64, :] = high
+        st.pb[k, 64:128, :] = low
+        if k > 0:
+            xb = ahead + product(st.wb_te[k - 1], high, low)
+        lb = run + product(st.wb_env[k], high, low)
+
+    st.tz[...] = st.tz[...] * lb
+    pb = product(sc.wb_emb[...], *keep_pair(st.zb, (), st.z1[...] * lb))[0:8]
+    for t in range(TILES):
+        part = pb[:, tile(t)]
+        sc.ybar[0, t] += st.bes[0, :, tile(t)] * part
+        sc.dbar[t] = geo[0, t : t + 1, :] * st.bes[1, :, tile(t)] * part
 
     bars = [jnp.sum(sc.ybar[m], axis=1) for m in range(9)]
     slopes = jax.vjp(geometry, *xyz)[1]((jnp.sum(sc.dbar[...], axis=1), bars[0], bars[1:]))
@@ -577,7 +661,8 @@
         payload[at : at + ranks, 0:32] = part + jnp.where(
             rows_of((ranks, 32)) == me, total, 0.0
         )
-    payload[3 * ranks : 3 * ranks + 3, 0:32] = tgt[...]
+    for q in range(3):
+        payload[3 * ranks + q : 3 * ranks + q + 1, 0:32] = tgt[q]
     payload[3 * ranks + 3 : 3 * ranks + 4, 0:32] = (lanes((1, 32)) < live[0, 0]).astype(f32)
 
     def spread(j, carry):
@@ -587,11 +672,11 @@
     lax.fori_loop(0, ranks, spread, 0)
 
 
-def outer(*pairs):
-    full = None
-    for x, y in pairs:
-        part = lax.dot_general(x, y, (((1,), (1,)), ((), ())), preferred_element_type=f32)
-        full = part if full is None else full + part
+def cross(x, y):
+    return lax.dot_general(x, y, (((1,), (1,)), ((), ())), preferred_element_type=f32)
+
+
+def settle(full):
     rows, columns = full.shape[0] // 2, full.shape[1] // 2
     if columns == 64:
         return full[:rows] + (spin(full[:rows], 64) + full[rows:])
@@ -626,7 +711,7 @@
         at = slice(q * ranks, q * ranks + ranks)
         error = mask * (total[at] - tm[at, :])
         loss = loss + jnp.where(mine, error * error, 0.0)
-        forces[q : q + 1, :] = jnp.sum(jnp.where(mine, total[at], 0.0), axis=0, keepdims=True)[:, 0:32]
+        forces[q] = jnp.sum(jnp.where(mine, total[at], 0.0), axis=0, keepdims=True)[:, 0:32]
         error = 2.0 * error
         aim[at, :] = error
         own = jnp.sum(jnp.where(mine, error, 0.0), axis=0, keepdims=True)
@@ -649,23 +734,24 @@
     for m in range(8):
         gd[m + 1] = yd[m]
     gd[9] = fd * (1.0 / math.sqrt(NEI))
+    tiles = []
     for t in range(TILES):
         b, slope = st.bes[0, :, tile(t)], st.bes[1, :, tile(t)]
         row = fd[t : t + 1] * b + (geo[0, t : t + 1, :] * dd[t : t + 1]) * slope
-        put(sc.phid, 0, tile(t), jnp.concatenate([row, jnp.zeros((FEAT - 8, 128), f32)], 0))
-
-    for c in range(CHUNKS):
-        cs = chunk(c)
-        zd = product(st.wf_emb[...], *pair(sc.phid, cs))
-        sc.zd[:, cs] = zd
-        ld = st.z1[:, cs] * zd
-        sc.run[:, cs] = ld
-        put(sc.latd, 0, cs, ld, (0,))
+        tiles.append(jnp.concatenate([row, jnp.zeros((FEAT - 8, 128), f32)], 0))
+    phid = keep_pair(sc.phid, (), jnp.concatenate(tiles, 1))
+    fw, fdw = across(geo, 0), spread_rows(fd)
+
+    zd = product(st.wf_emb[...], *phid)
+    sc.zd[...] = zd
+    latent = st.z1[...] * zd
+    lat = keep_pair(sc.latd, (0,), latent)
+    pqd = product(st.wf_env[0], *lat)
+    base = product(st.wf_one[0], *lat)
+    ahead = product(st.wf_env[1], *lat)
+    sc.pqd[0] = pqd
 
     for k in range(LAYERS):
-        for c in range(CHUNKS):
-            cs = chunk(c)
-            sc.pqd[k, :, cs] = product(st.wf_env[k], *pair(sc.latd, cs, (k,)))
         for r in range(0, 32, 16):
             rs = slice(r, r + 16)
             sums = None
@@ -673,7 +759,7 @@
                 ts = tile(t)
                 p = st.pq[k, rs, ts]
                 a = p * geo[9, t : t + 1, :]
-                ad = sc.pqd[k, rs, ts] * geo[9, t : t + 1, :] + p * gd[9, t : t + 1, :]
+                ad = pqd[rs, ts] * geo[9, t : t + 1, :] + p * gd[9, t : t + 1, :]
                 terms = [ad] + [
                     ad * geo[m, t : t + 1, :] + a * gd[m, t : t + 1, :] for m in range(1, 9)
                 ]
@@ -684,17 +770,19 @@
             rs = slice(r, r + 8)
             envs = [[st.env[j, m, rs, :] for m in range(9)] for j in range(k + 1)]
             envds = [[sc.envd[j, m, rs, :] for m in range(9)] for j in range(k + 1)]
-            _, (base, factors) = jax.jvp(atom_terms, (envs,), (envds,))
+            _, (level, factors) = jax.jvp(atom_terms, (envs,), (envds,))
             for l in range(3):
-                sc.bd[k, l, rs, :] = base[l]
+                sc.bd[k, l, rs, :] = level[l]
             for m in range(8):
                 sc.ehd[k, m, rs, :] = factors[m]
+        high = [[None] * TILES for _ in range(6)]
+        low = [[None] * TILES for _ in range(6)]
         for r in range(0, 32, 16):
             rs = slice(r, r + 16)
             ru = slice(32 + r, 48 + r)
             for t in range(TILES):
                 ts = tile(t)
-                qd = sc.pqd[k, ru, ts]
+                qd = pqd[ru, ts]
                 if k > 0:
                     qd = mix * (
                         sc.qd[k - 1, rs, ts] * st.pq[k, ru, ts] + st.qq[k - 1, rs, ts] * qd
@@ -713,43 +801,112 @@
                 sc.vvd[k, rs, ts] = moves[1]
                 sc.vvd[k, ru, ts] = moves[2]
                 for l in range(3):
-                    put(sc.ivd, 32 * l + r, ts, qd * values[l] + q * moves[l], (k,))
-        for c in range(CHUNKS):
-            cs = chunk(c)
-            ind = sc.run[:, cs] + product(st.wf_inv[k], *pair(sc.ivd, cs, (k,)))
-            hd = product(st.wf_one[k], *put(sc.ind, 0, cs, ind, (k,)))
-            sc.hd[k, :, cs] = hd
-            od = product(st.wf_two[k], *put(sc.sd, 0, cs, st.s1[k, :, cs] * hd, (k,)))
-            ld = sc.run[:, cs] + wide(gd, 0, c) * st.oo[k, :, cs] + wide(geo, 0, c) * od
-            sc.run[:, cs] = ld
-            put(sc.latd, 0, cs, ld, (k + 1,))
-
-    per = CH // 128
-    vector = jnp.zeros((128, 128), f32)
-    for c in range(CHUNKS):
-        cs = chunk(c)
-        hhd = product(st.wf_head[...], *pair(sc.latd, cs, (3,)))
-        fw, fdw = wide(geo, 0, c), wide(gd, 0, c)
-        h1 = st.h1[:, cs]
-        whcol = jnp.concatenate([st.whcol[...]] * per, 1)
-        part = fw * h1 * hhd + fdw * st.sh[:, cs]
-        for j in range(per):
-            vector = vector + part[:, 128 * j : 128 * j + 128]
-        back = put(sc.hht, 0, cs, whcol * (fdw * h1 + fw * st.h2[:, cs] * hhd))
-        sc.run[:, cs] = product(st.wb_head[...], *back)
-    sc.grad[AT_HEAD : AT_HEAD + 64, :] = outer((sc.latd[3], st.hhb[...]), (st.latx[3], sc.hht[...]))
+                    n = 2 * l + r // 16
+                    high[n][t], low[n][t] = split(qd * values[l] + q * moves[l])
+        high, low = joined(high), joined(low)
+        sc.ivd[k, 0:96, :] = high
+        sc.ivd[k, 96:192, :] = low
+        hd = base + product(st.wf_io[k], high, low)
+        sc.hd[k] = hd
+        pair_s = keep_pair(sc.sd, (k,), st.s1[k] * hd)
+        if k < LAYERS - 1:
+            pqd = ahead + fdw * st.ts[k] + fw * product(st.wf_te[k], *pair_s)
+            sc.pqd[k + 1] = pqd
+        else:
+            hhd = ahead + fdw * st.th[...] + fw * product(st.wf_th[...], *pair_s)
+        od = product(st.wf_two[k], *pair_s)
+        latent = latent + fdw * st.oo[k] + fw * od
+        lat = keep_pair(sc.latd, (k + 1,), latent)
+        if k < LAYERS - 1:
+            base = product(st.wf_one[k + 1], *lat)
+            ahead = product(st.wf_env[k + 2] if k + 2 < LAYERS else st.wf_head[...], *lat)
+
+    whcol = jnp.concatenate([st.whcol[...]] * TILES, 1)
+    back = keep_pair(sc.hht, (), whcol * (fdw * st.h1[...] + fw * st.h2[...] * hhd))
+    xt = product(st.wb_th[...], *back)
+    lt = product(st.wb_head[...], *back)
+    part = fw * st.h1[...] * hhd + fdw * st.sh[...]
+    vector = part[:, tile(0)]
+    for t in range(1, TILES):
+        vector = vector + part[:, tile(t)]
     sc.grad[AT_VEC : AT_VEC + 1, :] = jnp.sum(vector.T, axis=0, keepdims=True)
 
+    queue = []
+    spare = [0]
+
+    def work(count):
+        for _ in range(min(count, len(queue))):
+            queue.pop(0)()
+
+    def single(rows, columns, first, second, finish):
+        def begin():
+            sc.part[0:rows, 0:columns] = cross(*first())
+
+        def end():
+            finish(settle(sc.part[0:rows, 0:columns] + cross(*second())))
+
+        queue.extend((begin, end))
+
+    def plain(at, count):
+        def finish(value):
+            sc.grad[at : at + count, :] = value
+
+        return finish
+
+    def packed(at, count):
+        def finish(value):
+            spare[0] = (spare[0] + 1) % 8
+            sc.grad[at : at + count, :] = pack(value, sc.tmp.at[spare[0]])[0:count]
+
+        return finish
+
+    def middle(k):
+        def finish(value):
+            moved = value[0:96]
+            high, low = split(moved)
+            at = AT_ONE + 64 * k
+            sc.grad[at : at + 64, :] = value[96:160] + product(st.wf_inv[k], high, low)
+            inv = cross(jnp.concatenate([high, low, high], 1), st.wb_one[k])
+            inv = jnp.concatenate([inv, jnp.zeros((96, 64), f32)], 1)
+            packed(AT_INV + 48 * k, 48)(inv)
+
+        return finish
+
+    def stack(lat, inv):
+        return jnp.concatenate([inv[0:96, :], lat[0:64, :], inv[96:192, :], lat[64:128, :]], 0)
+
+    single(
+        128,
+        256,
+        lambda: (sc.latd[3], st.hhb[...]),
+        lambda: (st.latx[3], sc.hht[...]),
+        plain(AT_HEAD, 64),
+    )
+
     for k in reversed(range(LAYERS)):
-        for c in range(CHUNKS):
-            cs = chunk(c)
-            lt = sc.run[:, cs]
-            ot = wide(gd, 0, c) * st.lb[k, :, cs] + wide(geo, 0, c) * lt
-            tt = product(st.wb_two[k], *put(sc.ot, 0, cs, ot))
-            ht = tt * st.s1[k, :, cs] + st.t2[k, :, cs] * sc.hd[k, :, cs]
-            it = product(st.wb_one[k], *put(sc.ht, 0, cs, ht))
-            sc.vt[:, cs] = product(st.wb_inv[k], *put(sc.it, 0, cs, it))
-            sc.run[:, cs] = lt + it
+        ht = (fdw * st.xb[k] + fw * xt) * st.s1[k] + st.t2[k] * sc.hd[k]
+        pair_h = keep_pair(sc.ht, (k,), ht)
+        vt = product(st.wb_io[k], *pair_h)
+        it = product(st.wb_one[k], *pair_h)
+        keep_pair(sc.ot, (k,), fdw * st.lb[k] + fw * lt)
+        run = lt + it
+        if k > 0:
+            ahead = product(st.wb_two[k - 1], *split(run))
+        work(2)
+        single(
+            320,
+            256,
+            lambda k=k: (stack(sc.latd[k], sc.ivd[k]), st.hb[k]),
+            lambda k=k: (stack(st.latx[k], st.ivx[k]), sc.ht[k]),
+            middle(k),
+        )
+        single(
+            256,
+            128,
+            lambda k=k: (sc.sd[k], st.ob[k]),
+            lambda k=k: (st.sx[k], sc.ot[k]),
+            packed(AT_TWO + 64 * k, 64),
+        )
         for r in range(0, 32, 16):
             rs = slice(r, r + 16)
             ru = slice(32 + r, 48 + r)
@@ -759,11 +916,11 @@
                 q, qd = st.qq[k, rs, ts], sc.qd[k, rs, ts]
                 ls = [slice(32 * l + r, 32 * l + r + 16) for l in range(3)]
                 vb = [st.vb[k, s, ts] for s in ls]
-                vt = [sc.vt[s, ts] for s in ls]
+                vs = [vt[s, ts] for s in ls]
                 qt = (
-                    vt[0] * st.bb[k, 0, rs, :]
-                    + vt[1] * st.vv[k, rs, ts]
-                    + vt[2] * st.vv[k, ru, ts]
+                    vs[0] * st.bb[k, 0, rs, :]
+                    + vs[1] * st.vv[k, rs, ts]
+                    + vs[2] * st.vv[k, ru, ts]
                     + vb[0] * sc.bd[k, 0, rs, :]
                     + vb[1] * sc.vvd[k, rs, ts]
                     + vb[2] * sc.vvd[k, ru, ts]
@@ -775,14 +932,15 @@
                     )
                 sc.qt[k, rs, ts] = qt
                 back = [x * q for x in vb]
-                turn = [x * q + y * qd for x, y in zip(vt, vb, strict=True)]
-                terms = list(turn)
+                twist = [x * q + y * qd for x, y in zip(vs, vb, strict=True)]
+                terms = list(twist)
                 for m in range(1, 9):
                     l = degree(m)
-                    terms.append(turn[l] * geo[m, t : t + 1, :] + back[l] * gd[m, t : t + 1, :])
+                    terms.append(twist[l] * geo[m, t : t + 1, :] + back[l] * gd[m, t : t + 1, :])
                 sums = terms if sums is None else [x + y for x, y in zip(sums, terms, strict=True)]
             for n in range(11):
                 sc.cott[n, rs, :] = group_sum(sums[n])
+        work(1)
         for r in range(0, 32, 8):
             rs = slice(r, r + 8)
             envs = [[st.env[j, m, rs, :] for m in range(9)] for j in range(k + 1)]
@@ -800,6 +958,9 @@
                         sc.et[j, m, rs, :] = back[j][m]
                     else:
                         sc.et[j, m, rs, :] += back[j][m]
+        work(1)
+        high = [[None] * TILES for _ in range(4)]
+        low = [[None] * TILES for _ in range(4)]
         for r in range(0, 32, 16):
             rs = slice(r, r + 16)
             for t in range(TILES):
@@ -811,28 +972,36 @@
                         + geo[m, t : t + 1, :] * sc.et[k, m, rs, :]
                         + gd[m, t : t + 1, :] * st.eb[k, m, rs, :]
                     )
-                pt = at * geo[9, t : t + 1, :] + st.ab[k, rs, ts] * gd[9, t : t + 1, :]
-                put(sc.pt, r, ts, pt)
                 qt = sc.qt[k, rs, ts]
                 if k > 0:
                     qt = mix * (sc.qd[k - 1, rs, ts] * st.qb[k, rs, ts] + st.qq[k - 1, rs, ts] * qt)
-                put(sc.pt, 32 + r, ts, qt)
-        for c in range(CHUNKS):
-            cs = chunk(c)
-            lt = sc.run[:, cs] + product(st.wb_env[k], *pair(sc.pt, cs))
-            sc.run[:, cs] = lt
-            if k == 0:
-                put(sc.zt, 0, cs, lt * st.z1[:, cs] + st.tz[:, cs] * sc.zd[:, cs])
-        at = AT_TWO + 64 * k
-        sc.grad[at : at + 64, :] = pack(outer((sc.sd[k], st.ob[k]), (st.sx[k], sc.ot[...])), sc.tmp)
-        at = AT_ONE + 64 * k
-        sc.grad[at : at + 64, :] = outer((sc.ind[k], st.hb[k]), (st.inx[k], sc.ht[...]))
-        at = AT_INV + 48 * k
-        sc.grad[at : at + 48, :] = pack(outer((sc.ivd[k], st.ib[k]), (st.ivx[k], sc.it[...])), sc.tmp)
-        at = AT_ENV + 32 * k
-        sc.grad[at : at + 32, :] = pack(outer((sc.latd[k], st.pb[k]), (st.latx[k], sc.pt[...])), sc.tmp)
-    packed = pack(outer((sc.phid[...], st.zb[...]), (st.phi[...], sc.zt[...])), sc.tmp)
-    sc.grad[0:9, :] = packed[0:9]
+                pt = at * geo[9, t : t + 1, :] + st.ab[k, rs, ts] * gd[9, t : t + 1, :]
+                high[r // 16][t], low[r // 16][t] = split(pt)
+                high[2 + r // 16][t], low[2 + r // 16][t] = split(qt)
+        high, low = joined(high), joined(low)
+        sc.pt[k, 0:64, :] = high
+        sc.pt[k, 64:128, :] = low
+        if k > 0:
+            xt = ahead + product(st.wb_te[k - 1], high, low)
+        lt = run + product(st.wb_env[k], high, low)
+        single(
+            128,
+            128,
+            lambda k=k: (sc.latd[k], st.pb[k]),
+            lambda k=k: (st.latx[k], sc.pt[k]),
+            packed(AT_ENV + 32 * k, 32),
+        )
+        work(2)
+
+    keep_pair(sc.zt, (), lt * st.z1[...] + st.tz[...] * sc.zd[...])
+    single(
+        2 * FEAT,
+        128,
+        lambda: (sc.phid[...], st.zb[...]),
+        lambda: (st.phi[...], sc.zt[...]),
+        packed(AT_EMBED, 9),
+    )
+    work(len(queue))
     sc.grad[ROWS:PADDED, :] = jnp.zeros((PADDED - ROWS, 128), f32)
     lane = lanes((1, 128))
     amount = 3.0 * live[0, 0].astype(f32)
@@ -879,6 +1048,7 @@
 
 
 VMEM = pl.BlockSpec(memory_space=pltpu.VMEM)
+HBM = pl.BlockSpec(memory_space=pltpu.HBM)
 SMEM = pl.BlockSpec(memory_space=pltpu.SMEM)
 
 
@@ -888,7 +1058,6 @@
 
 def local(
     ranks,
-    wide_axes,
     params,
     first_moment,
     second_moment,
@@ -906,35 +1075,35 @@
     par = params.reshape(flat)
     live = live_atoms.reshape(1, 1)
     tall = 3 * ranks + 8
-    parts = len(wide_axes[1])
     state = [shape(s, t) for _, s, t in STATE]
+    sources = (
+        edge_vectors.reshape(3, 8, 128),
+        owner_rank.reshape(8, 128),
+        neighbour_local.reshape(8, 128),
+        neighbour_species.reshape(8, 128),
+        centre_species.reshape(1, ATOMS),
+        target_forces.reshape(3, 1, ATOMS),
+        par,
+    )
     pay, *kept = pl.pallas_call(
         functools.partial(first_kernel, ranks, "atoms"),
         out_shape=[shape((ranks, tall, 128), f32), *state],
-        in_specs=[VMEM] * 6 + [SMEM, VMEM],
+        in_specs=[SMEM] + [HBM] * 7,
         out_specs=[VMEM] * (1 + len(state)),
         scratch_shapes=[
-            pltpu.VMEM((16, 192), bf16),
+            *[pltpu.VMEM(x.shape, x.dtype) for x in sources],
+            pltpu.SemaphoreType.DMA((7,)),
             pltpu.VMEM((tall, 128), f32),
             pltpu.VMEM((6 * ranks, EDGES), bf16),
             *scratch(SCRATCH_A),
         ],
         compiler_params=pltpu.CompilerParams(vmem_limit_bytes=16 * 2**20),
         name="forward",
-    )(
-        par,
-        edge_vectors.reshape(3, 8, 128),
-        owner_rank.reshape(8, 128),
-        neighbour_local.reshape(8, 128),
-        neighbour_species.reshape(8, 128),
-        centre_species.reshape(1, ATOMS),
-        live,
-        target_forces.reshape(3, ATOMS),
-    )
+    )(live, *sources)
     got = lax.all_to_all(pay, "atoms", split_axis=0, concat_axis=0, tiled=True)
     keep, give, forces = pl.pallas_call(
         functools.partial(second_kernel, ranks, "atoms", "low"),
-        out_shape=[shape((HALF, 128), f32), shape((HALF, 128), f32), shape((3, ATOMS), f32)],
+        out_shape=[shape((HALF, 128), f32), shape((HALF, 128), f32), shape((3, 1, ATOMS), f32)],
         in_specs=[SMEM, VMEM] + [VMEM] * len(state),
         out_specs=[VMEM] * 3,
         scratch_shapes=[
@@ -975,7 +1144,7 @@
         loss.reshape(()),
         count.reshape(()),
         norm.reshape(()),
-        forces.reshape(3, 1, ATOMS),
+        forces,
         new_first.reshape(-1),
         new_second.reshape(-1),
         new_params.reshape(-1),
@@ -1003,7 +1172,7 @@
     )
     out_specs = (P(), P(), P(), P(None, grp, "atoms"), P(), P(), P(), P(), P())
     return jax.shard_map(
-        functools.partial(local, ranks, (("atoms", "high"), grp)),
+        functools.partial(local, ranks),
         mesh=fine,
         in_specs=in_specs,
         out_specs=out_specs,

time: 77.3 us -> 70.1 us (0.907)
  Pallas kernels: 29.6 us -> 22.4 us
    pallas_call x1, Pallas kernels: 15.6 us -> 11.7 us  [local(): pl.pallas_call(functools.partial(second_kernel, ranks, 'atoms', 'low'), o...]
    pallas_call x1, Pallas kernels: 12.3 us -> 8.95 us  [local(): pl.pallas_call(functools.partial(first_kernel, ranks, 'atoms'), out_shape...]
  transfers between devices with their start and end apart: 2 -> 2, of which waited for: 2 -> 2; matrix products, arithmetic and copies ran while one was open for 1% -> 0% of each run, Pallas kernels for 0% -> 0%
where the time goes in v1:
time: 70.1 us; the launch traced here: 69.7 us
  blocking collectives  37.8 us (54%)
  Pallas kernels  22.4 us (32%)
  local copies, waits for them, and re-layouts  5.11 us (7%)
  waiting for transfers between devices  2.87 us (4%)
  between operations  1.36 us (2%)
    all_to_all x1, blocking collectives, local(): got = lax.all_to_all(pay, 'atoms', split_axis=0, concat_axis=0, tiled=True)  14.4 us
    all_to_all x1, blocking collectives, local(): lax.all_to_all(held, axes, split_axis=0, concat_axis=0, tiled=True).sum(0)  12.1 us
    pallas_call x1, Pallas kernels, local(): pl.pallas_call(functools.partial(second_kernel, ranks, 'atoms', 'low'), o...  11.7 us
    all_to_all x1, blocking collectives, local(): mine = lax.all_to_all(summed, axes, split_axis=0, concat_axis=0, tiled=True)  11.3 us
    pallas_call x1, Pallas kernels, local(): pl.pallas_call(functools.partial(first_kernel, ranks, 'atoms'), out_shape...  8.95 us
    unnamed x22, local copies, waits for them, and re-layouts  5.09 us
    pallas_call x1, Pallas kernels, local(): pl.pallas_call(functools.partial(third_kernel, 'low'), out_shape=[one, on...  1.7 us
    ppermute x1, waiting for transfers between devices, local(): other = lax.ppermute(mine, 'low', swap)  1.44 us
  transfers between devices with their start and end apart: 2, of which 2 were waited for; matrix products, arithmetic and copies ran while one was open for 0% of the time, Pallas kernels for 0%

profile of v1, /device:TPU:0, one launch (start us, length us, event | category | flops | bytes accessed | tf_op | source)
XLA Modules:
  0.0 69.7 jit_solution(18344392051204707337)
XLA Ops:
  1.3 0.0 copy-start
  1.3 1.0 %copy-done = f32[89344]{0:T(1024)S(1)} copy-done((f32[89344]{0:T(1024)S(1)}, f32[89344]{0:T(1024)}, u32[]{:S(2)}) %copy-start) | copy-done | bytes 357400
  2.3 0.0 copy-start.5
  2.3 0.7 %copy-done.5 = f32[3,1,1024]{2,1,0:T(1,128)S(1)} copy-done((f32[3,1,1024]{2,1,0:T(1,128)S(1)}, f32[3,1,1024]{2,1,0:T(1,128)}, u32[]{:S(2)}) %copy-start.5) | copy-done | bytes 12312
  3.0 0.0 copy-start.6
  3.0 0.7 copy-done.6
  3.7 0.0 copy-start.7
  3.7 0.7 copy-done.7
  4.4 0.0 copy-start.8
  4.4 0.7 copy-done.8
  5.0 0.0 copy-start.9
  5.0 0.7 copy-done.9
  5.7 0.0 copy-start.10
  5.7 0.7 copy-done.10
  6.4 9.0 %forward.1 = (f32[8,32,128]{2,1,0:T(8,128)S(1)}, bf16[64,96]{1,0:T(8,128)(2,1)S(1)}, bf16[3,64,192]{2,1,0:T(8,128)(2,1)S(1)}, bf16[3,64,192]{2,1,0:T(8,128)(2,1)...) custom-call(s32[1,1]{1,0:T(1,128)S(6)} %copy.20.live, ...), custom_call_target="tpu_custom_call" | custom-call | tf_op jit(solution)/shard_map/forward/pallas_call | solution.py:1088
  15.3 14.4 %all_to_all.15.got = f32[8,32,128]{2,1,0:T(8,128)S(1)} all-to-all(f32[8,32,128]{2,1,0:T(8,128)S(1)} %get-tuple-element.75), channel_id=1, replica_groups=mesh['atoms'=8,'high'=2,'low'=2] {'atoms'}, dimensions={0} | all-to-all | bytes 262144 | tf_op jit(solution)/shard_map/all_to_all | solution.py:1103
  29.8 11.7 %gradient.1 = (f32[384,128]{1,0:T(8,128)S(1)}, f32[384,128]{1,0:T(8,128)S(1)}, f32[3,1,32]{2,1,0:T(1,128)}) custom-call(s32[1,1]{1,0:T(1,128)S(6)} %copy.20.live, f32[8,32,128]{2,1,0:T(8,128)S(1)} %all_to_all.15.got, bf16[64,96]{1,0:T(8,128)(2,1)S(1)} %get-tuple-element.76.refs_0_, bf16[3,64,192]{2,1,0:T(8,128)(2,1)S(1)} %get-tuple-element.77.refs_1_, ...), custom_call_target="tpu_custom_call" | custom-call | tf_op jit(solution)/shard_map/gradient/pallas_call | solution.py:1104
  41.5 0.0 copy-start.1
  41.5 0.0 copy-start.2
  41.5 0.0 copy-start.3
  41.5 0.0 copy-start.4
  41.5 0.1 collective-permute-start
  41.6 1.4 %collective-permute-done = f32[384,128]{1,0:T(8,128)S(1)} collective-permute-done((f32[384,128]{1,0:T(8,128)S(1)}, f32[384,128]{1,0:T(8,128)S(1)}, u32[]{:S(2)}, u32[]{:S(2)}) %collective-permute-start) | collective-permute-done | bytes 196640 | tf_op jit(solution)/shard_map/ppermute | solution.py:1119
  43.1 12.1 %all_to_all.16 = f32[16,24,128]{2,1,0:T(8,128)S(1)} all-to-all(f32[16,24,128]{2,1,0:T(8,128)S(1)} %bitcast.29), channel_id=1, replica_groups=mesh['atoms'=8,'high'=2,'low'=2] {'atoms','high'}, dimensions={0} | all-to-all | bytes 393216 | tf_op jit(solution)/shard_map/all_to_all | solution.py:1122
  55.2 11.3 %all_to_all.17 = f32[16,24,128]{2,1,0:T(8,128)S(1)} all-to-all(f32[16,24,128]{2,1,0:T(8,128)S(1)} %broadcast_in_dim.2), channel_id=1, replica_groups=mesh['atoms'=8,'high'=2,'low'=2] {'atoms','high'}, dimensions={0} | all-to-all | bytes 393216 | tf_op jit(solution)/shard_map/all_to_all | solution.py:1124
  66.5 0.0 collective-permute-start.1
  66.5 1.4 %collective-permute-done.1.other = f32[384,128]{1,0:T(8,128)S(1)} collective-permute-done((f32[384,128]{1,0:T(8,128)S(1)}, f32[384,128]{1,0:T(8,128)S(1)}, u32[]{:S(2)}, u32[]{:S(2)}) %collective-permute-start.1) | collective-permute-done | bytes 196640 | tf_op jit(solution)/shard_map/ppermute | solution.py:1126
  68.0 0.0 copy-done.1
  68.0 0.0 copy-done.2
  68.0 0.0 copy-done.3
  68.0 0.0 copy-done.4
  68.0 1.7 %update.1 = (f32[1,1]{1,0:T(1,128)}, f32[1,1]{1,0:T(1,128)}, f32[1,1]{1,0:T(1,128)}, f32[698,128]{1,0:T(8,128)}, f32[698,128]{1,0:T(8,128)}, /*index=5*/f32[698,...) custom-call(f32[384,128]{1,0:T(8,128)S(1)} %bitcast.21, f32[384,128]{1,0:T(8,128)S(1)} %collective-permute-done.1.other, ...), custom_call_target="tpu_custom_call" | custom-call | tf_op jit(solution)/shard_map/update/pallas_call | solution.py:1128
  (3 shorter events, 0.1 us)
Async XLA Ops:
  1.3 1.0 %copy-start = (f32[89344]{0:T(1024)S(1)}, f32[89344]{0:T(1024)}, u32[]{:S(2)}) copy-start(f32[89344]{0:T(1024)} %param.11) | copy-start | bytes 1072132
  2.3 0.7 %copy-start.5 = (f32[3,1,1024]{2,1,0:T(1,128)S(1)}, f32[3,1,1024]{2,1,0:T(1,128)}, u32[]{:S(2)}) copy-start(f32[3,1,1024]{2,1,0:T(1,128)} %param.15) | copy-start | bytes 36868
  3.0 0.7 copy-start.6
  3.7 0.7 copy-start.7
  4.4 0.7 copy-start.8
  5.0 0.7 copy-start.9
  5.7 0.7 copy-start.10
  41.5 26.4 %copy-start.1 = (f32[89344]{0:T(1024)S(1)}, f32[89344]{0:T(1024)}, u32[]{:S(2)}) copy-start(f32[89344]{0:T(1024)} %param.11) | copy-start | bytes 1072132
  41.5 26.4 %copy-start.2 = (f32[89344]{0:T(1024)S(1)}, f32[89344]{0:T(1024)}, u32[]{:S(2)}) copy-start(f32[89344]{0:T(1024)} %param.12) | copy-start | bytes 1072132
  41.5 26.4 %copy-start.3 = (f32[89344]{0:T(1024)S(1)}, f32[89344]{0:T(1024)}, u32[]{:S(2)}) copy-start(f32[89344]{0:T(1024)} %param.13) | copy-start | bytes 1072132
  41.5 26.4 %copy-start.4 = (f32[89344]{0:T(1024)S(1)}, f32[89344]{0:T(1024)}, u32[]{:S(2)}) copy-start(f32[89344]{0:T(1024)} %param.14) | copy-start | bytes 1072132
  41.5 1.5 %collective-permute-start = (f32[384,128]{1,0:T(8,128)S(1)}, f32[384,128]{1,0:T(8,128)S(1)}, u32[]{:S(2)}, u32[]{:S(2)}) collective-permute-start(f32[384,128]{1,0:T(8,128)S(1)} %get-tuple-element.131), channel_id=1, source_target_pairs={{0,1},{1,0},{2,3},{3,2},{4,5},{5,4},{6,7},{7,6},{8,9},{9,8},{10,11... | collective-permute-start | bytes 589832 | tf_op jit(solution)/shard_map/ppermute | solution.py:1119
  66.5 1.4 %collective-permute-start.1 = (f32[384,128]{1,0:T(8,128)S(1)}, f32[384,128]{1,0:T(8,128)S(1)}, u32[]{:S(2)}, u32[]{:S(2)}) collective-permute-start(f32[384,128]{1,0:T(8,128)S(1)} %bitcast.20), channel_id=1, source_target_pairs={{0,1},{1,0},{2,3},{3,2},{4,5},{5,4},{6,7},{7,6},{8,9},{9,8},{10,11... | collective-permute-start | bytes 589832 | tf_op jit(solution)/shard_map/ppermute | solution.py:1126

commit v2 on v1

--- a/solution.py
+++ b/solution.py
@@ -50,21 +50,15 @@
 
 STATE = [
     ("wf_emb", (LATENT, 3 * FEAT), bf16),
-    ("wf_env", (3, 64, 192), bf16),
-    ("wb_env", (3, 64, 192), bf16),
+    ("wf_first", (64, 192), bf16),
+    ("wf_lat", (3, 256, 192), bf16),
+    ("wf_io", (3, 128, 288), bf16),
+    ("wf_s", (3, 192, 384), bf16),
     ("wf_inv", (3, 64, 288), bf16),
-    ("wf_one", (3, 128, 192), bf16),
-    ("wb_one", (3, 64, 384), bf16),
-    ("wf_io", (3, 128, 288), bf16),
-    ("wb_io", (3, 96, 384), bf16),
-    ("wf_two", (3, 64, 384), bf16),
+    ("wb_hh", (192, 384), bf16),
+    ("wb_h", (3, 160, 384), bf16),
+    ("wb_p", (3, 192, 192), bf16),
     ("wb_two", (3, 128, 192), bf16),
-    ("wf_te", (2, 64, 384), bf16),
-    ("wb_te", (2, 128, 192), bf16),
-    ("wf_th", (128, 384), bf16),
-    ("wb_th", (128, 384), bf16),
-    ("wf_head", (128, 192), bf16),
-    ("wb_head", (64, 384), bf16),
     ("whcol", (128, 128), f32),
     ("place", (3, 8, 128), f32),
     ("owner", (8, 128), jnp.int32),
@@ -115,6 +109,7 @@
 SCRATCH_B = [
     ("tmp", (8, 128, 128), f32),
     ("part", (320, 256), f32),
+    ("mid", (3, 160, 128), f32),
     ("cdir", (3, 8, 128), f32),
     ("gd", (10, 8, 128), f32),
     ("phid", (2 * FEAT, EDGES), bf16),
@@ -270,17 +265,19 @@
     return jnp.where(lanes(value.shape) < 64, value, spin(value, 64))
 
 
-def store_64(ref, lead, doubled):
+def store_64(ref, lead, doubled, at=0):
     high, low = split(doubled)
-    ref[(*lead, slice(None), slice(0, 128))] = high
-    ref[(*lead, slice(None), slice(128, 192))] = low[:, 0:64]
-
-
-def store_128(ref, lead, value):
+    rows = slice(at, at + doubled.shape[0])
+    ref[(*lead, rows, slice(0, 128))] = high
+    ref[(*lead, rows, slice(128, 192))] = low[:, 0:64]
+
+
+def store_128(ref, lead, value, at=0):
     high, low = split(value)
-    ref[(*lead, slice(None), slice(0, 128))] = high
-    ref[(*lead, slice(None), slice(128, 256))] = high
-    ref[(*lead, slice(None), slice(256, 384))] = low
+    rows = slice(at, at + value.shape[0])
+    ref[(*lead, rows, slice(0, 128))] = high
+    ref[(*lead, rows, slice(128, 256))] = high
+    ref[(*lead, rows, slice(256, 384))] = low
 
 
 def store_96(ref, lead, value):
@@ -348,39 +345,42 @@
     low = w - high
     turn = jnp.concatenate([high, high, low, jnp.zeros((32, 128), f32)], 0).T[0:64]
     st.wf_emb[...] = turn[:, 0 : 3 * FEAT].astype(bf16)
-    envs, ones = [], []
+    envs = []
     for k in range(LAYERS):
         w = doubled(AT_ENV + 32 * k, 64)
         envs.append(w)
-        store_64(st.wb_env, (k,), w)
-        store_64(st.wf_env, (k,), jnp.concatenate([w, w], 0).T[0:64])
+        store_64(st.wb_p, (k,), w)
+        turn = jnp.concatenate([w, w], 0).T[0:64]
+        if k == 0:
+            store_64(st.wf_first, (), turn)
+        else:
+            store_64(st.wf_lat, (k - 1,), turn, 128)
     head = par[AT_HEAD : AT_HEAD + 64, :]
+    store_128(st.wb_hh, (), head, 128)
+    store_64(st.wf_lat, (2,), jnp.concatenate([head, head], 0).T, 128)
     for k in range(LAYERS):
         one = par[AT_ONE + 64 * k : AT_ONE + 64 * k + 64, :]
-        store_128(st.wb_one, (k,), one)
-        store_64(st.wf_one, (k,), jnp.concatenate([one, one], 0).T)
+        store_128(st.wb_h, (k,), one, 96)
+        store_64(st.wf_lat, (k,), jnp.concatenate([one, one], 0).T)
         w = doubled(AT_INV + 48 * k, 96)
         store_96(st.wf_inv, (k,), jnp.concatenate([w, jnp.zeros((32, 128), f32)], 0).T[0:64])
         high, low = split(w)
-        left = jnp.concatenate([high, low[:, 0:64]], 1)
-        w = weights_product(left, one)
-        store_128(st.wb_io, (k,), w)
+        w = weights_product(jnp.concatenate([high, low[:, 0:64]], 1), one)
+        store_128(st.wb_h, (k,), w)
         store_96(st.wf_io, (k,), jnp.concatenate([w, jnp.zeros((32, 128), f32)], 0).T)
         w = doubled(AT_TWO + 64 * k, 128)
         high, low = split(w)
         left = jnp.concatenate([high, low[:, 0:64]], 1)
         st.wb_two[k] = left
-        store_128(st.wf_two, (k,), w.T[0:64])
+        store_128(st.wf_s, (k,), w.T[0:64])
         if k < LAYERS - 1:
             w = weights_product(left, envs[k + 1])
-            store_64(st.wb_te, (k,), w)
-            store_128(st.wf_te, (k,), w.T[0:64])
+            store_64(st.wb_p, (k + 1,), w, 64)
+            store_128(st.wf_s, (k,), w.T[0:64], 64)
         else:
             w = weights_product(left, head)
-            store_128(st.wb_th, (), w)
-            store_128(st.wf_th, (), w.T)
-    store_128(st.wb_head, (), head)
-    store_64(st.wf_head, (), jnp.concatenate([head, head], 0).T)
+            store_128(st.wb_hh, (), w)
+            store_128(st.wf_s, (k,), w.T, 64)
     st.whcol[...] = jnp.broadcast_to(par[AT_VEC : AT_VEC + 1, :], (128, 128)).T
 
 
@@ -414,7 +414,7 @@
     ]
     for copy in copies:
         copy.start()
-    for copy in copies:
+    for copy in copies[:-1]:
         copy.wait()
 
     order = sc.tmp.at[10]
@@ -467,6 +467,7 @@
         st.hot[:, tile(t)] = (rows_of((ATOMS, 128)) == local[t : t + 1]).astype(f32).astype(bf16)
     phi = keep_pair(st.phi, (), jnp.concatenate(tiles, 1))
 
+    copies[-1].wait()
     prepare(par, st, sc)
     fw = spread_rows(f)
 
@@ -475,10 +476,10 @@
     st.tz[...] = s2
     latent = s
     lat = keep_pair(st.latx, (0,), s)
-    pq = product(st.wf_env[0], *lat)
-    base = product(st.wf_one[0], *lat)
-    ahead = product(st.wf_env[1], *lat)
+    pq = product(st.wf_first[...], *lat)
     st.pq[0] = pq
+    both_of = product(st.wf_lat[0, 0:192, :], *lat)
+    base, ahead = both_of[0:128], both_of[128:192]
 
     for k in range(LAYERS):
         for r in range(0, 32, 16):
@@ -525,22 +526,22 @@
         st.s1[k] = s1
         st.t2[k] = s2
         pair_s = keep_pair(st.sx, (k,), s)
-        if k < LAYERS - 1:
-            step = product(st.wf_te[k], *pair_s)
+        last = k == LAYERS - 1
+        both_of = product(st.wf_s[k] if last else st.wf_s[k, 0:128, :], *pair_s)
+        o, step = both_of[0:64], both_of[64:]
+        if last:
+            st.th[...] = step
+            hh = ahead + fw * step
+        else:
             st.ts[k] = step
             pq = ahead + fw * step
             st.pq[k + 1] = pq
-        else:
-            step = product(st.wf_th[...], *pair_s)
-            st.th[...] = step
-            hh = ahead + fw * step
-        o = product(st.wf_two[k], *pair_s)
         st.oo[k] = o
         latent = latent + fw * o
         lat = keep_pair(st.latx, (k + 1,), latent)
-        if k < LAYERS - 1:
-            base = product(st.wf_one[k + 1], *lat)
-            ahead = product(st.wf_env[k + 2] if k + 2 < LAYERS else st.wf_head[...], *lat)
+        if not last:
+            both_of = product(st.wf_lat[k + 1] if k + 2 == LAYERS else st.wf_lat[k + 1, 0:192, :], *lat)
+            base, ahead = both_of[0:128], both_of[128:]
 
     s, s1, s2 = silu_parts(hh)
     st.sh[...] = s
@@ -550,16 +551,16 @@
     back = keep_pair(st.hhb, (), fw * whcol * s1)
     for t, share in enumerate(shares(whcol * s)):
         sc.ybar[0, t] = share
-    xb = product(st.wb_th[...], *back)
-    lb = product(st.wb_head[...], *back)
+    both_of = product(st.wb_hh[...], *back)
+    xb, lb = both_of[0:128], both_of[128:192]
 
     for k in reversed(range(LAYERS)):
         st.xb[k] = xb
         sb = fw * xb
         pair_h = keep_pair(st.hb, (k,), st.s1[k] * sb)
         st.t2[k] = st.t2[k] * sb
-        vb = product(st.wb_io[k], *pair_h)
-        ib = product(st.wb_one[k], *pair_h)
+        both_of = product(st.wb_h[k], *pair_h)
+        vb, ib = both_of[0:96], both_of[96:160]
         st.vb[k] = vb
         st.lb[k] = lb
         keep_pair(st.ob, (k,), fw * lb)
@@ -630,9 +631,10 @@
         high, low = joined(high), joined(low)
         st.pb[k, 0:64, :] = high
         st.pb[k, 64:128, :] = low
+        both_of = product(st.wb_p[k] if k > 0 else st.wb_p[k, 0:64, :], high, low)
+        lb = run + both_of[0:64]
         if k > 0:
-            xb = ahead + product(st.wb_te[k - 1], high, low)
-        lb = run + product(st.wb_env[k], high, low)
+            xb = ahead + both_of[64:192]
 
     st.tz[...] = st.tz[...] * lb
     pb = product(sc.wb_emb[...], *keep_pair(st.zb, (), st.z1[...] * lb))[0:8]
@@ -746,10 +748,10 @@
     sc.zd[...] = zd
     latent = st.z1[...] * zd
     lat = keep_pair(sc.latd, (0,), latent)
-    pqd = product(st.wf_env[0], *lat)
-    base = product(st.wf_one[0], *lat)
-    ahead = product(st.wf_env[1], *lat)
+    pqd = product(st.wf_first[...], *lat)
     sc.pqd[0] = pqd
+    both_of = product(st.wf_lat[0, 0:192, :], *lat)
+    base, ahead = both_of[0:128], both_of[128:192]
 
     for k in range(LAYERS):
         for r in range(0, 32, 16):
@@ -809,22 +811,24 @@
         hd = base + product(st.wf_io[k], high, low)
         sc.hd[k] = hd
         pair_s = keep_pair(sc.sd, (k,), st.s1[k] * hd)
-        if k < LAYERS - 1:
-            pqd = ahead + fdw * st.ts[k] + fw * product(st.wf_te[k], *pair_s)
+        last = k == LAYERS - 1
+        both_of = product(st.wf_s[k] if last else st.wf_s[k, 0:128, :], *pair_s)
+        od, step = both_of[0:64], both_of[64:]
+        if last:
+            hhd = ahead + fdw * st.th[...] + fw * step
+        else:
+            pqd = ahead + fdw * st.ts[k] + fw * step
             sc.pqd[k + 1] = pqd
-        else:
-            hhd = ahead + fdw * st.th[...] + fw * product(st.wf_th[...], *pair_s)
-        od = product(st.wf_two[k], *pair_s)
         latent = latent + fdw * st.oo[k] + fw * od
         lat = keep_pair(sc.latd, (k + 1,), latent)
-        if k < LAYERS - 1:
-            base = product(st.wf_one[k + 1], *lat)
-            ahead = product(st.wf_env[k + 2] if k + 2 < LAYERS else st.wf_head[...], *lat)
+        if not last:
+            both_of = product(st.wf_lat[k + 1] if k + 2 == LAYERS else st.wf_lat[k + 1, 0:192, :], *lat)
+            base, ahead = both_of[0:128], both_of[128:]
 
     whcol = jnp.concatenate([st.whcol[...]] * TILES, 1)
     back = keep_pair(sc.hht, (), whcol * (fdw * st.h1[...] + fw * st.h2[...] * hhd))
-    xt = product(st.wb_th[...], *back)
-    lt = product(st.wb_head[...], *back)
+    both_of = product(st.wb_hh[...], *back)
+    xt, lt = both_of[0:128], both_of[128:192]
     part = fw * st.h1[...] * hhd + fdw * st.sh[...]
     vector = part[:, tile(0)]
     for t in range(1, TILES):
@@ -862,15 +866,21 @@
 
     def middle(k):
         def finish(value):
-            moved = value[0:96]
-            high, low = split(moved)
+            sc.mid[k] = value
+
+        return finish
+
+    def split_middle():
+        parts = [split(sc.mid[k, 0:96, :]) for k in range(LAYERS)]
+        ones = [product(st.wf_inv[k], *parts[k]) for k in range(LAYERS)]
+        invs = []
+        for k, (high, low) in enumerate(parts):
+            inv = cross(jnp.concatenate([high, low, high], 1), st.wb_h[k, 96:160, :])
+            invs.append(jnp.concatenate([inv, jnp.zeros((96, 64), f32)], 1))
+        for k in range(LAYERS):
             at = AT_ONE + 64 * k
-            sc.grad[at : at + 64, :] = value[96:160] + product(st.wf_inv[k], high, low)
-            inv = cross(jnp.concatenate([high, low, high], 1), st.wb_one[k])
-            inv = jnp.concatenate([inv, jnp.zeros((96, 64), f32)], 1)
-            packed(AT_INV + 48 * k, 48)(inv)
-
-        return finish
+            sc.grad[at : at + 64, :] = sc.mid[k, 96:160, :] + ones[k]
+            packed(AT_INV + 48 * k, 48)(invs[k])
 
     def stack(lat, inv):
         return jnp.concatenate([inv[0:96, :], lat[0:64, :], inv[96:192, :], lat[64:128, :]], 0)
@@ -886,8 +896,8 @@
     for k in reversed(range(LAYERS)):
         ht = (fdw * st.xb[k] + fw * xt) * st.s1[k] + st.t2[k] * sc.hd[k]
         pair_h = keep_pair(sc.ht, (k,), ht)
-        vt = product(st.wb_io[k], *pair_h)
-        it = product(st.wb_one[k], *pair_h)
+        both_of = product(st.wb_h[k], *pair_h)
+        vt, it = both_of[0:96], both_of[96:160]
         keep_pair(sc.ot, (k,), fdw * st.lb[k] + fw * lt)
         run = lt + it
         if k > 0:
@@ -981,9 +991,10 @@
         high, low = joined(high), joined(low)
         sc.pt[k, 0:64, :] = high
         sc.pt[k, 64:128, :] = low
+        both_of = product(st.wb_p[k] if k > 0 else st.wb_p[k, 0:64, :], high, low)
+        lt = run + both_of[0:64]
         if k > 0:
-            xt = ahead + product(st.wb_te[k - 1], high, low)
-        lt = run + product(st.wb_env[k], high, low)
+            xt = ahead + both_of[64:192]
         single(
             128,
             128,
@@ -1002,6 +1013,7 @@
         packed(AT_EMBED, 9),
     )
     work(len(queue))
+    split_middle()
     sc.grad[ROWS:PADDED, :] = jnp.zeros((PADDED - ROWS, 128), f32)
     lane = lanes((1, 128))
     amount = 3.0 * live[0, 0].astype(f32)
@@ -1099,7 +1111,7 @@
         ],
         compiler_params=pltpu.CompilerParams(vmem_limit_bytes=16 * 2**20),
         name="forward",
-    )(live, *sources)
+    )(live, *[pltpu.with_memory_space_constraint(x, pltpu.HBM) for x in sources])
     got = lax.all_to_all(pay, "atoms", split_axis=0, concat_axis=0, tiled=True)
     keep, give, forces = pl.pallas_call(
         functools.partial(second_kernel, ranks, "atoms", "low"),

time: 70.1 us -> 63.7 us (0.909)
  local copies, waits for them, and re-layouts: 5.11 us -> 0.03 us
  Pallas kernels: 22.4 us -> 21.2 us
    unnamed x22 -> x8, local copies, waits for them, and re-layouts: 5.09 us -> 0.01 us
    pallas_call x1, Pallas kernels: 11.7 us -> 9.99 us  [local(): pl.pallas_call(functools.partial(second_kernel, ranks, 'atoms', 'low'), o...]
where the time goes in v2:
time: 63.7 us; the launch traced here: 63.4 us
  blocking collectives  37.8 us (59%)
  Pallas kernels  21.2 us (33%)
  waiting for transfers between devices  2.87 us (5%)
  between operations  1.34 us (2%)
    all_to_all x1, blocking collectives, local(): got = lax.all_to_all(pay, 'atoms', split_axis=0, concat_axis=0, tiled=True)  14.4 us
    all_to_all x1, blocking collectives, local(): lax.all_to_all(held, axes, split_axis=0, concat_axis=0, tiled=True).sum(0)  12.1 us
    all_to_all x1, blocking collectives, local(): mine = lax.all_to_all(summed, axes, split_axis=0, concat_axis=0, tiled=True)  11.3 us
    pallas_call x1, Pallas kernels, local(): pl.pallas_call(functools.partial(second_kernel, ranks, 'atoms', 'low'), o...  9.99 us
    pallas_call x1, Pallas kernels, local(): pl.pallas_call(functools.partial(first_kernel, ranks, 'atoms'), out_shape...  9.54 us
    pallas_call x1, Pallas kernels, local(): pl.pallas_call(functools.partial(third_kernel, 'low'), out_shape=[one, on...  1.7 us
    ppermute x1, waiting for transfers between devices, local(): other = lax.ppermute(mine, 'low', swap)  1.44 us
    ppermute x1, waiting for transfers between devices, local(): held = keep + lax.ppermute(give, 'low', swap)  1.43 us
  transfers between devices with their start and end apart: 2, of which 2 were waited for; matrix products, arithmetic and copies ran while one was open for 0% of the time, Pallas kernels for 0%

profile of v2, /device:TPU:0, one launch (start us, length us, event | category | flops | bytes accessed | tf_op | source)
XLA Modules:
  0.0 63.4 jit_solution(18228672974933867786)
XLA Ops:
  1.3 9.5 %forward.1 = (f32[8,32,128]{2,1,0:T(8,128)S(1)}, bf16[64,96]{1,0:T(8,128)(2,1)S(1)}, bf16[64,192]{1,0:T(8,128)(2,1)S(1)}, bf16[3,256,192]{2,1,0:T(8,128)(2,1)S(1...) custom-call(s32[1,1]{1,0:T(1,128)S(6)} %copy.20.live, ...), custom_call_target="tpu_custom_call" | custom-call | tf_op jit(solution)/shard_map/forward/pallas_call | solution.py:1100
  10.8 14.4 %all_to_all.15.got = f32[8,32,128]{2,1,0:T(8,128)S(1)} all-to-all(f32[8,32,128]{2,1,0:T(8,128)S(1)} %get-tuple-element.69), channel_id=1, replica_groups=mesh['atoms'=8,'high'=2,'low'=2] {'atoms'}, dimensions={0} | all-to-all | bytes 262144 | tf_op jit(solution)/shard_map/all_to_all | solution.py:1115
  25.3 10.0 %gradient.1 = (f32[384,128]{1,0:T(8,128)S(1)}, f32[384,128]{1,0:T(8,128)S(1)}, f32[3,1,32]{2,1,0:T(1,128)}) custom-call(s32[1,1]{1,0:T(1,128)S(6)} %copy.20.live, f32[8,32,128]{2,1,0:T(8,128)S(1)} %all_to_all.15.got, bf16[64,96]{1,0:T(8,128)(2,1)S(1)} %get-tuple-element.70.refs_0_, bf16[64,192]{1,0:T(8,128)(2,1)S(1)} %get-tuple-element.71.refs_1_, ...), custom_call_target="tpu_custom_call" | custom-call | tf_op jit(solution)/shard_map/gradient/pallas_call | solution.py:1116
  35.3 0.0 copy-start
  35.3 0.0 copy-start.1
  35.3 0.0 copy-start.2
  35.3 0.0 copy-start.3
  35.3 0.1 collective-permute-start
  35.4 1.4 %collective-permute-done = f32[384,128]{1,0:T(8,128)S(1)} collective-permute-done((f32[384,128]{1,0:T(8,128)S(1)}, f32[384,128]{1,0:T(8,128)S(1)}, u32[]{:S(2)}, u32[]{:S(2)}) %collective-permute-start) | collective-permute-done | bytes 196640 | tf_op jit(solution)/shard_map/ppermute | solution.py:1131
  36.8 12.1 %all_to_all.16 = f32[16,24,128]{2,1,0:T(8,128)S(1)} all-to-all(f32[16,24,128]{2,1,0:T(8,128)S(1)} %bitcast.25), channel_id=1, replica_groups=mesh['atoms'=8,'high'=2,'low'=2] {'atoms','high'}, dimensions={0} | all-to-all | bytes 393216 | tf_op jit(solution)/shard_map/all_to_all | solution.py:1134
  49.0 11.3 %all_to_all.17 = f32[16,24,128]{2,1,0:T(8,128)S(1)} all-to-all(f32[16,24,128]{2,1,0:T(8,128)S(1)} %broadcast_in_dim.2), channel_id=1, replica_groups=mesh['atoms'=8,'high'=2,'low'=2] {'atoms','high'}, dimensions={0} | all-to-all | bytes 393216 | tf_op jit(solution)/shard_map/all_to_all | solution.py:1136
  60.3 0.0 collective-permute-start.1
  60.3 1.4 %collective-permute-done.1.other = f32[384,128]{1,0:T(8,128)S(1)} collective-permute-done((f32[384,128]{1,0:T(8,128)S(1)}, f32[384,128]{1,0:T(8,128)S(1)}, u32[]{:S(2)}, u32[]{:S(2)}) %collective-permute-start.1) | collective-permute-done | bytes 196640 | tf_op jit(solution)/shard_map/ppermute | solution.py:1138
  61.7 0.0 copy-done
  61.7 0.0 copy-done.1
  61.7 0.0 copy-done.2
  61.7 0.0 copy-done.3
  61.7 1.7 %update.1 = (f32[1,1]{1,0:T(1,128)}, f32[1,1]{1,0:T(1,128)}, f32[1,1]{1,0:T(1,128)}, f32[698,128]{1,0:T(8,128)}, f32[698,128]{1,0:T(8,128)}, /*index=5*/f32[698,...) custom-call(f32[384,128]{1,0:T(8,128)S(1)} %bitcast.21, f32[384,128]{1,0:T(8,128)S(1)} %collective-permute-done.1.other, ...), custom_call_target="tpu_custom_call" | custom-call | tf_op jit(solution)/shard_map/update/pallas_call | solution.py:1140
  (3 shorter events, 0.1 us)
Async XLA Ops:
  35.3 26.4 %copy-start = (f32[89344]{0:T(1024)S(1)}, f32[89344]{0:T(1024)}, u32[]{:S(2)}) copy-start(f32[89344]{0:T(1024)} %param.11) | copy-start | bytes 1072132
  35.3 26.4 %copy-start.1 = (f32[89344]{0:T(1024)S(1)}, f32[89344]{0:T(1024)}, u32[]{:S(2)}) copy-start(f32[89344]{0:T(1024)} %param.12) | copy-start | bytes 1072132
  35.3 26.4 %copy-start.2 = (f32[89344]{0:T(1024)S(1)}, f32[89344]{0:T(1024)}, u32[]{:S(2)}) copy-start(f32[89344]{0:T(1024)} %param.13) | copy-start | bytes 1072132
  35.3 26.4 %copy-start.3 = (f32[89344]{0:T(1024)S(1)}, f32[89344]{0:T(1024)}, u32[]{:S(2)}) copy-start(f32[89344]{0:T(1024)} %param.14) | copy-start | bytes 1072132
  35.3 1.5 %collective-permute-start = (f32[384,128]{1,0:T(8,128)S(1)}, f32[384,128]{1,0:T(8,128)S(1)}, u32[]{:S(2)}, u32[]{:S(2)}) collective-permute-start(f32[384,128]{1,0:T(8,128)S(1)} %get-tuple-element.119), channel_id=1, source_target_pairs={{0,1},{1,0},{2,3},{3,2},{4,5},{5,4},{6,7},{7,6},{8,9},{9,8},{10,11... | collective-permute-start | bytes 589832 | tf_op jit(solution)/shard_map/ppermute | solution.py:1131
  60.3 1.4 %collective-permute-start.1 = (f32[384,128]{1,0:T(8,128)S(1)}, f32[384,128]{1,0:T(8,128)S(1)}, u32[]{:S(2)}, u32[]{:S(2)}) collective-permute-start(f32[384,128]{1,0:T(8,128)S(1)} %bitcast.20), channel_id=1, source_target_pairs={{0,1},{1,0},{2,3},{3,2},{4,5},{5,4},{6,7},{7,6},{8,9},{9,8},{10,11... | collective-permute-start | bytes 589832 | tf_op jit(solution)/shard_map/ppermute | solution.py:1138

commit v3 on v2

--- a/solution.py
+++ b/solution.py
@@ -414,7 +414,7 @@
     ]
     for copy in copies:
         copy.start()
-    for copy in copies[:-1]:
+    for copy in copies[:6]:
         copy.wait()
 
     order = sc.tmp.at[10]
@@ -467,7 +467,7 @@
         st.hot[:, tile(t)] = (rows_of((ATOMS, 128)) == local[t : t + 1]).astype(f32).astype(bf16)
     phi = keep_pair(st.phi, (), jnp.concatenate(tiles, 1))
 
-    copies[-1].wait()
+    copies[6].wait()
     prepare(par, st, sc)
     fw = spread_rows(f)
 
@@ -667,8 +667,14 @@
         payload[3 * ranks + q : 3 * ranks + q + 1, 0:32] = tgt[q]
     payload[3 * ranks + 3 : 3 * ranks + 4, 0:32] = (lanes((1, 32)) < live[0, 0]).astype(f32)
 
+    deep = pay.shape[1]
+    packed = payload[0:deep, :]
+    for g in range(1, 4):
+        packed = packed + spin(payload[g * deep : g * deep + deep, :], 32 * g)
+    payload[0:deep, :] = packed
+
     def spread(j, carry):
-        pay[j] = payload[...]
+        pay[j] = payload[0:deep, :]
         return carry
 
     lax.fori_loop(0, ranks, spread, 0)
@@ -699,12 +705,17 @@
     me = lax.axis_index(axis)
     geo, gd = st.geo, sc.gd
 
-    total = got[0, 0 : 3 * ranks, :]
+    deep = got.shape[1]
+    total = got[0]
     for j in range(1, ranks):
-        total = total + got[j, 0 : 3 * ranks, :]
+        total = total + got[j]
+    first = lanes((deep, 128)) < 32
+    total = jnp.concatenate([jnp.where(first, spin(total, -32 * g), 0.0) for g in range(4)], 0)
     for j in range(ranks):
+        own = got[j, 3 * ranks - 3 * deep : 3 * ranks - 3 * deep + 4, :]
         for q in range(4):
-            tm[q * ranks + j : q * ranks + j + 1, :] = got[j, 3 * ranks + q : 3 * ranks + q + 1, :]
+            tm[q * ranks + j : q * ranks + j + 1, :] = own[q : q + 1]
+    tm[...] = jnp.where(lanes((4 * ranks, 128)) < 32, spin(tm[...], -96), 0.0)
     mask = tm[3 * ranks : 4 * ranks, :]
     mine = rows_of((ranks, 128)) == me
     loss = jnp.zeros((ranks, 128), f32)
@@ -870,13 +881,16 @@
 
         return finish
 
-    def split_middle():
+    def middle_products():
         parts = [split(sc.mid[k, 0:96, :]) for k in range(LAYERS)]
         ones = [product(st.wf_inv[k], *parts[k]) for k in range(LAYERS)]
         invs = []
         for k, (high, low) in enumerate(parts):
             inv = cross(jnp.concatenate([high, low, high], 1), st.wb_h[k, 96:160, :])
             invs.append(jnp.concatenate([inv, jnp.zeros((96, 64), f32)], 1))
+        return ones, invs
+
+    def finish_middle(ones, invs):
         for k in range(LAYERS):
             at = AT_ONE + 64 * k
             sc.grad[at : at + 64, :] = sc.mid[k, 96:160, :] + ones[k]
@@ -1013,7 +1027,7 @@
         packed(AT_EMBED, 9),
     )
     work(len(queue))
-    split_middle()
+    finish_middle(*middle_products())
     sc.grad[ROWS:PADDED, :] = jnp.zeros((PADDED - ROWS, 128), f32)
     lane = lanes((1, 128))
     amount = 3.0 * live[0, 0].astype(f32)
@@ -1086,7 +1100,7 @@
     flat = (ROWS, 128)
     par = params.reshape(flat)
     live = live_atoms.reshape(1, 1)
-    tall = 3 * ranks + 8
+    tall = 32 * -(-(3 * ranks + 4) // 32)
     state = [shape(s, t) for _, s, t in STATE]
     sources = (
         edge_vectors.reshape(3, 8, 128),
@@ -1099,7 +1113,7 @@
     )
     pay, *kept = pl.pallas_call(
         functools.partial(first_kernel, ranks, "atoms"),
-        out_shape=[shape((ranks, tall, 128), f32), *state],
+        out_shape=[shape((ranks, tall // 4, 128), f32), *state],
         in_specs=[SMEM] + [HBM] * 7,
         out_specs=[VMEM] * (1 + len(state)),
         scratch_shapes=[

time: 63.7 us -> 62.8 us (0.986)
  blocking collectives: 37.8 us -> 36.8 us
    all_to_all x1, blocking collectives: 14.4 us -> 13.8 us  [local(): got = lax.all_to_all(pay, 'atoms', split_axis=0, concat_axis=0, tiled=True)]
where the time goes in v3:
time: 62.8 us; the launch traced here: 62.5 us
  blocking collectives  36.8 us (59%)
  Pallas kernels  21.3 us (34%)
  waiting for transfers between devices  2.87 us (5%)
  between operations  1.34 us (2%)
    all_to_all x1, blocking collectives, local(): got = lax.all_to_all(pay, 'atoms', split_axis=0, concat_axis=0, tiled=True)  13.8 us
    all_to_all x1, blocking collectives, local(): lax.all_to_all(held, axes, split_axis=0, concat_axis=0, tiled=True).sum(0)  11.5 us
    all_to_all x1, blocking collectives, local(): mine = lax.all_to_all(summed, axes, split_axis=0, concat_axis=0, tiled=True)  11.5 us
    pallas_call x1, Pallas kernels, local(): pl.pallas_call(functools.partial(second_kernel, ranks, 'atoms', 'low'), o...  10.1 us
    pallas_call x1, Pallas kernels, local(): pl.pallas_call(functools.partial(first_kernel, ranks, 'atoms'), out_shape...  9.56 us
    pallas_call x1, Pallas kernels, local(): pl.pallas_call(functools.partial(third_kernel, 'low'), out_shape=[one, on...  1.7 us
    ppermute x1, waiting for transfers between devices, local(): other = lax.ppermute(mine, 'low', swap)  1.44 us
    ppermute x1, waiting for transfers between devices, local(): held = keep + lax.ppermute(give, 'low', swap)  1.43 us
  transfers between devices with their start and end apart: 2, of which 2 were waited for; matrix products, arithmetic and copies ran while one was open for 0% of the time, Pallas kernels for 0%

profile of v3, /device:TPU:0, one launch (start us, length us, event | category | flops | bytes accessed | tf_op | source)
XLA Modules:
  0.0 62.5 jit_solution(14103353526852199860)
XLA Ops:
  1.3 9.6 %forward.1 = (f32[8,8,128]{2,1,0:T(8,128)S(1)}, bf16[64,96]{1,0:T(8,128)(2,1)S(1)}, bf16[64,192]{1,0:T(8,128)(2,1)S(1)}, bf16[3,256,192]{2,1,0:T(8,128)(2,1)S(1)...) custom-call(s32[1,1]{1,0:T(1,128)S(6)} %copy.20.live, ...), custom_call_target="tpu_custom_call" | custom-call | tf_op jit(solution)/shard_map/forward/pallas_call | solution.py:1114
  10.9 13.8 %all_to_all.15.got = f32[8,8,128]{2,1,0:T(8,128)S(1)} all-to-all(f32[8,8,128]{2,1,0:T(8,128)S(1)} %get-tuple-element.69), channel_id=1, replica_groups=mesh['atoms'=8,'high'=2,'low'=2] {'atoms'}, dimensions={0} | all-to-all | bytes 65536 | tf_op jit(solution)/shard_map/all_to_all | solution.py:1129
  24.6 10.1 %gradient.1 = (f32[384,128]{1,0:T(8,128)S(1)}, f32[384,128]{1,0:T(8,128)S(1)}, f32[3,1,32]{2,1,0:T(1,128)}) custom-call(s32[1,1]{1,0:T(1,128)S(6)} %copy.20.live, f32[8,8,128]{2,1,0:T(8,128)S(1)} %all_to_all.15.got, bf16[64,96]{1,0:T(8,128)(2,1)S(1)} %get-tuple-element.70.refs_0_, bf16[64,192]{1,0:T(8,128)(2,1)S(1)} %get-tuple-element.71.refs_1_, ...), custom_call_target="tpu_custom_call" | custom-call | tf_op jit(solution)/shard_map/gradient/pallas_call | solution.py:1130
  34.7 0.0 copy-start
  34.7 0.0 copy-start.1
  34.7 0.0 copy-start.2
  34.7 0.0 copy-start.3
  34.7 0.1 collective-permute-start
  34.8 1.4 %collective-permute-done = f32[384,128]{1,0:T(8,128)S(1)} collective-permute-done((f32[384,128]{1,0:T(8,128)S(1)}, f32[384,128]{1,0:T(8,128)S(1)}, u32[]{:S(2)}, u32[]{:S(2)}) %collective-permute-start) | collective-permute-done | bytes 196640 | tf_op jit(solution)/shard_map/ppermute | solution.py:1145
  36.2 11.5 %all_to_all.16 = f32[16,24,128]{2,1,0:T(8,128)S(1)} all-to-all(f32[16,24,128]{2,1,0:T(8,128)S(1)} %bitcast.25), channel_id=1, replica_groups=mesh['atoms'=8,'high'=2,'low'=2] {'atoms','high'}, dimensions={0} | all-to-all | bytes 393216 | tf_op jit(solution)/shard_map/all_to_all | solution.py:1148
  47.8 11.5 %all_to_all.17 = f32[16,24,128]{2,1,0:T(8,128)S(1)} all-to-all(f32[16,24,128]{2,1,0:T(8,128)S(1)} %broadcast_in_dim.2), channel_id=1, replica_groups=mesh['atoms'=8,'high'=2,'low'=2] {'atoms','high'}, dimensions={0} | all-to-all | bytes 393216 | tf_op jit(solution)/shard_map/all_to_all | solution.py:1150
  59.3 0.0 collective-permute-start.1
  59.3 1.4 %collective-permute-done.1.other = f32[384,128]{1,0:T(8,128)S(1)} collective-permute-done((f32[384,128]{1,0:T(8,128)S(1)}, f32[384,128]{1,0:T(8,128)S(1)}, u32[]{:S(2)}, u32[]{:S(2)}) %collective-permute-start.1) | collective-permute-done | bytes 196640 | tf_op jit(solution)/shard_map/ppermute | solution.py:1152
  60.8 0.0 copy-done
  60.8 0.0 copy-done.1
  60.8 0.0 copy-done.2
  60.8 0.0 copy-done.3
  60.8 1.7 %update.1 = (f32[1,1]{1,0:T(1,128)}, f32[1,1]{1,0:T(1,128)}, f32[1,1]{1,0:T(1,128)}, f32[698,128]{1,0:T(8,128)}, f32[698,128]{1,0:T(8,128)}, /*index=5*/f32[698,...) custom-call(f32[384,128]{1,0:T(8,128)S(1)} %bitcast.21, f32[384,128]{1,0:T(8,128)S(1)} %collective-permute-done.1.other, ...), custom_call_target="tpu_custom_call" | custom-call | tf_op jit(solution)/shard_map/update/pallas_call | solution.py:1154
  (3 shorter events, 0.1 us)
Async XLA Ops:
  34.7 26.1 %copy-start = (f32[89344]{0:T(1024)S(1)}, f32[89344]{0:T(1024)}, u32[]{:S(2)}) copy-start(f32[89344]{0:T(1024)} %param.11) | copy-start | bytes 1072132
  34.7 26.1 %copy-start.1 = (f32[89344]{0:T(1024)S(1)}, f32[89344]{0:T(1024)}, u32[]{:S(2)}) copy-start(f32[89344]{0:T(1024)} %param.12) | copy-start | bytes 1072132
  34.7 26.1 %copy-start.2 = (f32[89344]{0:T(1024)S(1)}, f32[89344]{0:T(1024)}, u32[]{:S(2)}) copy-start(f32[89344]{0:T(1024)} %param.13) | copy-start | bytes 1072132
  34.7 26.1 %copy-start.3 = (f32[89344]{0:T(1024)S(1)}, f32[89344]{0:T(1024)}, u32[]{:S(2)}) copy-start(f32[89344]{0:T(1024)} %param.14) | copy-start | bytes 1072132
  34.7 1.5 %collective-permute-start = (f32[384,128]{1,0:T(8,128)S(1)}, f32[384,128]{1,0:T(8,128)S(1)}, u32[]{:S(2)}, u32[]{:S(2)}) collective-permute-start(f32[384,128]{1,0:T(8,128)S(1)} %get-tuple-element.119), channel_id=1, source_target_pairs={{0,1},{1,0},{2,3},{3,2},{4,5},{5,4},{6,7},{7,6},{8,9},{9,8},{10,11... | collective-permute-start | bytes 589832 | tf_op jit(solution)/shard_map/ppermute | solution.py:1145
  59.3 1.4 %collective-permute-start.1 = (f32[384,128]{1,0:T(8,128)S(1)}, f32[384,128]{1,0:T(8,128)S(1)}, u32[]{:S(2)}, u32[]{:S(2)}) collective-permute-start(f32[384,128]{1,0:T(8,128)S(1)} %bitcast.20), channel_id=1, source_target_pairs={{0,1},{1,0},{2,3},{3,2},{4,5},{5,4},{6,7},{7,6},{8,9},{9,8},{10,11... | collective-permute-start | bytes 589832 | tf_op jit(solution)/shard_map/ppermute | solution.py:1152

commit v4 on v3

--- a/solution.py
+++ b/solution.py
@@ -407,7 +407,7 @@
     vec, own, loc, nsp, cen, tgt, par = rest[0:7]
     sems, payload, scatter = rest[7:10]
     sc = Refs(SCRATCH_A, rest[10:])
-    me = lax.axis_index(axis)
+    me = 2 * lax.axis_index(axis[0]) + lax.axis_index(axis[1])
     copies = [
         pltpu.make_async_copy(source, target, sems.at[n])
         for n, (source, target) in enumerate(zip(sources, rest[0:7], strict=True))
@@ -702,7 +702,7 @@
     st = Refs(STATE, refs[: len(STATE)])
     keep, give, forces, tm, aim = refs[len(STATE) : len(STATE) + 5]
     sc = Refs(SCRATCH_B, refs[len(STATE) + 5 :])
-    me = lax.axis_index(axis)
+    me = 2 * lax.axis_index(axis[0]) + lax.axis_index(axis[1])
     geo, gd = st.geo, sc.gd
 
     deep = got.shape[1]
@@ -1040,10 +1040,14 @@
 
 
 def third_kernel(pick, mine, other, par, first, second, avg, *outs):
-    loss, count, norm, new_first, new_second, new_par, low, new_avg = outs
+    loss, count, norm, new_first, new_second, new_par, low, new_avg, order = outs
     half = lax.axis_index(pick)
-    lower = jnp.where(half == 0, mine[...], other[...])
-    upper = jnp.where(half == 0, other[...], mine[...])
+    spot = 2 * lax.axis_index("near") + lax.axis_index("high")
+    for k in range(4):
+        order[half, spot ^ k] = mine[k]
+        order[1 - half, spot ^ k] = other[k]
+    lower = jnp.concatenate([order[0, k] for k in range(4)], 0)
+    upper = jnp.concatenate([order[1, k] for k in range(4)], 0)
     last = ROWS - HALF
     scalars = upper[last : last + 1]
     loss[...] = scalars[:, 0:1]
@@ -1073,6 +1077,8 @@
         new_avg[rows, :] = average_keep * avg[rows, :] + (1.0 - average_keep) * weights
 
 
+ATOM_AXES = ("far", "near")
+PLANE = ("near", "high")
 VMEM = pl.BlockSpec(memory_space=pltpu.VMEM)
 HBM = pl.BlockSpec(memory_space=pltpu.HBM)
 SMEM = pl.BlockSpec(memory_space=pltpu.SMEM)
@@ -1112,7 +1118,7 @@
         par,
     )
     pay, *kept = pl.pallas_call(
-        functools.partial(first_kernel, ranks, "atoms"),
+        functools.partial(first_kernel, ranks, ATOM_AXES),
         out_shape=[shape((ranks, tall // 4, 128), f32), *state],
         in_specs=[SMEM] + [HBM] * 7,
         out_specs=[VMEM] * (1 + len(state)),
@@ -1126,9 +1132,9 @@
         compiler_params=pltpu.CompilerParams(vmem_limit_bytes=16 * 2**20),
         name="forward",
     )(live, *[pltpu.with_memory_space_constraint(x, pltpu.HBM) for x in sources])
-    got = lax.all_to_all(pay, "atoms", split_axis=0, concat_axis=0, tiled=True)
+    got = lax.all_to_all(pay, ATOM_AXES, split_axis=0, concat_axis=0, tiled=True)
     keep, give, forces = pl.pallas_call(
-        functools.partial(second_kernel, ranks, "atoms", "low"),
+        functools.partial(second_kernel, ranks, ATOM_AXES, "low"),
         out_shape=[shape((HALF, 128), f32), shape((HALF, 128), f32), shape((3, 1, ATOMS), f32)],
         in_specs=[SMEM, VMEM] + [VMEM] * len(state),
         out_specs=[VMEM] * 3,
@@ -1141,14 +1147,21 @@
         name="gradient",
     )(live, got, *kept)
     swap = [(0, 1), (1, 0)]
-    axes, size = ("atoms", "high"), ranks * 2
-    held = keep + lax.ppermute(give, "low", swap)
-    pieces = size * 8 * -(-HALF // (8 * size))
-    held = jnp.pad(held, ((0, pieces - HALF), (0, 0))).reshape(size, pieces // size, 128)
-    summed = lax.all_to_all(held, axes, split_axis=0, concat_axis=0, tiled=True).sum(0)
-    summed = jnp.broadcast_to(summed[None], (size, *summed.shape))
-    mine = lax.all_to_all(summed, axes, split_axis=0, concat_axis=0, tiled=True)
-    mine = mine.reshape(pieces, 128)[:HALF]
+    held = (keep + lax.ppermute(give, "low", swap)).reshape(4, HALF // 4, 128)
+    spot = 2 * lax.axis_index("near") + lax.axis_index("high")
+    across_plane = [[(i, i ^ k) for i in range(4)] for k in (1, 2, 3)]
+    part = lax.dynamic_index_in_dim(held, spot, 0, False)
+    for k in (1, 2, 3):
+        piece = lax.dynamic_index_in_dim(held, spot ^ k, 0, False)
+        part = part + lax.ppermute(piece, PLANE, across_plane[k - 1])
+    far = ranks // 2
+    if far == 4:
+        one, two, three = (lax.ppermute(part, "far", [(i, i ^ k) for i in range(4)]) for k in (1, 2, 3))
+        whole = (part + one) + (two + three)
+    else:
+        whole = jnp.broadcast_to(part[None], (far, *part.shape))
+        whole = lax.all_to_all(whole, "far", split_axis=0, concat_axis=0, tiled=True).sum(0)
+    mine = jnp.stack([whole] + [lax.ppermute(whole, PLANE, p) for p in across_plane])
     other = lax.ppermute(mine, "low", swap)
     one, vec = shape((1, 1), f32), shape(flat, f32)
     loss, count, norm, new_first, new_second, new_params, low, new_average = pl.pallas_call(
@@ -1156,6 +1169,7 @@
         out_shape=[one, one, one, vec, vec, vec, shape(flat, bf16), vec],
         in_specs=[VMEM] * 6,
         out_specs=[VMEM] * 8,
+        scratch_shapes=[pltpu.VMEM((2, 4, HALF // 4, 128), f32)],
         compiler_params=pltpu.CompilerParams(vmem_limit_bytes=16 * 2**20),
         name="update",
     )(
@@ -1181,22 +1195,23 @@
 
 def solution(mesh):
     ranks, groups = mesh.shape["atoms"], mesh.shape["grp"]
-    fine = Mesh(mesh.devices.reshape(ranks, groups // 2, 2), ("atoms", "high", "low"))
-    grp = ("high", "low")
+    shape = (ranks // 2, 2, groups // 2, 2)
+    fine = Mesh(mesh.devices.reshape(shape), ("far", "near", "high", "low"))
+    grp, atoms = ("high", "low"), ATOM_AXES
     in_specs = (
         P(),
         P(),
         P(),
         P(),
-        P(None, grp, "atoms"),
-        P(grp, "atoms", None),
-        P(grp, "atoms"),
-        P(grp, "atoms"),
-        P(grp, "atoms"),
-        P(grp, "atoms"),
-        P(None, grp, "atoms"),
+        P(None, grp, atoms),
+        P(grp, atoms, None),
+        P(grp, atoms),
+        P(grp, atoms),
+        P(grp, atoms),
+        P(grp, atoms),
+        P(None, grp, atoms),
     )
-    out_specs = (P(), P(), P(), P(None, grp, "atoms"), P(), P(), P(), P(), P())
+    out_specs = (P(), P(), P(), P(None, grp, atoms), P(), P(), P(), P(), P())
     return jax.shard_map(
         functools.partial(local, ranks),
         mesh=fine,

time: 62.8 us -> 61.1 us (0.973)
  blocking collectives: 36.8 us -> 13.8 us
  starting transfers between devices: 0.07 us -> 11.7 us
  waiting for transfers between devices: 2.87 us -> 12.6 us
    all_to_all x3 -> x1, blocking collectives: 36.8 us -> 13.8 us  [local(): lax.all_to_all(pay, ATOM_AXES, split_axis=0, concat_axis=0, tiled=True)]
    ppermute x1 -> x10, starting transfers between devices: 0.07 us -> 11.6 us  [the longest x3 4.45 us: local(): lax.ppermute(part, 'far', [(i, i ^ k) for i in range(4)])]
    ppermute x1 -> x10, waiting for transfers between devices: 1.43 us -> 11.2 us  [the longest x3 3.46 us: local(): part = part + lax.ppermute(piece, PLANE, across_plane[k - 1])]
  transfers between devices with their start and end apart: 2 -> 11, of which waited for: 2 -> 10; matrix products, arithmetic and copies ran while one was open for 0% -> 0% of each run, Pallas kernels for 0% -> 0%
where the time goes in v4:
time: 61.1 us; the launch traced here: 60.9 us
  Pallas kernels  21.3 us (35%)
  blocking collectives  13.8 us (23%)
  waiting for transfers between devices  12.6 us (21%)
  starting transfers between devices  11.7 us (19%)
  between operations  1.39 us (2%)
    all_to_all x1, blocking collectives, local(): lax.all_to_all(pay, ATOM_AXES, split_axis=0, concat_axis=0, tiled=True)  13.8 us
    pallas_call x1, Pallas kernels, local(): pl.pallas_call(functools.partial(second_kernel, ranks, ATOM_AXES, 'low'),...  10.1 us
    pallas_call x1, Pallas kernels, local(): pl.pallas_call(functools.partial(first_kernel, ranks, ATOM_AXES), out_sha...  9.56 us
    ppermute x3, starting transfers between devices, local(): lax.ppermute(part, 'far', [(i, i ^ k) for i in range(4)])  4.45 us
    ppermute x3, starting transfers between devices, local(): part = part + lax.ppermute(piece, PLANE, across_plane[k - 1])  3.55 us
    ppermute x3, starting transfers between devices, local(): lax.ppermute(whole, PLANE, p)  3.55 us
    ppermute x3, waiting for transfers between devices, local(): part = part + lax.ppermute(piece, PLANE, across_plane[k - 1])  3.46 us
    ppermute x3, waiting for transfers between devices, local(): lax.ppermute(whole, PLANE, p)  3.4 us
  transfers between devices with their start and end apart: 11, of which 10 were waited for; matrix products, arithmetic and copies ran while one was open for 0% of the time, Pallas kernels for 0%

profile of v4, /device:TPU:0, one launch (start us, length us, event | category | flops | bytes accessed | tf_op | source)
XLA Modules:
  0.0 60.9 jit_solution(12397983194503099281)
XLA Ops:
  1.3 9.6 %forward.1 = (f32[8,8,128]{2,1,0:T(8,128)S(1)}, bf16[64,96]{1,0:T(8,128)(2,1)S(1)}, bf16[64,192]{1,0:T(8,128)(2,1)S(1)}, bf16[3,256,192]{2,1,0:T(8,128)(2,1)S(1)...) custom-call(s32[1,1]{1,0:T(1,128)S(6)} %copy.20.live, ...), custom_call_target="tpu_custom_call" | custom-call | tf_op jit(solution)/shard_map/forward/pallas_call | solution.py:1120
  10.9 13.8 %all_to_all.5.got = f32[8,8,128]{2,1,0:T(8,128)S(1)} all-to-all(f32[8,8,128]{2,1,0:T(8,128)S(1)} %get-tuple-element.69), channel_id=1, replica_groups=mesh['far'=4,'near'=2,'high'=2,'low'=2] {'far','near'}, dimensions={0} | all-to-all | bytes 65536 | tf_op jit(solution)/shard_map/all_to_all | solution.py:1135
  24.6 10.1 %gradient.1 = (f32[384,128]{1,0:T(8,128)S(1)}, f32[384,128]{1,0:T(8,128)S(1)}, f32[3,1,32]{2,1,0:T(1,128)}) custom-call(s32[1,1]{1,0:T(1,128)S(6)} %copy.20.live, f32[8,8,128]{2,1,0:T(8,128)S(1)} %all_to_all.5.got, bf16[64,96]{1,0:T(8,128)(2,1)S(1)} %get-tuple-element.70.refs_0_, bf16[64,192]{1,0:T(8,128)(2,1)S(1)} %get-tuple-element.71.refs_1_, ...), custom_call_target="tpu_custom_call" | custom-call | tf_op jit(solution)/shard_map/gradient/pallas_call | solution.py:1136
  34.7 0.0 copy-start
  34.7 0.0 copy-start.1
  34.7 0.0 copy-start.2
  34.7 0.0 copy-start.3
  34.7 0.1 collective-permute-start
  34.8 1.4 %collective-permute-done = f32[384,128]{1,0:T(8,128)S(1)} collective-permute-done((f32[384,128]{1,0:T(8,128)S(1)}, f32[384,128]{1,0:T(8,128)S(1)}, u32[]{:S(2)}, u32[]{:S(2)}) %collective-permute-start) | collective-permute-done | bytes 196640 | tf_op jit(solution)/shard_map/ppermute | solution.py:1150
  36.2 1.5 %collective-permute-start.1 = (f32[96,128]{1,0:T(8,128)S(1)}, f32[96,128]{1,0:T(8,128)S(1)}, u32[]{:S(2)}, u32[]{:S(2)}) collective-permute-start(f32[96,128]{1,0:T(8,128)S(1)} %get-tuple-element.129), channel_id=1, source_target_pairs={{0,2},{2,0},{4,6},{6,4},{1,3},{3,1},{5,7},{7,5},{8,10},{10,8},{12,... | collective-permute-start | bytes 147464 | tf_op jit(solution)/shard_map/ppermute | solution.py:1156
  37.8 0.5 collective-permute-start.2
  38.3 1.5 %collective-permute-start.3 = (f32[96,128]{1,0:T(8,128)S(1)}, f32[96,128]{1,0:T(8,128)S(1)}, u32[]{:S(2)}, u32[]{:S(2)}) collective-permute-start(f32[96,128]{1,0:T(8,128)S(1)} %get-tuple-element.130), channel_id=1, source_target_pairs={{0,6},{2,4},{4,2},{6,0},{1,7},{3,5},{5,3},{7,1},{8,14},{10,12},{12... | collective-permute-start | bytes 147464 | tf_op jit(solution)/shard_map/ppermute | solution.py:1156
  39.8 0.6 collective-permute-done.1
  40.4 2.0 %collective-permute-done.2 = f32[96,128]{1,0:T(8,128)S(1)} collective-permute-done((f32[96,128]{1,0:T(8,128)S(1)}, f32[96,128]{1,0:T(8,128)S(1)}, u32[]{:S(2)}, u32[]{:S(2)}) %collective-permute-start.2) | collective-permute-done | bytes 49184 | tf_op jit(solution)/shard_map/ppermute | solution.py:1156
  42.4 0.9 %collective-permute-done.3 = f32[96,128]{1,0:T(8,128)S(1)} collective-permute-done((f32[96,128]{1,0:T(8,128)S(1)}, f32[96,128]{1,0:T(8,128)S(1)}, u32[]{:S(2)}, u32[]{:S(2)}) %collective-permute-start.3) | collective-permute-done | bytes 49184 | tf_op jit(solution)/shard_map/ppermute | solution.py:1156
  43.3 0.8 %collective-permute-start.4 = (f32[96,128]{1,0:T(8,128)S(1)}, f32[96,128]{1,0:T(8,128)S(1)}, u32[]{:S(2)}, u32[]{:S(2)}) collective-permute-start(f32[96,128]{1,0:T(8,128)S(1)} %fusion.1), channel_id=1, source_target_pairs={{0,8},{8,0},{16,24},{24,16},{1,9},{9,1},{17,25},{25,17},{2,10},{10... | collective-permute-start | bytes 147464 | tf_op jit(solution)/shard_map/ppermute | solution.py:1159
  44.0 0.6 %collective-permute-start.5 = (f32[96,128]{1,0:T(8,128)S(1)}, f32[96,128]{1,0:T(8,128)S(1)}, u32[]{:S(2)}, u32[]{:S(2)}) collective-permute-start(f32[96,128]{1,0:T(8,128)S(1)} %fusion.1), channel_id=1, source_target_pairs={{0,16},{8,24},{16,0},{24,8},{1,17},{9,25},{17,1},{25,9},{2,18},{10... | collective-permute-start | bytes 147464 | tf_op jit(solution)/shard_map/ppermute | solution.py:1159
  44.7 3.0 %collective-permute-start.6 = (f32[96,128]{1,0:T(8,128)S(1)}, f32[96,128]{1,0:T(8,128)S(1)}, u32[]{:S(2)}, u32[]{:S(2)}) collective-permute-start(f32[96,128]{1,0:T(8,128)S(1)} %fusion.1), channel_id=1, source_target_pairs={{0,24},{8,16},{16,8},{24,0},{1,25},{9,17},{17,9},{25,1},{2,26},{10... | collective-permute-start | bytes 147464 | tf_op jit(solution)/shard_map/ppermute | solution.py:1159
  47.7 0.0 collective-permute-done.4
  47.7 1.3 %collective-permute-done.5 = f32[96,128]{1,0:T(8,128)S(1)} collective-permute-done((f32[96,128]{1,0:T(8,128)S(1)}, f32[96,128]{1,0:T(8,128)S(1)}, u32[]{:S(2)}, u32[]{:S(2)}) %collective-permute-start.5) | collective-permute-done | bytes 49184 | tf_op jit(solution)/shard_map/ppermute | solution.py:1159
  49.0 1.6 %collective-permute-done.6 = f32[96,128]{1,0:T(8,128)S(1)} collective-permute-done((f32[96,128]{1,0:T(8,128)S(1)}, f32[96,128]{1,0:T(8,128)S(1)}, u32[]{:S(2)}, u32[]{:S(2)}) %collective-permute-start.6) | collective-permute-done | bytes 49184 | tf_op jit(solution)/shard_map/ppermute | solution.py:1159
  50.6 0.6 %collective-permute-start.7 = (f32[96,128]{1,0:T(8,128)S(1)}, f32[96,128]{1,0:T(8,128)S(1)}, u32[]{:S(2)}, u32[]{:S(2)}) collective-permute-start(f32[96,128]{1,0:T(8,128)S(1)} %add_add_fusion), channel_id=1, source_target_pairs={{0,2},{2,0},{4,6},{6,4},{1,3},{3,1},{5,7},{7,5},{8,10},{10,8},{12,... | collective-permute-start | bytes 147464 | tf_op jit(solution)/shard_map/ppermute | solution.py:1164
  51.2 1.4 %collective-permute-start.8 = (f32[96,128]{1,0:T(8,128)S(1)}, f32[96,128]{1,0:T(8,128)S(1)}, u32[]{:S(2)}, u32[]{:S(2)}) collective-permute-start(f32[96,128]{1,0:T(8,128)S(1)} %add_add_fusion), channel_id=1, source_target_pairs={{0,4},{2,6},{4,0},{6,2},{1,5},{3,7},{5,1},{7,3},{8,12},{10,14},{12... | collective-permute-start | bytes 147464 | tf_op jit(solution)/shard_map/ppermute | solution.py:1164
  52.6 1.6 %collective-permute-start.9 = (f32[96,128]{1,0:T(8,128)S(1)}, f32[96,128]{1,0:T(8,128)S(1)}, u32[]{:S(2)}, u32[]{:S(2)}) collective-permute-start(f32[96,128]{1,0:T(8,128)S(1)} %add_add_fusion), channel_id=1, source_target_pairs={{0,6},{2,4},{4,2},{6,0},{1,7},{3,5},{5,3},{7,1},{8,14},{10,12},{12... | collective-permute-start | bytes 147464 | tf_op jit(solution)/shard_map/ppermute | solution.py:1164
  54.2 0.6 collective-permute-done.7
  54.8 0.5 collective-permute-done.8
  55.3 2.3 %collective-permute-done.9 = f32[96,128]{1,0:T(8,128)S(1)} collective-permute-done((f32[96,128]{1,0:T(8,128)S(1)}, f32[96,128]{1,0:T(8,128)S(1)}, u32[]{:S(2)}, u32[]{:S(2)}) %collective-permute-start.9) | collective-permute-done | bytes 49184 | tf_op jit(solution)/shard_map/ppermute | solution.py:1164
  57.6 0.1 collective-permute-start.10
  57.7 1.4 %collective-permute-done.10.other = f32[4,96,128]{2,1,0:T(8,128)S(1)} collective-permute-done((f32[4,96,128]{2,1,0:T(8,128)S(1)}, f32[4,96,128]{2,1,0:T(8,128)S(1)}, u32[]{:S(2)}, u32[]{:S(2)}) %collective-permute-start.10) | collective-permute-done | bytes 196640 | tf_op jit(solution)/shard_map/ppermute | solution.py:1165
  59.1 0.0 copy-done
  59.1 0.0 copy-done.1
  59.1 0.0 copy-done.2
  59.1 0.0 copy-done.3
  59.1 1.7 %update.1 = (f32[1,1]{1,0:T(1,128)}, f32[1,1]{1,0:T(1,128)}, f32[1,1]{1,0:T(1,128)}, f32[698,128]{1,0:T(8,128)}, f32[698,128]{1,0:T(8,128)}, /*index=5*/f32[698,...) custom-call(f32[4,96,128]{2,1,0:T(8,128)S(1)} %pad_maximum_fusion.mine, ...), custom_call_target="tpu_custom_call" | custom-call | tf_op jit(solution)/shard_map/update/pallas_call | solution.py:1167
  (5 shorter events, 0.1 us)
Async XLA Ops:
  34.7 24.5 %copy-start = (f32[89344]{0:T(1024)S(1)}, f32[89344]{0:T(1024)}, u32[]{:S(2)}) copy-start(f32[89344]{0:T(1024)} %param.11) | copy-start | bytes 1072132
  34.7 24.5 %copy-start.1 = (f32[89344]{0:T(1024)S(1)}, f32[89344]{0:T(1024)}, u32[]{:S(2)}) copy-start(f32[89344]{0:T(1024)} %param.12) | copy-start | bytes 1072132
  34.7 24.5 %copy-start.2 = (f32[89344]{0:T(1024)S(1)}, f32[89344]{0:T(1024)}, u32[]{:S(2)}) copy-start(f32[89344]{0:T(1024)} %param.13) | copy-start | bytes 1072132
  34.7 24.5 %copy-start.3 = (f32[89344]{0:T(1024)S(1)}, f32[89344]{0:T(1024)}, u32[]{:S(2)}) copy-start(f32[89344]{0:T(1024)} %param.14) | copy-start | bytes 1072132
  34.7 1.5 %collective-permute-start = (f32[384,128]{1,0:T(8,128)S(1)}, f32[384,128]{1,0:T(8,128)S(1)}, u32[]{:S(2)}, u32[]{:S(2)}) collective-permute-start(f32[384,128]{1,0:T(8,128)S(1)} %get-tuple-element.119), channel_id=1, source_target_pairs={{0,1},{1,0},{2,3},{3,2},{4,5},{5,4},{6,7},{7,6},{8,9},{9,8},{10,11... | collective-permute-start | bytes 589832 | tf_op jit(solution)/shard_map/ppermute | solution.py:1150
  36.2 4.2 %collective-permute-start.1 = (f32[96,128]{1,0:T(8,128)S(1)}, f32[96,128]{1,0:T(8,128)S(1)}, u32[]{:S(2)}, u32[]{:S(2)}) collective-permute-start(f32[96,128]{1,0:T(8,128)S(1)} %get-tuple-element.129), channel_id=1, source_target_pairs={{0,2},{2,0},{4,6},{6,4},{1,3},{3,1},{5,7},{7,5},{8,10},{10,8},{12,... | collective-permute-start | bytes 147464 | tf_op jit(solution)/shard_map/ppermute | solution.py:1156
  37.8 4.6 %collective-permute-start.2 = (f32[96,128]{1,0:T(8,128)S(1)}, f32[96,128]{1,0:T(8,128)S(1)}, u32[]{:S(2)}, u32[]{:S(2)}) collective-permute-start(f32[96,128]{1,0:T(8,128)S(1)} %get-tuple-element.131), channel_id=1, source_target_pairs={{0,4},{2,6},{4,0},{6,2},{1,5},{3,7},{5,1},{7,3},{8,12},{10,14},{12... | collective-permute-start | bytes 147464 | tf_op jit(solution)/shard_map/ppermute | solution.py:1156
  38.3 5.0 %collective-permute-start.3 = (f32[96,128]{1,0:T(8,128)S(1)}, f32[96,128]{1,0:T(8,128)S(1)}, u32[]{:S(2)}, u32[]{:S(2)}) collective-permute-start(f32[96,128]{1,0:T(8,128)S(1)} %get-tuple-element.130), channel_id=1, source_target_pairs={{0,6},{2,4},{4,2},{6,0},{1,7},{3,5},{5,3},{7,1},{8,14},{10,12},{12... | collective-permute-start | bytes 147464 | tf_op jit(solution)/shard_map/ppermute | solution.py:1156
  43.3 4.5 %collective-permute-start.4 = (f32[96,128]{1,0:T(8,128)S(1)}, f32[96,128]{1,0:T(8,128)S(1)}, u32[]{:S(2)}, u32[]{:S(2)}) collective-permute-start(f32[96,128]{1,0:T(8,128)S(1)} %fusion.1), channel_id=1, source_target_pairs={{0,8},{8,0},{16,24},{24,16},{1,9},{9,1},{17,25},{25,17},{2,10},{10... | collective-permute-start | bytes 147464 | tf_op jit(solution)/shard_map/ppermute | solution.py:1159
  44.0 5.0 %collective-permute-start.5 = (f32[96,128]{1,0:T(8,128)S(1)}, f32[96,128]{1,0:T(8,128)S(1)}, u32[]{:S(2)}, u32[]{:S(2)}) collective-permute-start(f32[96,128]{1,0:T(8,128)S(1)} %fusion.1), channel_id=1, source_target_pairs={{0,16},{8,24},{16,0},{24,8},{1,17},{9,25},{17,1},{25,9},{2,18},{10... | collective-permute-start | bytes 147464 | tf_op jit(solution)/shard_map/ppermute | solution.py:1159
  44.7 5.9 %collective-permute-start.6 = (f32[96,128]{1,0:T(8,128)S(1)}, f32[96,128]{1,0:T(8,128)S(1)}, u32[]{:S(2)}, u32[]{:S(2)}) collective-permute-start(f32[96,128]{1,0:T(8,128)S(1)} %fusion.1), channel_id=1, source_target_pairs={{0,24},{8,16},{16,8},{24,0},{1,25},{9,17},{17,9},{25,1},{2,26},{10... | collective-permute-start | bytes 147464 | tf_op jit(solution)/shard_map/ppermute | solution.py:1159
  50.6 4.2 %collective-permute-start.7 = (f32[96,128]{1,0:T(8,128)S(1)}, f32[96,128]{1,0:T(8,128)S(1)}, u32[]{:S(2)}, u32[]{:S(2)}) collective-permute-start(f32[96,128]{1,0:T(8,128)S(1)} %add_add_fusion), channel_id=1, source_target_pairs={{0,2},{2,0},{4,6},{6,4},{1,3},{3,1},{5,7},{7,5},{8,10},{10,8},{12,... | collective-permute-start | bytes 147464 | tf_op jit(solution)/shard_map/ppermute | solution.py:1164
  51.2 4.1 %collective-permute-start.8 = (f32[96,128]{1,0:T(8,128)S(1)}, f32[96,128]{1,0:T(8,128)S(1)}, u32[]{:S(2)}, u32[]{:S(2)}) collective-permute-start(f32[96,128]{1,0:T(8,128)S(1)} %add_add_fusion), channel_id=1, source_target_pairs={{0,4},{2,6},{4,0},{6,2},{1,5},{3,7},{5,1},{7,3},{8,12},{10,14},{12... | collective-permute-start | bytes 147464 | tf_op jit(solution)/shard_map/ppermute | solution.py:1164
  52.6 5.0 %collective-permute-start.9 = (f32[96,128]{1,0:T(8,128)S(1)}, f32[96,128]{1,0:T(8,128)S(1)}, u32[]{:S(2)}, u32[]{:S(2)}) collective-permute-start(f32[96,128]{1,0:T(8,128)S(1)} %add_add_fusion), channel_id=1, source_target_pairs={{0,6},{2,4},{4,2},{6,0},{1,7},{3,5},{5,3},{7,1},{8,14},{10,12},{12... | collective-permute-start | bytes 147464 | tf_op jit(solution)/shard_map/ppermute | solution.py:1164
  57.6 1.5 %collective-permute-start.10 = (f32[4,96,128]{2,1,0:T(8,128)S(1)}, f32[4,96,128]{2,1,0:T(8,128)S(1)}, u32[]{:S(2)}, u32[]{:S(2)}) collective-permute-start(f32[4,96,128]{2,1,0:T(8,128)S(1)} %pad_maximum_fusion.mine), channel_id=1, source_target_pairs={{0,1},{1,0},{2,3},{3,2},{4,5},{5,4},{6,7},{7,6},{8,9},{9,8},{10,11... | collective-permute-start | bytes 589832 | tf_op jit(solution)/shard_map/ppermute | solution.py:1165

commit v5 on v4

--- a/solution.py
+++ b/solution.py
@@ -45,7 +45,7 @@
 AT_HEAD = AT_TWO + 192
 AT_VEC = AT_HEAD + 64
 ROWS = AT_VEC + 1
-PADDED = 768
+PADDED = 704
 HALF = PADDED // 2
 
 STATE = [

time: 61.1 us -> 60.9 us (level)
  no operation moved by 1% of the time
where the time goes in v5:
time: 60.9 us; the launch traced here: 60.6 us
  Pallas kernels  21.3 us (35%)
  blocking collectives  13.8 us (23%)
  waiting for transfers between devices  12.4 us (20%)
  starting transfers between devices  11.7 us (19%)
  between operations  1.38 us (2%)
    all_to_all x1, blocking collectives, local(): lax.all_to_all(pay, ATOM_AXES, split_axis=0, concat_axis=0, tiled=True)  13.8 us
    pallas_call x1, Pallas kernels, local(): pl.pallas_call(functools.partial(second_kernel, ranks, ATOM_AXES, 'low'),...  10.1 us
    pallas_call x1, Pallas kernels, local(): pl.pallas_call(functools.partial(first_kernel, ranks, ATOM_AXES), out_sha...  9.56 us
    ppermute x3, starting transfers between devices, local(): lax.ppermute(part, 'far', [(i, i ^ k) for i in range(4)])  4.45 us
    ppermute x3, starting transfers between devices, local(): part = part + lax.ppermute(piece, PLANE, across_plane[k - 1])  3.55 us
    ppermute x3, starting transfers between devices, local(): lax.ppermute(whole, PLANE, p)  3.55 us
    ppermute x3, waiting for transfers between devices, local(): part = part + lax.ppermute(piece, PLANE, across_plane[k - 1])  3.41 us
    ppermute x3, waiting for transfers between devices, local(): lax.ppermute(whole, PLANE, p)  3.35 us
  transfers between devices with their start and end apart: 11, of which 10 were waited for; matrix products, arithmetic and copies ran while one was open for 0% of the time, Pallas kernels for 0%

profile of v5, /device:TPU:0, one launch (start us, length us, event | category | flops | bytes accessed | tf_op | source)
XLA Modules:
  0.0 60.6 jit_solution(15173104652448146046)
XLA Ops:
  1.3 9.6 %forward.1 = (f32[8,8,128]{2,1,0:T(8,128)S(1)}, bf16[64,96]{1,0:T(8,128)(2,1)S(1)}, bf16[64,192]{1,0:T(8,128)(2,1)S(1)}, bf16[3,256,192]{2,1,0:T(8,128)(2,1)S(1)...) custom-call(s32[1,1]{1,0:T(1,128)S(6)} %copy.20.live, ...), custom_call_target="tpu_custom_call" | custom-call | tf_op jit(solution)/shard_map/forward/pallas_call | solution.py:1120
  10.9 13.8 %all_to_all.5.got = f32[8,8,128]{2,1,0:T(8,128)S(1)} all-to-all(f32[8,8,128]{2,1,0:T(8,128)S(1)} %get-tuple-element.69), channel_id=1, replica_groups=mesh['far'=4,'near'=2,'high'=2,'low'=2] {'far','near'}, dimensions={0} | all-to-all | bytes 65536 | tf_op jit(solution)/shard_map/all_to_all | solution.py:1135
  24.6 10.1 %gradient.1 = (f32[352,128]{1,0:T(8,128)S(1)}, f32[352,128]{1,0:T(8,128)S(1)}, f32[3,1,32]{2,1,0:T(1,128)}) custom-call(s32[1,1]{1,0:T(1,128)S(6)} %copy.20.live, f32[8,8,128]{2,1,0:T(8,128)S(1)} %all_to_all.5.got, bf16[64,96]{1,0:T(8,128)(2,1)S(1)} %get-tuple-element.70.refs_0_, bf16[64,192]{1,0:T(8,128)(2,1)S(1)} %get-tuple-element.71.refs_1_, ...), custom_call_target="tpu_custom_call" | custom-call | tf_op jit(solution)/shard_map/gradient/pallas_call | solution.py:1136
  34.7 0.0 copy-start
  34.7 0.0 copy-start.1
  34.7 0.0 copy-start.2
  34.7 0.0 copy-start.3
  34.7 0.1 collective-permute-start
  34.8 1.4 %collective-permute-done = f32[352,128]{1,0:T(8,128)S(1)} collective-permute-done((f32[352,128]{1,0:T(8,128)S(1)}, f32[352,128]{1,0:T(8,128)S(1)}, u32[]{:S(2)}, u32[]{:S(2)}) %collective-permute-start) | collective-permute-done | bytes 180256 | tf_op jit(solution)/shard_map/ppermute | solution.py:1150
  36.2 1.5 %collective-permute-start.1 = (f32[88,128]{1,0:T(8,128)S(1)}, f32[88,128]{1,0:T(8,128)S(1)}, u32[]{:S(2)}, u32[]{:S(2)}) collective-permute-start(f32[88,128]{1,0:T(8,128)S(1)} %get-tuple-element.129), channel_id=1, source_target_pairs={{0,2},{2,0},{4,6},{6,4},{1,3},{3,1},{5,7},{7,5},{8,10},{10,8},{12,... | collective-permute-start | bytes 135176 | tf_op jit(solution)/shard_map/ppermute | solution.py:1156
  37.8 0.5 collective-permute-start.2
  38.2 1.5 %collective-permute-start.3 = (f32[88,128]{1,0:T(8,128)S(1)}, f32[88,128]{1,0:T(8,128)S(1)}, u32[]{:S(2)}, u32[]{:S(2)}) collective-permute-start(f32[88,128]{1,0:T(8,128)S(1)} %get-tuple-element.130), channel_id=1, source_target_pairs={{0,6},{2,4},{4,2},{6,0},{1,7},{3,5},{5,3},{7,1},{8,14},{10,12},{12... | collective-permute-start | bytes 135176 | tf_op jit(solution)/shard_map/ppermute | solution.py:1156
  39.8 0.6 collective-permute-done.1
  40.3 1.9 %collective-permute-done.2 = f32[88,128]{1,0:T(8,128)S(1)} collective-permute-done((f32[88,128]{1,0:T(8,128)S(1)}, f32[88,128]{1,0:T(8,128)S(1)}, u32[]{:S(2)}, u32[]{:S(2)}) %collective-permute-start.2) | collective-permute-done | bytes 45088 | tf_op jit(solution)/shard_map/ppermute | solution.py:1156
  42.3 0.9 %collective-permute-done.3 = f32[88,128]{1,0:T(8,128)S(1)} collective-permute-done((f32[88,128]{1,0:T(8,128)S(1)}, f32[88,128]{1,0:T(8,128)S(1)}, u32[]{:S(2)}, u32[]{:S(2)}) %collective-permute-start.3) | collective-permute-done | bytes 45088 | tf_op jit(solution)/shard_map/ppermute | solution.py:1156
  43.2 0.8 %collective-permute-start.4 = (f32[88,128]{1,0:T(8,128)S(1)}, f32[88,128]{1,0:T(8,128)S(1)}, u32[]{:S(2)}, u32[]{:S(2)}) collective-permute-start(f32[88,128]{1,0:T(8,128)S(1)} %fusion.1), channel_id=1, source_target_pairs={{0,8},{8,0},{16,24},{24,16},{1,9},{9,1},{17,25},{25,17},{2,10},{10... | collective-permute-start | bytes 135176 | tf_op jit(solution)/shard_map/ppermute | solution.py:1159
  44.0 0.6 %collective-permute-start.5 = (f32[88,128]{1,0:T(8,128)S(1)}, f32[88,128]{1,0:T(8,128)S(1)}, u32[]{:S(2)}, u32[]{:S(2)}) collective-permute-start(f32[88,128]{1,0:T(8,128)S(1)} %fusion.1), channel_id=1, source_target_pairs={{0,16},{8,24},{16,0},{24,8},{1,17},{9,25},{17,1},{25,9},{2,18},{10... | collective-permute-start | bytes 135176 | tf_op jit(solution)/shard_map/ppermute | solution.py:1159
  44.6 3.0 %collective-permute-start.6 = (f32[88,128]{1,0:T(8,128)S(1)}, f32[88,128]{1,0:T(8,128)S(1)}, u32[]{:S(2)}, u32[]{:S(2)}) collective-permute-start(f32[88,128]{1,0:T(8,128)S(1)} %fusion.1), channel_id=1, source_target_pairs={{0,24},{8,16},{16,8},{24,0},{1,25},{9,17},{17,9},{25,1},{2,26},{10... | collective-permute-start | bytes 135176 | tf_op jit(solution)/shard_map/ppermute | solution.py:1159
  47.7 0.0 collective-permute-done.4
  47.7 1.3 %collective-permute-done.5 = f32[88,128]{1,0:T(8,128)S(1)} collective-permute-done((f32[88,128]{1,0:T(8,128)S(1)}, f32[88,128]{1,0:T(8,128)S(1)}, u32[]{:S(2)}, u32[]{:S(2)}) %collective-permute-start.5) | collective-permute-done | bytes 45088 | tf_op jit(solution)/shard_map/ppermute | solution.py:1159
  48.9 1.5 %collective-permute-done.6 = f32[88,128]{1,0:T(8,128)S(1)} collective-permute-done((f32[88,128]{1,0:T(8,128)S(1)}, f32[88,128]{1,0:T(8,128)S(1)}, u32[]{:S(2)}, u32[]{:S(2)}) %collective-permute-start.6) | collective-permute-done | bytes 45088 | tf_op jit(solution)/shard_map/ppermute | solution.py:1159
  50.5 0.6 %collective-permute-start.7 = (f32[88,128]{1,0:T(8,128)S(1)}, f32[88,128]{1,0:T(8,128)S(1)}, u32[]{:S(2)}, u32[]{:S(2)}) collective-permute-start(f32[88,128]{1,0:T(8,128)S(1)} %add_add_fusion), channel_id=1, source_target_pairs={{0,2},{2,0},{4,6},{6,4},{1,3},{3,1},{5,7},{7,5},{8,10},{10,8},{12,... | collective-permute-start | bytes 135176 | tf_op jit(solution)/shard_map/ppermute | solution.py:1164
  51.1 1.4 %collective-permute-start.8 = (f32[88,128]{1,0:T(8,128)S(1)}, f32[88,128]{1,0:T(8,128)S(1)}, u32[]{:S(2)}, u32[]{:S(2)}) collective-permute-start(f32[88,128]{1,0:T(8,128)S(1)} %add_add_fusion), channel_id=1, source_target_pairs={{0,4},{2,6},{4,0},{6,2},{1,5},{3,7},{5,1},{7,3},{8,12},{10,14},{12... | collective-permute-start | bytes 135176 | tf_op jit(solution)/shard_map/ppermute | solution.py:1164
  52.4 1.6 %collective-permute-start.9 = (f32[88,128]{1,0:T(8,128)S(1)}, f32[88,128]{1,0:T(8,128)S(1)}, u32[]{:S(2)}, u32[]{:S(2)}) collective-permute-start(f32[88,128]{1,0:T(8,128)S(1)} %add_add_fusion), channel_id=1, source_target_pairs={{0,6},{2,4},{4,2},{6,0},{1,7},{3,5},{5,3},{7,1},{8,14},{10,12},{12... | collective-permute-start | bytes 135176 | tf_op jit(solution)/shard_map/ppermute | solution.py:1164
  54.0 0.6 collective-permute-done.7
  54.6 0.5 collective-permute-done.8
  55.1 2.3 %collective-permute-done.9 = f32[88,128]{1,0:T(8,128)S(1)} collective-permute-done((f32[88,128]{1,0:T(8,128)S(1)}, f32[88,128]{1,0:T(8,128)S(1)}, u32[]{:S(2)}, u32[]{:S(2)}) %collective-permute-start.9) | collective-permute-done | bytes 45088 | tf_op jit(solution)/shard_map/ppermute | solution.py:1164
  57.4 0.1 collective-permute-start.10
  57.5 1.4 %collective-permute-done.10.other = f32[4,88,128]{2,1,0:T(8,128)S(1)} collective-permute-done((f32[4,88,128]{2,1,0:T(8,128)S(1)}, f32[4,88,128]{2,1,0:T(8,128)S(1)}, u32[]{:S(2)}, u32[]{:S(2)}) %collective-permute-start.10) | collective-permute-done | bytes 180256 | tf_op jit(solution)/shard_map/ppermute | solution.py:1165
  58.9 0.0 copy-done
  58.9 0.0 copy-done.1
  58.9 0.0 copy-done.2
  58.9 0.0 copy-done.3
  58.9 1.7 %update.1 = (f32[1,1]{1,0:T(1,128)}, f32[1,1]{1,0:T(1,128)}, f32[1,1]{1,0:T(1,128)}, f32[698,128]{1,0:T(8,128)}, f32[698,128]{1,0:T(8,128)}, /*index=5*/f32[698,...) custom-call(f32[4,88,128]{2,1,0:T(8,128)S(1)} %pad_maximum_fusion.mine, ...), custom_call_target="tpu_custom_call" | custom-call | tf_op jit(solution)/shard_map/update/pallas_call | solution.py:1167
  (5 shorter events, 0.1 us)
Async XLA Ops:
  34.7 24.2 %copy-start = (f32[89344]{0:T(1024)S(1)}, f32[89344]{0:T(1024)}, u32[]{:S(2)}) copy-start(f32[89344]{0:T(1024)} %param.11) | copy-start | bytes 1072132
  34.7 24.2 %copy-start.1 = (f32[89344]{0:T(1024)S(1)}, f32[89344]{0:T(1024)}, u32[]{:S(2)}) copy-start(f32[89344]{0:T(1024)} %param.12) | copy-start | bytes 1072132
  34.7 24.2 %copy-start.2 = (f32[89344]{0:T(1024)S(1)}, f32[89344]{0:T(1024)}, u32[]{:S(2)}) copy-start(f32[89344]{0:T(1024)} %param.13) | copy-start | bytes 1072132
  34.7 24.2 %copy-start.3 = (f32[89344]{0:T(1024)S(1)}, f32[89344]{0:T(1024)}, u32[]{:S(2)}) copy-start(f32[89344]{0:T(1024)} %param.14) | copy-start | bytes 1072132
  34.7 1.5 %collective-permute-start = (f32[352,128]{1,0:T(8,128)S(1)}, f32[352,128]{1,0:T(8,128)S(1)}, u32[]{:S(2)}, u32[]{:S(2)}) collective-permute-start(f32[352,128]{1,0:T(8,128)S(1)} %get-tuple-element.119), channel_id=1, source_target_pairs={{0,1},{1,0},{2,3},{3,2},{4,5},{5,4},{6,7},{7,6},{8,9},{9,8},{10,11... | collective-permute-start | bytes 540680 | tf_op jit(solution)/shard_map/ppermute | solution.py:1150
  36.2 4.1 %collective-permute-start.1 = (f32[88,128]{1,0:T(8,128)S(1)}, f32[88,128]{1,0:T(8,128)S(1)}, u32[]{:S(2)}, u32[]{:S(2)}) collective-permute-start(f32[88,128]{1,0:T(8,128)S(1)} %get-tuple-element.129), channel_id=1, source_target_pairs={{0,2},{2,0},{4,6},{6,4},{1,3},{3,1},{5,7},{7,5},{8,10},{10,8},{12,... | collective-permute-start | bytes 135176 | tf_op jit(solution)/shard_map/ppermute | solution.py:1156
  37.8 4.5 %collective-permute-start.2 = (f32[88,128]{1,0:T(8,128)S(1)}, f32[88,128]{1,0:T(8,128)S(1)}, u32[]{:S(2)}, u32[]{:S(2)}) collective-permute-start(f32[88,128]{1,0:T(8,128)S(1)} %get-tuple-element.131), channel_id=1, source_target_pairs={{0,4},{2,6},{4,0},{6,2},{1,5},{3,7},{5,1},{7,3},{8,12},{10,14},{12... | collective-permute-start | bytes 135176 | tf_op jit(solution)/shard_map/ppermute | solution.py:1156
  38.2 4.9 %collective-permute-start.3 = (f32[88,128]{1,0:T(8,128)S(1)}, f32[88,128]{1,0:T(8,128)S(1)}, u32[]{:S(2)}, u32[]{:S(2)}) collective-permute-start(f32[88,128]{1,0:T(8,128)S(1)} %get-tuple-element.130), channel_id=1, source_target_pairs={{0,6},{2,4},{4,2},{6,0},{1,7},{3,5},{5,3},{7,1},{8,14},{10,12},{12... | collective-permute-start | bytes 135176 | tf_op jit(solution)/shard_map/ppermute | solution.py:1156
  43.2 4.5 %collective-permute-start.4 = (f32[88,128]{1,0:T(8,128)S(1)}, f32[88,128]{1,0:T(8,128)S(1)}, u32[]{:S(2)}, u32[]{:S(2)}) collective-permute-start(f32[88,128]{1,0:T(8,128)S(1)} %fusion.1), channel_id=1, source_target_pairs={{0,8},{8,0},{16,24},{24,16},{1,9},{9,1},{17,25},{25,17},{2,10},{10... | collective-permute-start | bytes 135176 | tf_op jit(solution)/shard_map/ppermute | solution.py:1159
  44.0 4.9 %collective-permute-start.5 = (f32[88,128]{1,0:T(8,128)S(1)}, f32[88,128]{1,0:T(8,128)S(1)}, u32[]{:S(2)}, u32[]{:S(2)}) collective-permute-start(f32[88,128]{1,0:T(8,128)S(1)} %fusion.1), channel_id=1, source_target_pairs={{0,16},{8,24},{16,0},{24,8},{1,17},{9,25},{17,1},{25,9},{2,18},{10... | collective-permute-start | bytes 135176 | tf_op jit(solution)/shard_map/ppermute | solution.py:1159
  44.6 5.8 %collective-permute-start.6 = (f32[88,128]{1,0:T(8,128)S(1)}, f32[88,128]{1,0:T(8,128)S(1)}, u32[]{:S(2)}, u32[]{:S(2)}) collective-permute-start(f32[88,128]{1,0:T(8,128)S(1)} %fusion.1), channel_id=1, source_target_pairs={{0,24},{8,16},{16,8},{24,0},{1,25},{9,17},{17,9},{25,1},{2,26},{10... | collective-permute-start | bytes 135176 | tf_op jit(solution)/shard_map/ppermute | solution.py:1159
  50.5 4.1 %collective-permute-start.7 = (f32[88,128]{1,0:T(8,128)S(1)}, f32[88,128]{1,0:T(8,128)S(1)}, u32[]{:S(2)}, u32[]{:S(2)}) collective-permute-start(f32[88,128]{1,0:T(8,128)S(1)} %add_add_fusion), channel_id=1, source_target_pairs={{0,2},{2,0},{4,6},{6,4},{1,3},{3,1},{5,7},{7,5},{8,10},{10,8},{12,... | collective-permute-start | bytes 135176 | tf_op jit(solution)/shard_map/ppermute | solution.py:1164
  51.1 4.0 %collective-permute-start.8 = (f32[88,128]{1,0:T(8,128)S(1)}, f32[88,128]{1,0:T(8,128)S(1)}, u32[]{:S(2)}, u32[]{:S(2)}) collective-permute-start(f32[88,128]{1,0:T(8,128)S(1)} %add_add_fusion), channel_id=1, source_target_pairs={{0,4},{2,6},{4,0},{6,2},{1,5},{3,7},{5,1},{7,3},{8,12},{10,14},{12... | collective-permute-start | bytes 135176 | tf_op jit(solution)/shard_map/ppermute | solution.py:1164
  52.4 4.9 %collective-permute-start.9 = (f32[88,128]{1,0:T(8,128)S(1)}, f32[88,128]{1,0:T(8,128)S(1)}, u32[]{:S(2)}, u32[]{:S(2)}) collective-permute-start(f32[88,128]{1,0:T(8,128)S(1)} %add_add_fusion), channel_id=1, source_target_pairs={{0,6},{2,4},{4,2},{6,0},{1,7},{3,5},{5,3},{7,1},{8,14},{10,12},{12... | collective-permute-start | bytes 135176 | tf_op jit(solution)/shard_map/ppermute | solution.py:1164
  57.4 1.5 %collective-permute-start.10 = (f32[4,88,128]{2,1,0:T(8,128)S(1)}, f32[4,88,128]{2,1,0:T(8,128)S(1)}, u32[]{:S(2)}, u32[]{:S(2)}) collective-permute-start(f32[4,88,128]{2,1,0:T(8,128)S(1)} %pad_maximum_fusion.mine), channel_id=1, source_target_pairs={{0,1},{1,0},{2,3},{3,2},{4,5},{5,4},{6,7},{7,6},{8,9},{9,8},{10,11... | collective-permute-start | bytes 540680 | tf_op jit(solution)/shard_map/ppermute | solution.py:1165
